TPU v7x, 128 devices: a whole 4x4x4 slice. The times are simulated.
128 devices in a mesh: dp: 128 (over x, z, y, core).
Axes of the slice: x: 4, y: 4, z: 4, core: 2. Of those that a mesh axis runs over, the one named last changes fastest.
Arguments:
- hidden_in: bfloat16 [32768, 640], P('dp'), may hold values from -24 to 24
- query_weight: bfloat16 [640, 1024], P('dp'), may hold values from -0.25 to 0.25
- key_weight: bfloat16 [640, 256], P('dp'), may hold values from -0.25 to 0.25
- value_weight: bfloat16 [640, 256], P('dp'), may hold values from -0.25 to 0.25
- output_weight: bfloat16 [1024, 640], P('dp'), may hold values from -0.1875 to 0.1875
- gate_weight: bfloat16 [640, 2048], P('dp'), may hold values from -0.25 to 0.25
- up_weight: bfloat16 [640, 2048], P('dp'), may hold values from -0.25 to 0.25
- down_weight: bfloat16 [2048, 640], P('dp'), may hold values from -0.125 to 0.125
- input_gain: bfloat16 [640], P('dp'), may hold values from -0.5 to 0.5
- query_gain: bfloat16 [256], P('dp'), may hold values from -0.5 to 0.5
- key_gain: bfloat16 [256], P('dp'), may hold values from -0.5 to 0.5
- mixer_gain: bfloat16 [640], P('dp'), may hold values from -0.5 to 0.5
- middle_gain: bfloat16 [640], P('dp'), may hold values from -0.5 to 0.5
- output_gain: bfloat16 [640], P('dp'), may hold values from -0.5 to 0.5
- seq_lengths: int32 [64], replicated, may hold values from 1 to 1024, 32768 in all
- out_grad: bfloat16 [32768, 640], P('dp'), may hold values from -6 to 6
Outputs:
- mixed_out: bfloat16 [32768, 640], P('dp')
- input_grad: float32 [32768, 640], P('dp')
- query_weight_grad: float32 [640, 1024], P('dp')
- key_weight_grad: float32 [640, 256], P('dp')
- value_weight_grad: float32 [640, 256], P('dp')
- output_weight_grad: float32 [1024, 640], P('dp')
- gate_weight_grad: float32 [640, 2048], P('dp')
- up_weight_grad: float32 [640, 2048], P('dp')
- down_weight_grad: float32 [2048, 640], P('dp')
- input_gain_grad: float32 [640], P('dp')
- query_gain_grad: float32 [256], P('dp')
- key_gain_grad: float32 [256], P('dp')
- mixer_gain_grad: float32 [640], P('dp')
- middle_gain_grad: float32 [640], P('dp')
- output_gain_grad: float32 [640], P('dp')
Inputs may be any that keep to these rules, and one draw needn't show every extreme that they name: `seq_lengths`: lengths of the packed sequences in order; they sum to 32768, and the longest is exactly 1024.
All inputs are finite; a program needn't handle non-finite values.
Results may differ from a plain program's by a relative error of at most 0.025.
Values may be sent and summed in bfloat16 or wider, within the bound.
A program may use at most 128 MiB of HBM per device.

v0:
```python
import math

import jax
import jax.numpy as jnp
from jax import lax
from jax.sharding import PartitionSpec as P

WINDOW = 512


EPSILON = 1e-06
ROPE_BASE = 10000.0
NEG_FILL = -1e30


def side_by_side(arrays, axis, dim, along):
    both = jnp.concatenate(arrays, axis=along)
    whole, at, done = (lax.all_gather(both, axis, axis=dim, tiled=True), 0, [])
    for a in arrays:
        done.append(lax.slice_in_dim(whole, at, at + a.shape[along], axis=along))
        at += a.shape[along]
    return tuple(done)


def shifted(value, axis, steps):
    count = lax.axis_size(axis)
    first, last = (max(0, -steps), min(count, count - steps))
    return lax.ppermute(value, axis, [(source, source + steps) for source in range(first, last)])


def in_blocks(x, dim, size):
    lengths = x.shape
    tiles = x.reshape(*lengths[:dim], size, lengths[dim] // size, *lengths[dim + 1 :])
    return jnp.moveaxis(tiles, dim, 0)


def one_scatter(arrays, axis, dims):
    size = lax.axis_size(axis)
    tiles = [in_blocks(a, dim, size) for a, dim in zip(arrays, dims)]
    lines = jnp.concatenate([b.reshape(size, -1) for b in tiles], axis=1)
    rows = max(16, -(-lines.shape[1] // 1024) * 8)
    lines = jnp.pad(lines, ((0, 0), (0, rows * 128 - lines.shape[1]))).reshape(-1, 128)
    flat, at, done = (lax.psum_scatter(lines, axis, tiled=True).reshape(-1), 0, [])
    for b in tiles:
        part = b[0]
        done.append(flat[at : at + part.size].reshape(part.shape))
        at += part.size
    return tuple(done)


def norm_parts(values):
    inv_rms = lax.rsqrt(jnp.mean(values * values, axis=-1, keepdims=True) + EPSILON)
    return (values * inv_rms, inv_rms)


def norm_back(upstream, unit_rows, inv_rms):
    return inv_rms * (upstream - unit_rows * jnp.mean(unit_rows * upstream, axis=-1, keepdims=True))


def rotary(position, head_dim):
    frequency = ROPE_BASE ** (-2.0 * jnp.arange(head_dim // 2, dtype=jnp.float32) / head_dim)
    angles = position[:, None] * frequency[None, :]
    return (jnp.cos(angles), jnp.sin(angles))


def apply_rotary(values, cosine, sine_table):
    half_dim = values.shape[-1] // 2
    front_half = values[..., :half_dim]
    back_half = values[..., half_dim:]
    cos_wide = cosine[:, None, :]
    sin_wide = sine_table[:, None, :]
    return jnp.concatenate(
        [
            front_half * cos_wide - back_half * sin_wide,
            back_half * cos_wide + front_half * sin_wide,
        ],
        axis=-1,
    )


def rotary_back(upstream, cosine, sine_table):
    half_dim = upstream.shape[-1] // 2
    front_half = upstream[..., :half_dim]
    back_half = upstream[..., half_dim:]
    cos_wide = cosine[:, None, :]
    sin_wide = sine_table[:, None, :]
    return jnp.concatenate(
        [
            front_half * cos_wide + back_half * sin_wide,
            back_half * cos_wide - front_half * sin_wide,
        ],
        axis=-1,
    )


def seq_layout(indices, lengths):
    seq_ends = jnp.cumsum(lengths)
    passed = seq_ends[None, :] <= indices[:, None]
    segment = jnp.sum(passed.astype(jnp.int32), axis=1)
    seq_start = jnp.max(jnp.where(passed, seq_ends[None, :], 0), axis=1)
    return (segment, indices - seq_start)


def gelu_tanh(values):
    return jax.nn.gelu(values, approximate=True)


def mat_mul(left_side, right_side):
    return jnp.dot(left_side, right_side, preferred_element_type=jnp.float32)


def mat_mul_t(left_side, right_side):
    return lax.dot_general(
        left_side, right_side, (((1,), (1,)), ((), ())), preferred_element_type=jnp.float32
    )


def mat_t_mul(left_side, right_side):
    return lax.dot_general(
        left_side, right_side, (((0,), (0,)), ((), ())), preferred_element_type=jnp.float32
    )


def per_device(
    hidden_in,
    query_weight,
    key_weight,
    value_weight,
    output_weight,
    gate_weight,
    up_weight,
    down_weight,
    input_gain,
    query_gain,
    key_gain,
    mixer_gain,
    middle_gain,
    output_gain,
    seq_lengths,
    out_grad,
):
    tok_rows = hidden_in.shape[0]
    hop_count = (WINDOW + tok_rows - 2) // tok_rows
    head_dim = key_weight.shape[1]
    head_count = query_weight.shape[1] // head_dim
    score_scale = 1.0 / math.sqrt(head_dim)
    offset = lax.axis_index("dp") * tok_rows
    query_index = offset + jnp.arange(tok_rows, dtype=jnp.int32)
    key_index = (
        offset - hop_count * tok_rows + jnp.arange((hop_count + 1) * tok_rows, dtype=jnp.int32)
    )
    query_seg, position = seq_layout(query_index, seq_lengths)
    key_seg = seq_layout(key_index, seq_lengths)[0]
    distance = query_index[:, None] - key_index[None, :]
    allowed = (
        (query_seg[:, None] == key_seg[None, :])
        & (distance >= 0)
        & (distance < WINDOW)
        & (key_index[None, :] >= 0)
    )
    cosine, sine_table = rotary(position.astype(jnp.float32), head_dim)
    (
        query_full,
        key_full,
        value_full,
        output_full,
        input_full,
        qgain_full,
        kgain_full,
        mixer_full,
    ) = (
        *side_by_side((query_weight, key_weight, value_weight), "dp", 0, 1),
        lax.all_gather(output_weight, "dp", axis=0, tiled=True),
        lax.all_gather(input_gain, "dp", axis=0, tiled=True),
        lax.all_gather(query_gain, "dp", axis=0, tiled=True),
        lax.all_gather(key_gain, "dp", axis=0, tiled=True),
        lax.all_gather(mixer_gain, "dp", axis=0, tiled=True),
    )
    input_mult = 1.0 + input_full.astype(jnp.float32)
    query_mult = 1.0 + qgain_full.astype(jnp.float32)
    key_mult = 1.0 + kgain_full.astype(jnp.float32)
    mixer_mult = 1.0 + mixer_full.astype(jnp.float32)
    hidden = hidden_in.astype(jnp.float32)
    input_unit, input_inv = norm_parts(hidden)
    normed = (input_unit * input_mult).astype(jnp.bfloat16)
    query_raw = mat_mul(normed, query_full).reshape(tok_rows, head_count, head_dim)
    key_raw = mat_mul(normed, key_full)
    value_rows = mat_mul(normed, value_full).astype(jnp.bfloat16)
    query_unit, query_inv = norm_parts(query_raw)
    queries = apply_rotary(query_unit * query_mult, cosine, sine_table).astype(jnp.bfloat16)
    key_unit, key_inv = norm_parts(key_raw)
    key_rows = apply_rotary((key_unit * key_mult)[:, None, :], cosine, sine_table)[:, 0, :].astype(
        jnp.bfloat16
    )
    key_parts = []
    value_parts = []
    for step_back in range(hop_count, 0, -1):
        far_keys, far_values = shifted((key_rows, value_rows), "dp", step_back)
        key_parts.append(far_keys)
        value_parts.append(far_values)
    key_all = jnp.concatenate(key_parts + [key_rows], axis=0)
    value_all = jnp.concatenate(value_parts + [value_rows], axis=0)

    def masked_scores(query_block):
        raw_scores = (
            jnp.einsum("thd,kd->htk", query_block, key_all, preferred_element_type=jnp.float32)
            * score_scale
        )
        return jnp.where(allowed[None], raw_scores, NEG_FILL)

    scores = masked_scores(queries)
    row_max = jnp.max(scores, axis=-1, keepdims=True)
    exp_scores = jnp.exp(scores - row_max)
    row_total = jnp.sum(exp_scores, axis=-1, keepdims=True)
    probs_low = (exp_scores / row_total).astype(jnp.bfloat16)
    log_total = row_max + jnp.log(row_total)
    attended = (
        jnp.einsum("htk,kd->thd", probs_low, value_all, preferred_element_type=jnp.float32)
        .reshape(tok_rows, head_count * head_dim)
        .astype(jnp.bfloat16)
    )
    mixer_out = mat_mul(attended, output_full)
    mixer_unit, mixer_inv = norm_parts(mixer_out)
    middle = hidden + mixer_unit * mixer_mult
    gate_full, up_full, down_full, middle_full, outgain_full = (
        *side_by_side((gate_weight, up_weight), "dp", 0, 1),
        lax.all_gather(down_weight, "dp", axis=0, tiled=True),
        lax.all_gather(middle_gain, "dp", axis=0, tiled=True),
        lax.all_gather(output_gain, "dp", axis=0, tiled=True),
    )
    middle_mult = 1.0 + middle_full.astype(jnp.float32)
    output_mult = 1.0 + outgain_full.astype(jnp.float32)
    middle_unit, middle_inv = norm_parts(middle)
    middle_normed = (middle_unit * middle_mult).astype(jnp.bfloat16)
    gate_pre = mat_mul(middle_normed, gate_full)
    up_proj = mat_mul(middle_normed, up_full)
    activation, gelu_pullback = jax.vjp(gelu_tanh, gate_pre)
    hidden_units = (activation * up_proj).astype(jnp.bfloat16)
    ffn_out = mat_mul(hidden_units, down_full)
    ffn_unit, ffn_inv = norm_parts(ffn_out)
    mixed_out = (middle + ffn_unit * output_mult).astype(jnp.bfloat16)
    gate_back, up_back, down_back = (gate_full, up_full, down_full)
    grad_out = out_grad.astype(jnp.float32)
    output_gain_part = jnp.sum(grad_out * ffn_unit, axis=0)
    grad_ffn = norm_back(grad_out * output_mult, ffn_unit, ffn_inv).astype(jnp.bfloat16)
    grad_hidden = mat_mul_t(grad_ffn, down_back)
    down_grad_full = mat_t_mul(hidden_units, grad_ffn)
    grad_gate = gelu_pullback(grad_hidden * up_proj)[0].astype(jnp.bfloat16)
    grad_up = (grad_hidden * activation).astype(jnp.bfloat16)
    grad_middle_in = mat_mul_t(grad_gate, gate_back) + mat_mul_t(grad_up, up_back)
    middle_gain_part = jnp.sum(grad_middle_in * middle_unit, axis=0)
    gate_term = mat_t_mul(middle_normed, grad_gate)
    up_term = mat_t_mul(middle_normed, grad_up)
    down_grad, gate_grad, up_grad, middle_gain_grad, output_gain_grad = one_scatter(
        (down_grad_full, gate_term, up_term, middle_gain_part, output_gain_part),
        "dp",
        (0, 0, 0, 0, 0),
    )
    grad_middle = grad_out + norm_back(grad_middle_in * middle_mult, middle_unit, middle_inv)
    query_back, key_back, value_back, output_back = (query_full, key_full, value_full, output_full)
    mixer_gain_part = jnp.sum(grad_middle * mixer_unit, axis=0)
    grad_mixer = norm_back(grad_middle * mixer_mult, mixer_unit, mixer_inv).astype(jnp.bfloat16)
    output_grad_full = mat_t_mul(attended, grad_mixer)
    grad_attended = (
        mat_mul_t(grad_mixer, output_back)
        .astype(jnp.bfloat16)
        .reshape(tok_rows, head_count, head_dim)
    )
    probs = jnp.exp(masked_scores(queries) - log_total)
    grad_probs = jnp.einsum(
        "thd,kd->htk", grad_attended, value_all, preferred_element_type=jnp.float32
    )
    delta_rows = jnp.sum(probs * grad_probs, axis=-1, keepdims=True)
    grad_scores = (probs * (grad_probs - delta_rows)).astype(jnp.bfloat16)
    grad_queries = (
        jnp.einsum("htk,kd->thd", grad_scores, key_all, preferred_element_type=jnp.float32)
        * score_scale
    )
    grad_keys_all = (
        jnp.einsum("htk,thd->kd", grad_scores, queries, preferred_element_type=jnp.float32)
        * score_scale
    )
    grad_values_all = jnp.einsum(
        "htk,thd->kd", probs_low, grad_attended, preferred_element_type=jnp.float32
    )
    own_start = hop_count * tok_rows
    key_grad = grad_keys_all[own_start:]
    value_grad = grad_values_all[own_start:]
    for step_back in range(1, hop_count + 1):
        block_at = (hop_count - step_back) * tok_rows
        back_keys, back_values = (
            shifted(
                grad_keys_all[block_at : block_at + tok_rows].astype(jnp.bfloat16), "dp", -step_back
            ).astype(jnp.float32),
            shifted(
                grad_values_all[block_at : block_at + tok_rows].astype(jnp.bfloat16),
                "dp",
                -step_back,
            ).astype(jnp.float32),
        )
        key_grad = key_grad + back_keys
        value_grad = value_grad + back_values
    key_grad_rot = rotary_back(key_grad[:, None, :], cosine, sine_table)[:, 0, :]
    key_gain_part = jnp.sum(key_grad_rot * key_unit, axis=0)
    grad_key_raw = norm_back(key_grad_rot * key_mult, key_unit, key_inv).astype(jnp.bfloat16)
    grad_value = value_grad.astype(jnp.bfloat16)
    query_grad_rot = rotary_back(grad_queries, cosine, sine_table)
    query_gain_part = jnp.sum(query_grad_rot * query_unit, axis=(0, 1))
    grad_query_raw = (
        norm_back(query_grad_rot * query_mult, query_unit, query_inv)
        .astype(jnp.bfloat16)
        .reshape(tok_rows, head_count * head_dim)
    )
    grad_normed = (
        mat_mul_t(grad_query_raw, query_back)
        + mat_mul_t(grad_key_raw, key_back)
        + mat_mul_t(grad_value, value_back)
    )
    query_grad_full = mat_t_mul(normed, grad_query_raw)
    key_grad_full = mat_t_mul(normed, grad_key_raw)
    value_grad_full = mat_t_mul(normed, grad_value)
    input_gain_part = jnp.sum(grad_normed * input_unit, axis=0)
    input_grad = grad_middle + norm_back(grad_normed * input_mult, input_unit, input_inv)
    (
        query_wgrad,
        key_wgrad,
        value_wgrad,
        output_wgrad,
        input_gain_grad,
        query_gain_grad,
        key_gain_grad,
        mixer_gain_grad,
    ) = (
        lax.psum_scatter(query_grad_full, "dp", scatter_dimension=0, tiled=True),
        lax.psum_scatter(key_grad_full, "dp", scatter_dimension=0, tiled=True),
        lax.psum_scatter(value_grad_full, "dp", scatter_dimension=0, tiled=True),
        lax.psum_scatter(output_grad_full, "dp", scatter_dimension=0, tiled=True),
        lax.psum_scatter(input_gain_part, "dp", scatter_dimension=0, tiled=True),
        lax.psum_scatter(query_gain_part, "dp", scatter_dimension=0, tiled=True),
        lax.psum_scatter(key_gain_part, "dp", scatter_dimension=0, tiled=True),
        lax.psum_scatter(mixer_gain_part, "dp", scatter_dimension=0, tiled=True),
    )
    return (
        mixed_out,
        input_grad,
        query_wgrad,
        key_wgrad,
        value_wgrad,
        output_wgrad,
        gate_grad,
        up_grad,
        down_grad,
        input_gain_grad,
        query_gain_grad,
        key_gain_grad,
        mixer_gain_grad,
        middle_gain_grad,
        output_gain_grad,
    )


def solution(mesh):
    return jax.shard_map(
        per_device,
        mesh=mesh,
        in_specs=(
            P("dp", None),
            P("dp", None),
            P("dp", None),
            P("dp", None),
            P("dp", None),
            P("dp", None),
            P("dp", None),
            P("dp", None),
            P("dp"),
            P("dp"),
            P("dp"),
            P("dp"),
            P("dp"),
            P("dp"),
            P(),
            P("dp", None),
        ),
        out_specs=(
            P("dp", None),
            P("dp", None),
            P("dp", None),
            P("dp", None),
            P("dp", None),
            P("dp", None),
            P("dp", None),
            P("dp", None),
            P("dp", None),
            P("dp"),
            P("dp"),
            P("dp"),
            P("dp"),
            P("dp"),
            P("dp"),
        ),
        check_vma=False,
    )
```

profile of v0, /device:TPU:1, one launch (start us, length us, event | category | flops | bytes accessed | tf_op | source)
XLA Modules:
  0.0 643.1 jit_solution(1722805257441370570)
XLA Ops:
  17.8 69.6 %all-reduce.18 = (bf16[640]{0:T(1024)(128)(2,1)S(1)}, bf16[256]{0:T(256)(128)(2,1)S(1)}, bf16[256]{0:T(256)(128)(2,1)S(1)}, bf16[640]{0:T(1024)(128)(2,1)S(1)}, ...) all-reduce(bf16[640]{0:T(1024)(128)(2,1)S(1)} %dynamic-update-slice, ...), channel_id=1, replica_groups=mesh['dp'=128] {'dp'}, use_global_device_ids=true, to_apply=%add.1 | all-reduce | flops 3072 | bytes 12288
  91.1 3.0 reshape.405
  95.4 2.8 collective-permute-start.1
  98.3 3.6 collective-permute-start
  118.0 2.4 convolution_convert_fusion.1
  120.5 24.9 %all-gather.7.cloned.1.call-done = bf16[1024,640]{1,0:T(8,128)(2,1)} async-done(((bf16[8,640]{1,0:T(8,128)(2,1)}), bf16[1024,640]{1,0:T(8,128)(2,1)}) %all-gather.7.cloned.1.call-update) | async-done | bytes 1310736 | tf_op jit(solution)/shard_map/all_gather | solution.py:173
  150.4 66.3 %all-gather.13.cloned.1.call-done = bf16[128,5,4096]{2,1,0:T(8,128)(2,1)} async-done(((bf16[1,5,4096]{2,1,0:T(8,128)(2,1)}), bf16[128,5,4096]{2,1,0:T(8,128)(2,1)}) %all-gather.13.cloned.1.call-update) | async-done | bytes 5242896 | tf_op jit(solution)/shard_map/all_gather | solution.py:18
  216.7 8.7 %reshape.407 = bf16[640,4096]{1,0:T(8,128)(2,1)} reshape(bf16[128,5,4096]{2,1,0:T(8,128)(2,1)} %all-gather.13.cloned.1.call-done) | data formatting | bytes 10485760
  225.4 2.9 fusion.10
  229.6 4.6 multiply_convert_fusion.1
  234.3 48.5 %all-gather.9.cloned.1.call-done = bf16[2048,640]{1,0:T(8,128)(2,1)} async-done(((bf16[16,640]{1,0:T(8,128)(2,1)}), bf16[2048,640]{1,0:T(8,128)(2,1)}) %all-gather.9.cloned.1.call-update) | async-done | bytes 2621456 | tf_op jit(solution)/shard_map/all_gather | solution.py:227
  282.8 3.3 multiply_reduce_fusion.7
  287.8 2.3 fusion.18
  291.2 3.2 fusion.103
  294.4 3.3 fusion.101
  297.7 3.2 fusion.102
  327.9 6.4 reshape_reshape.10
  334.3 6.4 reshape_reshape.11
  340.7 5.5 reshape_reshape.9
  346.2 16.9 %concatenate.40 = f32[128,30730]{1,0:T(8,128)} concatenate(f32[128,10240]{1,0:T(8,128)} %reshape_reshape.9, f32[128,10240]{1,0:T(8,128)} %reshape_reshape.10, f32[128,10240]{1,0:T(8,128)} %reshape_reshape.11, f32[128,5]{1,0:T(8,128)S(1)} %reshape.385, f32[128,5]{1,0:T(8,128)S(1)} %reshape.386), dimensions={1} | concatenate | bytes 31467520 | tf_op jit(solution)/shard_map/concatenate | solution.py:40
  363.2 11.0 %pad.4 = f32[128,31744]{1,0:T(8,128)} pad(f32[128,30730]{1,0:T(8,128)} %concatenate.40, f32[]{:T(128)} %constant.21.clone.1), padding=0_0x0_1014 | pad | bytes 31986692 | tf_op jit(solution)/shard_map/jit(_pad)/pad | solution.py:42
  374.2 14.0 %reshape.387 = f32[31744,128]{1,0:T(8,128)} reshape(f32[128,31744]{1,0:T(8,128)} %pad.4) | data formatting | bytes 32505856 | tf_op jit(solution)/shard_map/reshape | solution.py:42
  398.2 69.4 %all-reduce.16 = (f32[640]{0:T(1024)S(1)}, f32[256]{0:T(256)S(1)}, f32[256]{0:T(256)S(1)}, f32[640]{0:T(1024)S(1)}) all-reduce(f32[640]{0:T(1024)S(1)} %get-tuple-element.19, f32[256]{0:T(256)S(1)} %reduce_sum.226, f32[256]{0:T(256)S(1)} %get-tuple-element.23, f32[640]{0:T(1024)S(1)} %get-tuple-element.15), channel_id=7, replica_groups=mesh['dp'=128] {'dp'}, use_global_device_ids=true, to_apply=%region_27.28.clone | all-reduce | flops 1792 | bytes 14336
  472.1 154.8 %all-reduce.21.cloned.1.call-done = (f32[640,1024]{1,0:T(8,128)}, f32[640,256]{1,0:T(8,128)}, f32[640,256]{1,0:T(8,128)}, f32[1024,640]{1,0:T(8,128)}, f32[31744,128]{1,0:T(8,128)}) async-done(((f32[640,1024]{1,0:T(8,128)}, f32[640,256]{1,0:T(8,128)}, f32[640,256]{1,0:T(8,128)}, f32[1024,640]{1,0:T(8,128)}, f32[31744,128]{1,0:T(8,128)}), (f32[640,1024]{1,0:T(8,128)}, f32[640,256]{1,0:T(8,128)}, ...) | async-done | bytes 22806544
  (225 shorter events, 91.2 us)
Async XLA Ops:
  7.2 83.9 %all-gather.11.cloned.1.call-start = ((), (), s32[]{:S(2)}) async-start(), calls=%async_computation.2 | async-start | bytes 3170304 | tf_op jit(solution)/shard_map/all_gather | solution.py:18
  8.6 136.8 %all-gather.7.cloned.1.call-start = ((), (), s32[]{:S(2)}) async-start(), calls=%async_computation | async-start | bytes 1320960 | tf_op jit(solution)/shard_map/all_gather | solution.py:173
  9.4 207.3 %all-gather.13.cloned.1.call-start = ((), (), s32[]{:S(2)}) async-start(), calls=%async_computation.3 | async-start | bytes 8454144 | tf_op jit(solution)/shard_map/all_gather | solution.py:18
  10.9 271.9 %all-gather.9.cloned.1.call-start = ((), (), s32[]{:S(2)}) async-start(), calls=%async_computation.1 | async-start | bytes 2641920 | tf_op jit(solution)/shard_map/all_gather | solution.py:227
  11.4 615.4 %all-reduce.21.cloned.1.call-start = ((), (), s32[]{:S(2)}) async-start(), calls=%async_computation.4 | async-start | bytes 45613056
  89.7 23.8 %copy-start.24 = (f32[256,128]{1,0:T(8,128)}, f32[256,128]{1,0:T(8,128)S(1)}, u32[]{:S(2)}) copy-start(f32[256,128]{1,0:T(8,128)S(1)} %get-tuple-element.70) | copy-start | bytes 393220
  94.1 14.3 %copy-start.7 = (bf16[640,1536]{1,0:T(8,128)(2,1)}, bf16[640,1536]{1,0:T(8,128)(2,1)S(1)}, u32[]{:S(2)}) copy-start(bf16[640,1536]{1,0:T(8,128)(2,1)S(1)} %reshape.405) | copy-start | bytes 5898244
  95.4 21.5 %collective-permute-start.1 = (bf16[256,256]{1,0:T(8,128)(2,1)}, bf16[256,256]{1,0:T(8,128)(2,1)}, u32[]{:S(2)}, u32[]{:S(2)}) collective-permute-start(bf16[256,256]{1,0:T(8,128)(2,1)} %convolution_convert_fusion.2), channel_id=1, source_target_pairs={{0,1},{1,2},{2,3},{3,4},{4,5},{5,6},{6,7},{7,8},{8,9},{9,10},{10,1... | collective-permute-start | bytes 393224 | tf_op jit(solution)/shard_map/ppermute | solution.py:28
  98.3 18.7 %collective-permute-start = (bf16[256,256]{1,0:T(8,128)(2,1)}, bf16[256,256]{1,0:T(8,128)(2,1)}, u32[]{:S(2)}, u32[]{:S(2)}) collective-permute-start(bf16[256,256]{1,0:T(8,128)(2,1)} %convolution_convert_fusion.2), channel_id=1, source_target_pairs={{0,2},{1,3},{2,4},{3,5},{4,6},{5,7},{6,8},{7,9},{8,10},{9,11},{10,... | collective-permute-start | bytes 393224 | tf_op jit(solution)/shard_map/ppermute | solution.py:28
  103.6 10.1 %collective-permute-start.3 = (bf16[256,256]{0,1:T(8,128)(2,1)}, bf16[256,256]{0,1:T(8,128)(2,1)}, u32[]{:S(2)}, u32[]{:S(2)}) collective-permute-start(bf16[256,256]{0,1:T(8,128)(2,1)} %maximum_bitcast_fusion.7), channel_id=1, source_target_pairs={{0,1},{1,2},{2,3},{3,4},{4,5},{5,6},{6,7},{7,8},{8,9},{9,10},{10,1... | collective-permute-start | bytes 393224 | tf_op jit(solution)/shard_map/ppermute | solution.py:28
  105.5 8.2 %collective-permute-start.2 = (bf16[256,256]{0,1:T(8,128)(2,1)}, bf16[256,256]{0,1:T(8,128)(2,1)}, u32[]{:S(2)}, u32[]{:S(2)}) collective-permute-start(bf16[256,256]{0,1:T(8,128)(2,1)} %maximum_bitcast_fusion.7), channel_id=1, source_target_pairs={{0,2},{1,3},{2,4},{3,5},{4,6},{5,7},{6,8},{7,9},{8,10},{9,11},{10,... | collective-permute-start | bytes 393224 | tf_op jit(solution)/shard_map/ppermute | solution.py:28
  108.4 4.9 copy-start
  225.4 4.2 copy-start.9
  282.8 3.7 copy-start.6
  282.8 4.6 copy-start.36
  282.8 4.6 copy-start.37
  308.0 80.2 %collective-permute-start.6 = (bf16[256,256]{1,0:T(8,128)(2,1)}, bf16[256,256]{1,0:T(8,128)(2,1)}, u32[]{:S(2)}, u32[]{:S(2)}) collective-permute-start(bf16[256,256]{1,0:T(8,128)(2,1)} %get-tuple-element.60), channel_id=1, source_target_pairs={{1,0},{2,1},{3,2},{4,3},{5,4},{6,5},{7,6},{8,7},{9,8},{10,9},{11,1... | collective-permute-start | bytes 393224 | tf_op jit(solution)/shard_map/ppermute | solution.py:28
  310.2 78.0 %collective-permute-start.7 = (bf16[256,256]{1,0:T(8,128)(2,1)}, bf16[256,256]{1,0:T(8,128)(2,1)}, u32[]{:S(2)}, u32[]{:S(2)}) collective-permute-start(bf16[256,256]{1,0:T(8,128)(2,1)} %get-tuple-element.61), channel_id=1, source_target_pairs={{2,0},{3,1},{4,2},{5,3},{6,4},{7,5},{8,6},{9,7},{10,8},{11,9},{12,... | collective-permute-start | bytes 393224 | tf_op jit(solution)/shard_map/ppermute | solution.py:28
  319.7 3.9 copy-start.16
  319.7 70.9 %collective-permute-start.4 = (bf16[256,256]{0,1:T(8,128)(2,1)S(1)}, bf16[256,256]{0,1:T(8,128)(2,1)S(1)}, u32[]{:S(2)}, u32[]{:S(2)}) collective-permute-start(bf16[256,256]{0,1:T(8,128)(2,1)S(1)} %get-tuple-element.62), channel_id=1, source_target_pairs={{1,0},{2,1},{3,2},{4,3},{5,4},{6,5},{7,6},{8,7},{9,8},{10,9},{11,1... | collective-permute-start | bytes 393224 | tf_op jit(solution)/shard_map/ppermute | solution.py:28
  321.8 68.8 %collective-permute-start.5 = (bf16[256,256]{0,1:T(8,128)(2,1)S(1)}, bf16[256,256]{0,1:T(8,128)(2,1)}, u32[]{:S(2)}, u32[]{:S(2)}) collective-permute-start(bf16[256,256]{0,1:T(8,128)(2,1)S(1)} %get-tuple-element.63), channel_id=1, source_target_pairs={{2,0},{3,1},{4,2},{5,3},{6,4},{7,5},{8,6},{9,7},{10,8},{11,9},{12,... | collective-permute-start | bytes 393224 | tf_op jit(solution)/shard_map/ppermute | solution.py:28
  388.2 4.7 copy-start.20
  389.4 3.8 copy-start.28
  396.3 73.6 %copy-start.14 = (f32[256,640]{1,0:T(8,128)S(1)}, f32[256,640]{1,0:T(8,128)}, u32[]{:S(2)}) copy-start(f32[256,640]{1,0:T(8,128)} %copy-done.13) | copy-start | bytes 1966084
  (29 other events, 53.2 us)
Sparse Core Ops, SparseCore 0:
  11.7 69.5 all-gather.10
  84.0 61.2 all-gather.6
  148.9 67.6 all-gather.12
  219.7 63.0 all-gather.8
  394.6 232.2 all-reduce.20
where the time goes:
time: 646 us; the launch traced here: 643 us
  waiting for transfers between devices  296 us (46%)
  blocking collectives  139 us (22%)
  local copies, waits for them, and re-layouts  104 us (16%)
  matrix products  49.7 us (8%)
  other arithmetic  22.3 us (3%)
  starting transfers between devices  17.7 us (3%)
  between operations  14.7 us (2%)
    unnamed x6, waiting for transfers between devices  156 us
    unnamed x2, blocking collectives  139 us
    all_gather x2, waiting for transfers between devices, side_by_side(): whole, at, done = (lax.all_gather(both, axis, axis=dim, tiled=True), 0, [])  66.3 us
    all_gather x1, waiting for transfers between devices, per_device(): lax.all_gather(down_weight, 'dp', axis=0, tiled=True)  48.5 us
    unnamed x107, local copies, waits for them, and re-layouts  34.1 us
    all_gather x1, waiting for transfers between devices, per_device(): lax.all_gather(output_weight, 'dp', axis=0, tiled=True)  24.9 us
    another operation x3, local copies, waits for them, and re-layouts, one_scatter(): lines = jnp.concatenate([b.reshape(size, -1) for b in tiles], axis=1)  18.3 us
    ppermute x8, starting transfers between devices, shifted(): lax.ppermute(value, axis, [(source, source + steps) for source in range(f...  17.5 us
  transfers between devices with their start and end apart: 13, of which 4 were waited for; matrix products, arithmetic and copies ran while one was open for 20% of the time, Pallas kernels for 0%

commit v1 on v0

--- a/solution.py
+++ b/solution.py
@@ -3,6 +3,8 @@
 import jax
 import jax.numpy as jnp
 from jax import lax
+from jax.experimental import pallas as pl
+from jax.experimental.pallas import tpu as pltpu
 from jax.sharding import PartitionSpec as P
 
 WINDOW = 512
@@ -11,41 +13,12 @@
 EPSILON = 1e-06
 ROPE_BASE = 10000.0
 NEG_FILL = -1e30
-
-
-def side_by_side(arrays, axis, dim, along):
-    both = jnp.concatenate(arrays, axis=along)
-    whole, at, done = (lax.all_gather(both, axis, axis=dim, tiled=True), 0, [])
-    for a in arrays:
-        done.append(lax.slice_in_dim(whole, at, at + a.shape[along], axis=along))
-        at += a.shape[along]
-    return tuple(done)
 
 
 def shifted(value, axis, steps):
     count = lax.axis_size(axis)
     first, last = (max(0, -steps), min(count, count - steps))
     return lax.ppermute(value, axis, [(source, source + steps) for source in range(first, last)])
-
-
-def in_blocks(x, dim, size):
-    lengths = x.shape
-    tiles = x.reshape(*lengths[:dim], size, lengths[dim] // size, *lengths[dim + 1 :])
-    return jnp.moveaxis(tiles, dim, 0)
-
-
-def one_scatter(arrays, axis, dims):
-    size = lax.axis_size(axis)
-    tiles = [in_blocks(a, dim, size) for a, dim in zip(arrays, dims)]
-    lines = jnp.concatenate([b.reshape(size, -1) for b in tiles], axis=1)
-    rows = max(16, -(-lines.shape[1] // 1024) * 8)
-    lines = jnp.pad(lines, ((0, 0), (0, rows * 128 - lines.shape[1]))).reshape(-1, 128)
-    flat, at, done = (lax.psum_scatter(lines, axis, tiled=True).reshape(-1), 0, [])
-    for b in tiles:
-        part = b[0]
-        done.append(flat[at : at + part.size].reshape(part.shape))
-        at += part.size
-    return tuple(done)
 
 
 def norm_parts(values):
@@ -119,6 +92,484 @@
     return lax.dot_general(
         left_side, right_side, (((0,), (0,)), ((), ())), preferred_element_type=jnp.float32
     )
+
+
+MESH = pl.DeviceIdType.MESH
+BF = jnp.bfloat16
+F32 = jnp.float32
+WX, WZ, WD, WO = 1408, 1536, 640, 384
+HID_A = 512
+VMEM_CAP = 60 << 20
+
+
+def place(x, z, y, c):
+    return ((x % 4) * 4 + (z % 4)) * 8 + (y % 4) * 2 + c
+
+
+class Links:
+    def __init__(self, send_sems, recv_sems):
+        me = lax.axis_index("dp")
+        self.at = {"x": me // 32, "z": (me // 8) % 4, "y": (me // 2) % 4}
+        self.core = me % 2
+        self.send_sems, self.recv_sems, self.used, self.open = send_sems, recv_sems, 0, []
+
+    def peer(self, axis, steps):
+        moved = dict(self.at)
+        moved[axis] = moved[axis] + steps
+        return place(moved["x"], moved["z"], moved["y"], self.core)
+
+    def sibling(self):
+        return place(self.at["x"], self.at["z"], self.at["y"], 1 - self.core)
+
+    def slot(self, axis, steps):
+        return (self.at[axis] + steps) % 4
+
+    def barrier(self):
+        sem = pltpu.get_barrier_semaphore()
+        partners = [self.sibling()]
+        for axis in ("x", "z", "y"):
+            partners += [self.peer(axis, o) for o in (1, 2, 3)]
+        for p in partners:
+            pl.semaphore_signal(sem, inc=1, device_id=(p,), device_id_type=MESH)
+        pl.semaphore_wait(sem, len(partners))
+
+    def send(self, src, dst, target):
+        i = self.used
+        self.used += 1
+        copy = pltpu.make_async_remote_copy(
+            src_ref=src,
+            dst_ref=dst,
+            send_sem=self.send_sems.at[i],
+            recv_sem=self.recv_sems.at[i],
+            device_id=(target,),
+            device_id_type=MESH,
+        )
+        copy.start()
+        self.open.append(copy.wait_send)
+        return copy
+
+    def local(self, src, dst):
+        i = self.used
+        self.used += 1
+        copy = pltpu.make_async_copy(src, dst, self.send_sems.at[i])
+        copy.start()
+        return copy
+
+    def finish(self):
+        for wait in self.open:
+            wait()
+
+
+def gather_kernel(
+    q_ref, k_ref, v_ref, o_ref, g_ref, u_ref, d_ref, n_ref,
+    wx, wz, wd, wo,
+    own_x, own_z, own_o, e_src_x, e_dst_x, e_src_z, e_dst_z, e_src_o, e_dst_o,
+    s1x, s1z, s1o, s2x, s2z, tmp, b3x, b3z,
+    send_sems, recv_sems,
+):
+    net = Links(send_sems, recv_sems)
+    core = net.core
+    other = 1 - core
+    sib = net.sibling()
+    own_x[...] = jnp.zeros_like(own_x)
+    own_z[...] = jnp.zeros_like(own_z)
+    own_o[...] = jnp.zeros_like(own_o)
+    own_x[0, 0:5, 0:1024] = q_ref[...].astype(F32)
+    own_x[0, 0:5, 1024:1280] = k_ref[...].astype(F32)
+    own_x[0, 0:5, 1280:1408] = n_ref[...].astype(F32)
+    own_x[1, 0:5, 0:256] = v_ref[...].astype(F32)
+    own_x[1, 0:5, 256:768] = g_ref[:, 0:HID_A].astype(F32)
+    own_x[1, 0:5, 768:1280] = u_ref[:, 0:HID_A].astype(F32)
+    own_z[0, 0:5, :] = g_ref[:, HID_A:].astype(F32)
+    own_z[1, 0:5, :] = u_ref[:, HID_A:].astype(F32)
+    own_o[0, 0:8, :] = o_ref[:, 0:384].astype(F32)
+    own_o[1, 0:8, 0:256] = o_ref[:, 384:640].astype(F32)
+    e_src_x[...] = own_x[other].astype(BF)
+    e_src_z[...] = own_z[other].astype(BF)
+    e_src_o[...] = own_o[other].astype(BF)
+    net.barrier()
+
+    swaps = [
+        net.send(e_src_x, e_dst_x, sib),
+        net.send(e_src_z, e_dst_z, sib),
+        net.send(e_src_o, e_dst_o, sib),
+    ]
+    xz = net.at["x"] * 4 + net.at["z"]
+    d_rows = wd.at[xz, net.at["y"], core]
+    d1 = [net.send(d_ref, d_rows, net.peer("z", o)) for o in (1, 2, 3)]
+    locals_ = [net.local(d_ref, d_rows)]
+
+    streams = []
+    for own, e_dst, s1, s2, b3, w, width, axes, swap in (
+        (own_x, e_dst_x, s1x, s2x, b3x, wx, WX, ("y", "z", "x"), swaps[0]),
+        (own_z, e_dst_z, s1z, s2z, b3z, wz, WZ, ("x", "y", "z"), swaps[1]),
+    ):
+        swap.wait_recv()
+        mine = own[core][0:5]
+        theirs = e_dst[...].astype(F32)[0:5]
+        first = core == 0
+        tmp[0:5, 0:width] = jnp.where(first, mine, theirs)
+        tmp[5:10, 0:width] = jnp.where(first, theirs, mine)
+        slot = s1.at[net.at[axes[0]]]
+        slot[...] = tmp[0:16, 0:width].astype(BF)
+        p1 = [net.send(slot, slot, net.peer(axes[0], o)) for o in (1, 2, 3)]
+        streams.append((s1, s2, b3, w, width, axes, p1))
+    swaps[2].wait_recv()
+    mine, theirs = own_o[core][0:8], e_dst_o[...].astype(F32)[0:8]
+    tmp[0:8, 0:WO] = jnp.where(core == 0, mine, theirs)
+    tmp[8:16, 0:WO] = jnp.where(core == 0, theirs, mine)
+    s1o[...] = tmp[0:16, 0:WO].astype(BF)
+    o_cols = pl.ds(pl.multiple_of(core * WO, 128), WO)
+    o_rows = wo.at[xz, net.at["y"], :, o_cols]
+    o1 = [net.send(s1o, o_rows, net.peer("z", o)) for o in (1, 2, 3)]
+    locals_.append(net.local(s1o, o_rows))
+
+    thirds = []
+    for s1, s2, b3, w, width, axes, p1 in streams:
+        for copy in p1:
+            copy.wait_recv()
+        for j in range(4):
+            tmp[10 * j : 10 * j + 10, 0:width] = s1[j].astype(F32)[0:10]
+        slot = s2.at[net.at[axes[1]]]
+        slot[...] = tmp[0:48, 0:width].astype(BF)
+        p2 = [net.send(slot, slot, net.peer(axes[1], o)) for o in (1, 2, 3)]
+        thirds.append((s2, b3, w, width, axes, p2))
+    for copy in d1 + o1:
+        copy.wait_recv()
+    for copy in locals_:
+        copy.wait()
+    x_rows = pl.ds(net.at["x"] * 4, 4)
+    d_part = wd.at[x_rows, net.at["y"], core]
+    o_part = wo.at[x_rows, net.at["y"], :, o_cols]
+    d2 = [net.send(d_part, d_part, net.peer("x", o)) for o in (1, 2, 3)]
+    o2 = [net.send(o_part, o_part, net.peer("x", o)) for o in (1, 2, 3)]
+
+    def view_of(w, width):
+        cols = pl.ds(pl.multiple_of(core * width, 128), width)
+        return lambda slot, at, n: w.at[slot, pl.ds(at, n), :, cols]
+
+    rings, ends = [], []
+    for s2, b3, w, width, axes, p2 in thirds:
+        for copy in p2:
+            copy.wait_recv()
+        for j in range(4):
+            tmp[40 * j : 40 * j + 40, 0:width] = s2[j].astype(F32)[0:40]
+        for j in range(10):
+            b3[j] = tmp[16 * j : 16 * j + 16, 0:width].astype(BF)
+        view = view_of(w, width)
+        dst = view(net.at[axes[2]], 0, 10)
+        ends.append(net.local(b3, dst).wait)
+        up = net.send(b3, dst, net.peer(axes[2], 1))
+        down = net.send(b3, dst, net.peer(axes[2], 3))
+        ends.append(net.send(b3, dst, sib).wait_recv)
+        rings.append((view, 10, axes[2], up, down))
+    for copy in d2 + o2:
+        copy.wait_recv()
+    for view in (
+        lambda slot, at, n: wd.at[pl.ds(at, n), slot, core],
+        lambda slot, at, n: wo.at[pl.ds(at, n), slot, :, o_cols],
+    ):
+        part = view(net.at["y"], 0, 16)
+        up = net.send(part, part, net.peer("y", 1))
+        down = net.send(part, part, net.peer("y", 3))
+        ends.append(net.send(part, part, sib).wait_recv)
+        rings.append((view, 16, "y", up, down))
+    fars = []
+    for view, n, axis, up, down in rings:
+        up.wait_recv()
+        part = view(net.slot(axis, 3), 0, n // 2)
+        fars.append((net.send(part, part, net.peer(axis, 1)), view, axis, 0, n // 2))
+        whole = view(net.slot(axis, 3), 0, n)
+        ends.append(net.send(whole, whole, sib).wait_recv)
+        down.wait_recv()
+        part = view(net.slot(axis, 1), n // 2, n // 2)
+        fars.append((net.send(part, part, net.peer(axis, 3)), view, axis, n // 2, n // 2))
+        whole = view(net.slot(axis, 1), 0, n)
+        ends.append(net.send(whole, whole, sib).wait_recv)
+    for copy, view, axis, at, n in fars:
+        copy.wait_recv()
+        part = view(net.slot(axis, 2), at, n)
+        ends.append(net.send(part, part, sib).wait_recv)
+    for wait in ends:
+        wait()
+    net.finish()
+
+
+def gather_all(q, k, v, o, g, u, d, n):
+    sems = 80
+    anywhere = pl.BlockSpec(memory_space=pl.ANY)
+    inside = pl.BlockSpec(memory_space=pltpu.VMEM)
+    return pl.pallas_call(
+        gather_kernel,
+        out_shape=(
+            jax.ShapeDtypeStruct((4, 10, 16, 2 * WX), BF),
+            jax.ShapeDtypeStruct((4, 10, 16, 2 * WZ), BF),
+            jax.ShapeDtypeStruct((16, 4, 2, 16, WD), BF),
+            jax.ShapeDtypeStruct((16, 4, 16, 2 * WO), BF),
+        ),
+        in_specs=[inside] * 8,
+        out_specs=(anywhere,) * 4,
+        scratch_shapes=[
+            pltpu.VMEM((2, 16, WX), F32),
+            pltpu.VMEM((2, 16, WZ), F32),
+            pltpu.VMEM((2, 16, WO), F32),
+            pltpu.VMEM((16, WX), BF),
+            pltpu.VMEM((16, WX), BF),
+            pltpu.VMEM((16, WZ), BF),
+            pltpu.VMEM((16, WZ), BF),
+            pltpu.VMEM((16, WO), BF),
+            pltpu.VMEM((16, WO), BF),
+            pltpu.VMEM((4, 16, WX), BF),
+            pltpu.VMEM((4, 16, WZ), BF),
+            pltpu.VMEM((16, WO), BF),
+            pltpu.VMEM((4, 48, WX), BF),
+            pltpu.VMEM((4, 48, WZ), BF),
+            pltpu.VMEM((160, WZ), F32),
+            pltpu.VMEM((10, 16, WX), BF),
+            pltpu.VMEM((10, 16, WZ), BF),
+            pltpu.SemaphoreType.DMA((sems,)),
+            pltpu.SemaphoreType.DMA((sems,)),
+        ],
+        compiler_params=pltpu.CompilerParams(
+            collective_id=0, has_side_effects=True, vmem_limit_bytes=VMEM_CAP
+        ),
+        name="gather_weights",
+    )(q, k, v, o, g, u, d, n)
+
+
+def scatter_kernel(
+    gx, gz, gd, go,
+    rx, rz, rd, ro,
+    ax, az, ad, ao, bx, bz, bd, bo,
+    fx, fz, fd, fo, nx, nz, nd, no,
+    t2x, t2z, t2d, t2o, r2x, r2z, r2d, r2o,
+    t1x, t1z, t1d, t1o, r1x, r1z, r1d, r1o,
+    sum_x, sum_z, sum_d, sum_o, swap_x, swap_z, swap_o, got_x, got_z, got_o,
+    send_sems, recv_sems,
+):
+    net = Links(send_sems, recv_sems)
+    core = net.core
+    other = 1 - core
+    sib = net.sibling()
+    xz = net.at["x"] * 4 + net.at["z"]
+
+    def cols(which, width):
+        return pl.ds(pl.multiple_of(which * width, 128), width)
+
+    views = {
+        "x": lambda t, which: gx.at[t, :, :, cols(which, WX)],
+        "z": lambda t, which: gz.at[t, :, :, cols(which, WZ)],
+        "d": lambda t, which: gd.at[:, t, which],
+        "o": lambda t, which: go.at[:, t, :, cols(which, WO)],
+    }
+    plan = (
+        ("x", ax, bx, fx, nx, 10, "x"),
+        ("z", az, bz, fz, nz, 10, "z"),
+        ("d", ad, bd, fd, nd, 16, "y"),
+        ("o", ao, bo, fo, no, 16, "y"),
+    )
+    order = (2, 1, 3, 0)
+    mine = {}
+    for steps in order:
+        for name, a, b, f, n, blocks, axis in plan:
+            t = net.slot(axis, steps)
+            mine[name, steps] = net.local(views[name](t, core), a.at[steps])
+    net.barrier()
+    swaps = {}
+    for steps in order:
+        for name, a, b, f, n, blocks, axis in plan:
+            t = net.slot(axis, steps)
+            swaps[name, steps] = net.send(views[name](t, other), b.at[steps], sib)
+
+    def add_rows(out, left, right, count):
+        def body(i, carry):
+            out[i] = (left[i].astype(F32) + right[i].astype(F32)).astype(BF)
+            return carry
+
+        lax.fori_loop(0, count, body, 0)
+
+    onward, near = {}, {}
+    for steps in order:
+        for name, a, b, f, n, blocks, axis in plan:
+            half = blocks // 2
+            mine[name, steps].wait()
+            swaps[name, steps].wait_recv()
+            add_rows(a.at[steps], a.at[steps], b.at[steps], blocks)
+            lo, hi = pl.ds(0, half), pl.ds(half, half)
+            if steps == 2:
+                onward[name, 1] = net.send(a.at[2, lo], f.at[0], net.peer(axis, 1))
+                onward[name, 3] = net.send(a.at[2, hi], f.at[1], net.peer(axis, 3))
+            elif steps == 1:
+                near[name, "a"] = net.send(a.at[1, hi], n.at[0, hi], net.peer(axis, 1))
+            elif steps == 3:
+                near[name, "b"] = net.send(a.at[3, lo], n.at[1, lo], net.peer(axis, 3))
+    for name, a, b, f, n, blocks, axis in plan:
+        half = blocks // 2
+        lo, hi = pl.ds(0, half), pl.ds(half, half)
+        onward[name, 1].wait_recv()
+        add_rows(a.at[1, lo], a.at[1, lo], f.at[0], half)
+        near[name, "c"] = net.send(a.at[1, lo], n.at[0, lo], net.peer(axis, 1))
+        onward[name, 3].wait_recv()
+        add_rows(a.at[3, hi], a.at[3, hi], f.at[1], half)
+        near[name, "d"] = net.send(a.at[3, hi], n.at[1, hi], net.peer(axis, 3))
+
+    def arrived(name):
+        for part in "abcd":
+            near[name, part].wait_recv()
+
+    def total3(a, n, i):
+        return a[0, i].astype(F32) + n[0, i].astype(F32) + n[1, i].astype(F32)
+
+    seconds = []
+    for name, a, n, total, t2, r2, t1, r1, width, axes in (
+        ("x", ax, nx, sum_x, t2x, r2x, t1x, r1x, WX, ("y", "z")),
+        ("z", az, nz, sum_z, t2z, r2z, t1z, r1z, WZ, ("x", "y")),
+    ):
+        arrived(name)
+        for i in range(10):
+            total[16 * i : 16 * i + 16] = total3(a, n, i)
+        for j in range(4):
+            t2[j, 0:32] = total[40 * j : 40 * j + 32].astype(BF)
+            t2[j, 32:48] = jnp.concatenate(
+                [total[40 * j + 32 : 40 * j + 40], jnp.zeros((8, width), F32)], axis=0
+            ).astype(BF)
+        p2 = [
+            net.send(t2.at[net.slot(axes[1], o)], r2.at[o - 1], net.peer(axes[1], o))
+            for o in (1, 2, 3)
+        ]
+        seconds.append((total, t2, r2, t1, r1, width, axes, p2))
+    flat2 = []
+    for name, a, n, t2, r2 in (("d", ad, nd, t2d, r2d), ("o", ao, no, t2o, r2o)):
+        arrived(name)
+
+        def body(i, carry, a=a, n=n, t2=t2):
+            t2[i] = total3(a, n, i).astype(BF)
+            return carry
+
+        lax.fori_loop(0, 16, body, 0)
+        p2 = [
+            net.send(
+                t2.at[pl.ds(net.slot("x", o) * 4, 4)], r2.at[o - 1], net.peer("x", o)
+            )
+            for o in (1, 2, 3)
+        ]
+        flat2.append(p2)
+
+    firsts = []
+    for total, t2, r2, t1, r1, width, axes, p2 in seconds:
+        for copy in p2:
+            copy.wait_recv()
+        own = t2[net.at[axes[1]]].astype(F32)
+        for o in range(3):
+            own = own + r2[o].astype(F32)
+        total[0:48] = own
+        for j in range(4):
+            part = total[10 * j : 10 * j + 10]
+            t1[j] = jnp.concatenate([part, jnp.zeros((6, width), F32)], axis=0).astype(BF)
+        p1 = [
+            net.send(t1.at[net.slot(axes[0], o)], r1.at[o - 1], net.peer(axes[0], o))
+            for o in (1, 2, 3)
+        ]
+        firsts.append((total, t1, r1, width, axes, p1))
+    flat1 = []
+    for (t2, r2, t1, r1), p2 in zip(((t2d, r2d, t1d, r1d), (t2o, r2o, t1o, r1o)), flat2):
+        for copy in p2:
+            copy.wait_recv()
+        for j in range(4):
+            value = t2[net.at["x"] * 4 + j].astype(F32)
+            for o in range(3):
+                value = value + r2[o, j].astype(F32)
+            t1[j] = value.astype(BF)
+        flat1.append(
+            [
+                net.send(t1.at[net.slot("z", o)], r1.at[o - 1], net.peer("z", o))
+                for o in (1, 2, 3)
+            ]
+        )
+
+    last = []
+    for (total, t1, r1, width, axes, p1), swap, got, out in zip(
+        firsts, (swap_x, swap_z), (got_x, got_z), (rx, rz)
+    ):
+        for copy in p1:
+            copy.wait_recv()
+        own = t1[net.at[axes[0]]].astype(F32)
+        for o in range(3):
+            own = own + r1[o].astype(F32)
+        total[0:16] = own
+        low_rows = total[0:8]
+        high_rows = total[5:13]
+        first = core == 0
+        swap[...] = jnp.where(first, high_rows, low_rows)
+        out[core] = jnp.where(first, low_rows, high_rows)
+        last.append((net.send(swap, got, sib), got, out))
+    for copy in flat1[0]:
+        copy.wait_recv()
+    own = t1d[net.at["z"]].astype(F32)
+    for o in range(3):
+        own = own + r1d[o].astype(F32)
+    rd[...] = own
+    for copy in flat1[1]:
+        copy.wait_recv()
+    own = t1o[net.at["z"]].astype(F32)
+    for o in range(3):
+        own = own + r1o[o].astype(F32)
+    first = core == 0
+    swap_o[...] = jnp.where(first, own[8:16], own[0:8])
+    ro[core] = jnp.where(first, own[0:8], own[8:16])
+    last.append((net.send(swap_o, got_o, sib), got_o, ro))
+    for copy, got, out in last:
+        copy.wait_recv()
+        out[other] = got[...]
+    net.finish()
+
+
+def scatter_all(gx, gz, gd, go):
+    sems = 120
+    anywhere = pl.BlockSpec(memory_space=pl.ANY)
+    inside = pl.BlockSpec(memory_space=pltpu.VMEM)
+    chunk = ((10, 16, WX), (10, 16, WZ), (16, 16, WD), (16, 16, WO))
+    halves = ((5, 16, WX), (5, 16, WZ), (8, 16, WD), (8, 16, WO))
+
+    def many(count, shapes, kind=BF):
+        return [pltpu.VMEM((count, *s) if count else s, kind) for s in shapes]
+
+    return pl.pallas_call(
+        scatter_kernel,
+        out_shape=(
+            jax.ShapeDtypeStruct((2, 8, WX), F32),
+            jax.ShapeDtypeStruct((2, 8, WZ), F32),
+            jax.ShapeDtypeStruct((16, WD), F32),
+            jax.ShapeDtypeStruct((2, 8, WO), F32),
+        ),
+        in_specs=[anywhere] * 4,
+        out_specs=(inside,) * 4,
+        scratch_shapes=[
+            *many(4, chunk),
+            *many(4, chunk),
+            *many(2, halves),
+            *many(2, chunk),
+            *many(0, ((4, 48, WX), (4, 48, WZ), (16, 16, WD), (16, 16, WO))),
+            *many(0, ((3, 48, WX), (3, 48, WZ), (3, 4, 16, WD), (3, 4, 16, WO))),
+            *many(0, ((4, 16, WX), (4, 16, WZ), (4, 16, WD), (4, 16, WO))),
+            *many(0, ((3, 16, WX), (3, 16, WZ), (3, 16, WD), (3, 16, WO))),
+            *many(0, ((160, WX), (160, WZ), (16, WD), (16, WO)), F32),
+            *many(0, ((8, WX), (8, WZ), (8, WO)) * 2, F32),
+            pltpu.SemaphoreType.DMA((sems,)),
+            pltpu.SemaphoreType.DMA((sems,)),
+        ],
+        compiler_params=pltpu.CompilerParams(
+            collective_id=1, has_side_effects=True, vmem_limit_bytes=VMEM_CAP
+        ),
+        name="scatter_grads",
+    )(gx, gz, gd, go)
+
+
+def turned_order():
+    spot = jnp.arange(640, dtype=jnp.int32)
+    z, y, x, rest = spot // 160, (spot // 40) % 4, (spot // 10) % 4, spot % 10
+    source = x * 160 + z * 40 + y * 10 + rest
+    return (jnp.arange(640, dtype=jnp.int32)[:, None] == source[None, :]).astype(jnp.bfloat16)
 
 
 def per_device(
@@ -159,23 +610,31 @@
         & (key_index[None, :] >= 0)
     )
     cosine, sine_table = rotary(position.astype(jnp.float32), head_dim)
-    (
-        query_full,
-        key_full,
-        value_full,
-        output_full,
-        input_full,
-        qgain_full,
-        kgain_full,
-        mixer_full,
-    ) = (
-        *side_by_side((query_weight, key_weight, value_weight), "dp", 0, 1),
-        lax.all_gather(output_weight, "dp", axis=0, tiled=True),
-        lax.all_gather(input_gain, "dp", axis=0, tiled=True),
-        lax.all_gather(query_gain, "dp", axis=0, tiled=True),
-        lax.all_gather(key_gain, "dp", axis=0, tiled=True),
-        lax.all_gather(mixer_gain, "dp", axis=0, tiled=True),
-    )
+    gains = jnp.stack(
+        [input_gain, mixer_gain, middle_gain, output_gain]
+        + [jnp.pad(a, (0, 3)) for a in (query_gain, key_gain)],
+        axis=1,
+    )
+    gains = jnp.pad(gains, ((0, 0), (0, 122)))
+    got_x, got_z, got_d, got_o = gather_all(
+        query_weight, key_weight, value_weight, output_weight, gate_weight, up_weight, down_weight,
+        gains,
+    )
+    got_x = got_x.reshape(640, 2 * WX)
+    got_z = got_z.reshape(640, 2 * WZ)
+    down_full = got_d.reshape(2048, 640)
+    output_full = got_o.reshape(1024, 2 * WO)[:, :640]
+    query_full = got_x[:, 0:1024]
+    key_full = got_x[:, 1024:1280]
+    value_full = got_x[:, WX : WX + 256]
+    gain_columns = got_x[:, 1280:1408]
+    input_full, mixer_full, middle_full, outgain_full = [gain_columns[:, i] for i in range(4)]
+    head_gains = gain_columns.reshape(128, 5, 128)
+    qgain_full = head_gains[:, :2, 4].reshape(256)
+    kgain_full = head_gains[:, :2, 5].reshape(256)
+    gate_a, up_a = got_x[:, WX + 256 : WX + 768], got_x[:, WX + 768 : WX + 1280]
+    gate_b, up_b = got_z[:, :WZ], got_z[:, WZ:]
+    turn = turned_order()
     input_mult = 1.0 + input_full.astype(jnp.float32)
     query_mult = 1.0 + qgain_full.astype(jnp.float32)
     key_mult = 1.0 + kgain_full.astype(jnp.float32)
@@ -222,40 +681,41 @@
     mixer_out = mat_mul(attended, output_full)
     mixer_unit, mixer_inv = norm_parts(mixer_out)
     middle = hidden + mixer_unit * mixer_mult
-    gate_full, up_full, down_full, middle_full, outgain_full = (
-        *side_by_side((gate_weight, up_weight), "dp", 0, 1),
-        lax.all_gather(down_weight, "dp", axis=0, tiled=True),
-        lax.all_gather(middle_gain, "dp", axis=0, tiled=True),
-        lax.all_gather(output_gain, "dp", axis=0, tiled=True),
-    )
     middle_mult = 1.0 + middle_full.astype(jnp.float32)
     output_mult = 1.0 + outgain_full.astype(jnp.float32)
     middle_unit, middle_inv = norm_parts(middle)
     middle_normed = (middle_unit * middle_mult).astype(jnp.bfloat16)
-    gate_pre = mat_mul(middle_normed, gate_full)
-    up_proj = mat_mul(middle_normed, up_full)
+    middle_turned = mat_mul(middle_normed, turn).astype(jnp.bfloat16)
+    gate_pre = jnp.concatenate([mat_mul(middle_normed, gate_a), mat_mul(middle_turned, gate_b)], axis=1)
+    up_proj = jnp.concatenate([mat_mul(middle_normed, up_a), mat_mul(middle_turned, up_b)], axis=1)
     activation, gelu_pullback = jax.vjp(gelu_tanh, gate_pre)
     hidden_units = (activation * up_proj).astype(jnp.bfloat16)
     ffn_out = mat_mul(hidden_units, down_full)
     ffn_unit, ffn_inv = norm_parts(ffn_out)
     mixed_out = (middle + ffn_unit * output_mult).astype(jnp.bfloat16)
-    gate_back, up_back, down_back = (gate_full, up_full, down_full)
     grad_out = out_grad.astype(jnp.float32)
     output_gain_part = jnp.sum(grad_out * ffn_unit, axis=0)
     grad_ffn = norm_back(grad_out * output_mult, ffn_unit, ffn_inv).astype(jnp.bfloat16)
-    grad_hidden = mat_mul_t(grad_ffn, down_back)
-    down_grad_full = mat_t_mul(hidden_units, grad_ffn)
+    grad_hidden = mat_mul_t(grad_ffn, down_full)
+    down_term = mat_t_mul(hidden_units, grad_ffn).astype(jnp.bfloat16)
     grad_gate = gelu_pullback(grad_hidden * up_proj)[0].astype(jnp.bfloat16)
     grad_up = (grad_hidden * activation).astype(jnp.bfloat16)
-    grad_middle_in = mat_mul_t(grad_gate, gate_back) + mat_mul_t(grad_up, up_back)
+    grad_turned = mat_mul_t(grad_gate[:, HID_A:], gate_b) + mat_mul_t(grad_up[:, HID_A:], up_b)
+    turned_high = grad_turned.astype(jnp.bfloat16)
+    turned_low = (grad_turned - turned_high.astype(jnp.float32)).astype(jnp.bfloat16)
+    grad_middle_in = (
+        mat_mul_t(grad_gate[:, :HID_A], gate_a)
+        + mat_mul_t(grad_up[:, :HID_A], up_a)
+        + mat_mul_t(turned_high, turn)
+        + mat_mul_t(turned_low, turn)
+    )
     middle_gain_part = jnp.sum(grad_middle_in * middle_unit, axis=0)
-    gate_term = mat_t_mul(middle_normed, grad_gate)
-    up_term = mat_t_mul(middle_normed, grad_up)
-    down_grad, gate_grad, up_grad, middle_gain_grad, output_gain_grad = one_scatter(
-        (down_grad_full, gate_term, up_term, middle_gain_part, output_gain_part),
-        "dp",
-        (0, 0, 0, 0, 0),
-    )
+    gate_up_a = mat_t_mul(
+        middle_normed, jnp.concatenate([grad_gate[:, :HID_A], grad_up[:, :HID_A]], axis=1)
+    ).astype(jnp.bfloat16)
+    gate_up_b = mat_t_mul(
+        middle_turned, jnp.concatenate([grad_gate[:, HID_A:], grad_up[:, HID_A:]], axis=1)
+    ).astype(jnp.bfloat16)
     grad_middle = grad_out + norm_back(grad_middle_in * middle_mult, middle_unit, middle_inv)
     query_back, key_back, value_back, output_back = (query_full, key_full, value_full, output_full)
     mixer_gain_part = jnp.sum(grad_middle * mixer_unit, axis=0)
@@ -316,30 +776,46 @@
         + mat_mul_t(grad_key_raw, key_back)
         + mat_mul_t(grad_value, value_back)
     )
-    query_grad_full = mat_t_mul(normed, grad_query_raw)
-    key_grad_full = mat_t_mul(normed, grad_key_raw)
-    value_grad_full = mat_t_mul(normed, grad_value)
     input_gain_part = jnp.sum(grad_normed * input_unit, axis=0)
     input_grad = grad_middle + norm_back(grad_normed * input_mult, input_unit, input_inv)
-    (
-        query_wgrad,
-        key_wgrad,
-        value_wgrad,
-        output_wgrad,
-        input_gain_grad,
-        query_gain_grad,
-        key_gain_grad,
-        mixer_gain_grad,
-    ) = (
-        lax.psum_scatter(query_grad_full, "dp", scatter_dimension=0, tiled=True),
-        lax.psum_scatter(key_grad_full, "dp", scatter_dimension=0, tiled=True),
-        lax.psum_scatter(value_grad_full, "dp", scatter_dimension=0, tiled=True),
-        lax.psum_scatter(output_grad_full, "dp", scatter_dimension=0, tiled=True),
-        lax.psum_scatter(input_gain_part, "dp", scatter_dimension=0, tiled=True),
-        lax.psum_scatter(query_gain_part, "dp", scatter_dimension=0, tiled=True),
-        lax.psum_scatter(key_gain_part, "dp", scatter_dimension=0, tiled=True),
-        lax.psum_scatter(mixer_gain_part, "dp", scatter_dimension=0, tiled=True),
-    )
+    qk_term = mat_t_mul(normed, jnp.concatenate([grad_query_raw, grad_key_raw], axis=1))
+    value_term = mat_t_mul(normed, grad_value)
+    gain_terms = jnp.stack(
+        [input_gain_part, mixer_gain_part, middle_gain_part, output_gain_part]
+        + [
+            jnp.pad(a.reshape(128, 2), ((0, 0), (0, 3))).reshape(640)
+            for a in (query_gain_part, key_gain_part)
+        ],
+        axis=1,
+    )
+    term_x = jnp.concatenate(
+        [
+            qk_term.astype(jnp.bfloat16),
+            jnp.pad(gain_terms, ((0, 0), (0, 122))).astype(jnp.bfloat16),
+            value_term.astype(jnp.bfloat16),
+            gate_up_a,
+            jnp.zeros((640, 128), jnp.bfloat16),
+        ],
+        axis=1,
+    )
+    term_o = jnp.pad(output_grad_full.astype(jnp.bfloat16), ((0, 0), (0, 128)))
+    sum_x, sum_z, down_grad, sum_o = scatter_all(
+        term_x.reshape(4, 10, 16, 2 * WX),
+        gate_up_b.reshape(4, 10, 16, 2 * WZ),
+        down_term.reshape(16, 4, 2, 16, WD),
+        term_o.reshape(16, 4, 16, 2 * WO),
+    )
+    query_wgrad = sum_x[0, :5, :1024]
+    key_wgrad = sum_x[0, :5, 1024:1280]
+    value_wgrad = sum_x[1, :5, :256]
+    gate_grad = jnp.concatenate([sum_x[1, :5, 256:768], sum_z[0, :5]], axis=1)
+    up_grad = jnp.concatenate([sum_x[1, :5, 768:1280], sum_z[1, :5]], axis=1)
+    output_wgrad = jnp.concatenate([sum_o[0], sum_o[1, :, :256]], axis=1)
+    sums = sum_x[0, :5, 1280:1408]
+    input_gain_grad, mixer_gain_grad, middle_gain_grad, output_gain_grad = [
+        sums[:, i] for i in range(4)
+    ]
+    query_gain_grad, key_gain_grad = sums[:2, 4], sums[:2, 5]
     return (
         mixed_out,
         input_grad,

time: 646 us -> 211 us (0.33)
  waiting for transfers between devices: 296 us -> 0.02 us
  blocking collectives: 139 us -> 0 us
  Pallas kernels: 0 us -> 95.6 us
  local copies, waits for them, and re-layouts: 104 us -> 33.7 us
  between operations: 14.7 us -> 1.64 us
  matrix products: 49.7 us -> 42.7 us
    unnamed x6 -> x0, waiting for transfers between devices: 156 us -> none
    all_gather x4 -> x0, waiting for transfers between devices: 140 us -> none  [the longest x2 66.3 us: side_by_side(): whole, at, done = (lax.all_gather(both, axis, axis=dim, tiled=True), 0, [])]
    unnamed x2 -> x0, blocking collectives: 139 us -> none
    pallas_call x0 -> x2, Pallas kernels: none -> 95.6 us  [the longest x1 48 us: scatter_all(): pl.pallas_call(scatter_kernel, out_shape=(jax.ShapeDtypeStruct((2, 8, WX)...]
    unnamed x107 -> x69, local copies, waits for them, and re-layouts: 34.1 us -> 6.68 us
    reshape x7 -> x3, local copies, waits for them, and re-layouts: 17.2 us -> 0.38 us  [the longest x2 0.31 us: per_device(): a.reshape(128, 2)]
    concatenate x1, local copies, waits for them, and re-layouts: 16.9 us -> 0.71 us  [per_device(): jnp.concatenate([qk_term.astype(jnp.bfloat16), jnp.pad(gain_terms, ((0, 0...]
    another operation x4 -> x18, local copies, waits for them, and re-layouts: 19.1 us -> 5.46 us  [the longest x9 4.69 us: per_device(): jnp.stack([input_gain, mixer_gain, middle_gain, output_gain] + [jnp.pad(a...]
  transfers between devices with their start and end apart: 13 -> 8, of which waited for: 4 -> 0; matrix products, arithmetic and copies ran while one was open for 20% -> 14% of each run, Pallas kernels for 0% -> 0%
where the time goes in v1:
time: 211 us; the launch traced here: 208 us
  Pallas kernels  95.6 us (45%)
  matrix products  42.7 us (20%)
  local copies, waits for them, and re-layouts  33.7 us (16%)
  starting transfers between devices  17.6 us (8%)
  other arithmetic  17 us (8%)
    pallas_call x1, Pallas kernels, scatter_all(): pl.pallas_call(scatter_kernel, out_shape=(jax.ShapeDtypeStruct((2, 8, WX)...  48 us
    pallas_call x1, Pallas kernels, gather_all(): pl.pallas_call(gather_kernel, out_shape=(jax.ShapeDtypeStruct((4, 10, 16,...  47.6 us
    ppermute x8, starting transfers between devices, shifted(): lax.ppermute(value, axis, [(source, source + steps) for source in range(f...  17.6 us
    dot_general x11, matrix products, mat_mul_t(): lax.dot_general(left_side, right_side, (((1,), (1,)), ((), ())), preferre...  11.6 us
    dot_general x6, matrix products, mat_t_mul(): lax.dot_general(left_side, right_side, (((0,), (0,)), ((), ())), preferre...  11.2 us
    dot_general x10, matrix products, mat_mul(): return jnp.dot(left_side, right_side, preferred_element_type=jnp.float32)  9.87 us
    unnamed x69, local copies, waits for them, and re-layouts  6.68 us
    another operation x9, local copies, waits for them, and re-layouts, per_device(): jnp.stack([input_gain, mixer_gain, middle_gain, output_gain] + [jnp.pad(a...  4.69 us
  transfers between devices with their start and end apart: 8, of which 0 were waited for; matrix products, arithmetic and copies ran while one was open for 14% of the time, Pallas kernels for 0%

profile of v1, /device:TPU:1, one launch (start us, length us, event | category | flops | bytes accessed | tf_op | source)
XLA Modules:
  0.0 208.3 jit_solution(16761214016297243251)
XLA Ops:
  5.9 47.6 %gather_weights.1 = (bf16[4,10,16,2816]{3,2,1,0:T(8,128)(2,1)}, bf16[4,10,16,3072]{3,2,1,0:T(8,128)(2,1)}, bf16[16,4,2,16,640]{4,3,2,1,0:T(8,128)(2,1)}, bf16[16,4,16,768]{3,2,1,0:T(8,128)(2,1)}) custom-call(bf16[5,1024]{1,0:T(8,128)(2,1)} %q_ref.1, bf16[5,256]{1,0:T(8,128)(2,1)} %k_ref.1, bf16[5,256]{1,0:T(8,128)(2,1)} %v_ref.1, bf16[8,640]{1,0:T(8,128)(2,1)} %o_ref.1, ...), custom_call_target="tpu_custom_call" | custom-call | tf_op jit(solution)/shard_map/gather_weights/pallas_call | solution.py:302
  53.5 2.1 %fusion.149 = (bf16[640,1]{1,0:T(8,128)(2,1)S(1)}, bf16[640,1]{1,0:T(8,128)(2,1)}, bf16[640,1]{1,0:T(8,128)(2,1)S(1)}, bf16[640,1]{1,0:T(8,128)(2,1)S(1)}) fusion(bf16[640,2816]{1,0:T(8,128)(2,1)} %bitcast.143), kind=kLoop, calls=%fused_computation.283 | loop fusion | bytes 10240 | tf_op jit(solution)/shard_map/slice | solution.py:631
  60.8 1.9 collective-permute-start.3
  62.7 3.2 %collective-permute-start.2 = (bf16[256,256]{0,1:T(8,128)(2,1)}, bf16[256,256]{0,1:T(8,128)(2,1)}, u32[]{:S(2)}, u32[]{:S(2)}) collective-permute-start(bf16[256,256]{0,1:T(8,128)(2,1)} %maximum_bitcast_fusion.7), channel_id=1, source_target_pairs={{0,2},{1,3},{2,4},{3,5},{4,6},{5,7},{6,8},{7,9},{8,10},{9,11},{10,... | collective-permute-start | bytes 393224 | tf_op jit(solution)/shard_map/ppermute | solution.py:21
  65.9 1.9 convolution_convert_fusion.8
  67.9 2.0 collective-permute-start.1
  69.9 3.6 %collective-permute-start = (bf16[256,256]{1,0:T(8,128)(2,1)}, bf16[256,256]{1,0:T(8,128)(2,1)}, u32[]{:S(2)}, u32[]{:S(2)}) collective-permute-start(bf16[256,256]{1,0:T(8,128)(2,1)} %convolution_convert_fusion.8), channel_id=1, source_target_pairs={{0,2},{1,3},{2,4},{3,5},{4,6},{5,7},{6,8},{7,9},{8,10},{9,11},{10,... | collective-permute-start | bytes 393224 | tf_op jit(solution)/shard_map/ppermute | solution.py:21
  73.5 2.0 fusion.40
  80.6 1.7 fusion.152
  83.3 1.7 convolution_convert_fusion.6
  94.7 2.7 %multiply_convert_fusion = (bf16[256,2048]{1,0:T(8,128)(2,1)S(1)}, bf16[256,2048]{1,0:T(8,128)(2,1)S(1)}) fusion(f32[256,1536]{1,0:T(8,128)S(1)} %fusion.18, f32[256,512]{1,0:T(8,128)S(1)} %fusion.75, f32[256,1536]{1,0:T(8,128)S(1)} %fusion.14, f32[256,512]{1,0:T(8,128)S(1)} %fusion.71, bf16[256,640]{1,0:T(8,128)(2,1)S(1)} %get-tuple-element.68, ...), kind=kOutput, calls=%fused_computation.25 | convolution fusion | flops 684720128 | bytes 9240576 | tf_op jit(solution)/shard_map/dot_general | solution.py:86
  102.1 2.6 %convolution_convert_fusion.1 = bf16[2048,640]{1,0:T(8,128)(2,1)} fusion(bf16[256,2048]{1,0:T(8,128)(2,1)S(1)} %multiply_convert_fusion.1, bf16[256,640]{1,0:T(8,128)(2,1)S(1)} %get-tuple-element.68), kind=kOutput, calls=%fused_computation.1 | convolution fusion | flops 672399360 | bytes 3997696 | tf_op jit(solution)/shard_map/dot_general | solution.py:92
  108.9 1.6 fusion.154
  110.5 1.7 fusion.1
  113.3 1.5 fusion.153
  116.8 2.0 collective-permute-start.4
  118.7 1.8 fusion.27
  125.4 2.3 %collective-permute-start.6 = (bf16[256,256]{1,0:T(8,128)(2,1)}, bf16[256,256]{1,0:T(8,128)(2,1)}, u32[]{:S(2)}, u32[]{:S(2)}) collective-permute-start(bf16[256,256]{1,0:T(8,128)(2,1)} %get-tuple-element.70), channel_id=1, source_target_pairs={{1,0},{2,1},{3,2},{4,3},{5,4},{6,5},{7,6},{8,7},{9,8},{10,9},{11,1... | collective-permute-start | bytes 393224 | tf_op jit(solution)/shard_map/ppermute | solution.py:21
  127.8 3.1 %convolution_convert_fusion = bf16[640,3072]{1,0:T(8,128)(2,1)} fusion(bf16[256,640]{1,0:T(8,128)(2,1)S(1)} %copy-done.6, bf16[256,1536]{1,0:T(8,128)(2,1)S(1)} %copy-done.7, bf16[256,1536]{1,0:T(8,128)(2,1)S(1)} %copy-done.8), kind=kOutput, calls=%fused_computation | convolution fusion | flops 1011744768 | bytes 5832704 | tf_op jit(solution)/shard_map/dot_general | solution.py:92
  137.3 1.9 convolution_add_fusion
  139.2 2.0 fusion
  142.3 1.5 fusion.64
  146.4 1.7 fusion.23
  148.8 48.0 %scatter_grads.1 = (f32[2,8,1408]{2,1,0:T(8,128)}, f32[2,8,1536]{2,1,0:T(8,128)}, f32[16,640]{1,0:T(8,128)}, f32[2,8,384]{2,1,0:T(8,128)}) custom-call(bf16[4,10,16,2816]{3,2,1,0:T(8,128)(2,1)} %bitcast.165, bf16[4,10,16,3072]{3,2,1,0:T(8,128)(2,1)} %bitcast.139, bf16[16,4,2,16,640]{4,3,2,1,0:T(8,128)(2,1)} %bitcast.142, bf16[16,4,16,768]{3,2,1,0:T(8,128)(2,1)} %bitcast.155), custom_call_target="tpu_custom_call" | custom-call | tf_op jit(solution)/shard_map/scatter_grads/pallas_call | solution.py:537
  (208 shorter events, 64.4 us)
Async XLA Ops:
  0.6 56.1 %copy-start.1 = (bf16[256,640]{1,0:T(8,128)(2,1)S(1)}, bf16[256,640]{1,0:T(8,128)(2,1)}, u32[]{:S(2)}) copy-start(bf16[256,640]{1,0:T(8,128)(2,1)} %param.16) | copy-start | bytes 983044
  0.7 56.8 %copy-start.26 = (s32[64]{0:T(128)S(1)}, s32[64]{0:T(128)}, u32[]{:S(2)}) copy-start(s32[64]{0:T(128)} %param.30) | copy-start | bytes 772
  59.4 10.4 %copy-start.12 = (f32[256,256]{0,1:T(8,128)}, f32[256,256]{0,1:T(8,128)S(1)}, u32[]{:S(2)}) copy-start(f32[256,256]{0,1:T(8,128)S(1)} %get-tuple-element.87) | copy-start | bytes 786436
  60.8 19.8 %collective-permute-start.3 = (bf16[256,256]{0,1:T(8,128)(2,1)}, bf16[256,256]{0,1:T(8,128)(2,1)}, u32[]{:S(2)}, u32[]{:S(2)}) collective-permute-start(bf16[256,256]{0,1:T(8,128)(2,1)} %maximum_bitcast_fusion.7), channel_id=1, source_target_pairs={{0,1},{1,2},{2,3},{3,4},{4,5},{5,6},{6,7},{7,8},{8,9},{9,10},{10,1... | collective-permute-start | bytes 393224 | tf_op jit(solution)/shard_map/ppermute | solution.py:21
  62.7 17.9 %collective-permute-start.2 = (bf16[256,256]{0,1:T(8,128)(2,1)}, bf16[256,256]{0,1:T(8,128)(2,1)}, u32[]{:S(2)}, u32[]{:S(2)}) collective-permute-start(bf16[256,256]{0,1:T(8,128)(2,1)} %maximum_bitcast_fusion.7), channel_id=1, source_target_pairs={{0,2},{1,3},{2,4},{3,5},{4,6},{5,7},{6,8},{7,9},{8,10},{9,11},{10,... | collective-permute-start | bytes 393224 | tf_op jit(solution)/shard_map/ppermute | solution.py:21
  67.9 15.4 %collective-permute-start.1 = (bf16[256,256]{1,0:T(8,128)(2,1)}, bf16[256,256]{1,0:T(8,128)(2,1)}, u32[]{:S(2)}, u32[]{:S(2)}) collective-permute-start(bf16[256,256]{1,0:T(8,128)(2,1)} %convolution_convert_fusion.8), channel_id=1, source_target_pairs={{0,1},{1,2},{2,3},{3,4},{4,5},{5,6},{6,7},{7,8},{8,9},{9,10},{10,1... | collective-permute-start | bytes 393224 | tf_op jit(solution)/shard_map/ppermute | solution.py:21
  69.9 13.4 %collective-permute-start = (bf16[256,256]{1,0:T(8,128)(2,1)}, bf16[256,256]{1,0:T(8,128)(2,1)}, u32[]{:S(2)}, u32[]{:S(2)}) collective-permute-start(bf16[256,256]{1,0:T(8,128)(2,1)} %convolution_convert_fusion.8), channel_id=1, source_target_pairs={{0,2},{1,3},{2,4},{3,5},{4,6},{5,7},{6,8},{7,9},{8,10},{9,11},{10,... | collective-permute-start | bytes 393224 | tf_op jit(solution)/shard_map/ppermute | solution.py:21
  77.8 4.6 %copy-start.18 = (bf16[256,4,128]{2,0,1:T(8,128)(2,1)}, bf16[256,4,128]{2,0,1:T(8,128)(2,1)S(1)}, u32[]{:S(2)}) copy-start(bf16[256,4,128]{2,0,1:T(8,128)(2,1)S(1)} %get-tuple-element.64) | copy-start | bytes 786436
  77.8 4.6 %copy-start.20 = (bf16[256,4,128]{2,0,1:T(8,128)(2,1)}, bf16[256,4,128]{2,0,1:T(8,128)(2,1)S(1)}, u32[]{:S(2)}) copy-start(bf16[256,4,128]{2,0,1:T(8,128)(2,1)S(1)} %get-tuple-element.65) | copy-start | bytes 786436
  114.8 5.7 %copy-start.16 = (f32[256,128]{1,0:T(8,128)S(1)}, f32[256,128]{1,0:T(8,128)}, u32[]{:S(2)}) copy-start(f32[256,128]{1,0:T(8,128)} %copy-done.15) | copy-start | bytes 393220
  115.5 18.4 %collective-permute-start.5 = (bf16[256,256]{0,1:T(8,128)(2,1)}, bf16[256,256]{0,1:T(8,128)(2,1)}, u32[]{:S(2)}, u32[]{:S(2)}) collective-permute-start(bf16[256,256]{0,1:T(8,128)(2,1)} %get-tuple-element.73), channel_id=1, source_target_pairs={{2,0},{3,1},{4,2},{5,3},{6,4},{7,5},{8,6},{9,7},{10,8},{11,9},{12,... | collective-permute-start | bytes 393224 | tf_op jit(solution)/shard_map/ppermute | solution.py:21
  116.8 17.1 %collective-permute-start.4 = (bf16[256,256]{0,1:T(8,128)(2,1)}, bf16[256,256]{0,1:T(8,128)(2,1)}, u32[]{:S(2)}, u32[]{:S(2)}) collective-permute-start(bf16[256,256]{0,1:T(8,128)(2,1)} %get-tuple-element.72), channel_id=1, source_target_pairs={{1,0},{2,1},{3,2},{4,3},{5,4},{6,5},{7,6},{8,7},{9,8},{10,9},{11,1... | collective-permute-start | bytes 393224 | tf_op jit(solution)/shard_map/ppermute | solution.py:21
  122.4 5.3 %copy-start.6 = (bf16[256,640]{1,0:T(8,128)(2,1)S(1)}, bf16[256,640]{1,0:T(8,128)(2,1)}, u32[]{:S(2)}) copy-start(bf16[256,640]{1,0:T(8,128)(2,1)} %copy-done.5) | copy-start | bytes 983044
  122.4 5.3 %copy-start.7 = (bf16[256,1536]{1,0:T(8,128)(2,1)S(1)}, bf16[256,1536]{1,0:T(8,128)(2,1)}, u32[]{:S(2)}) copy-start(bf16[256,1536]{1,0:T(8,128)(2,1)} %slice.230) | copy-start | bytes 2359300
  122.4 5.3 %copy-start.8 = (bf16[256,1536]{1,0:T(8,128)(2,1)S(1)}, bf16[256,1536]{1,0:T(8,128)(2,1)}, u32[]{:S(2)}) copy-start(bf16[256,1536]{1,0:T(8,128)(2,1)} %slice.229) | copy-start | bytes 2359300
  124.1 17.2 %collective-permute-start.7 = (bf16[256,256]{1,0:T(8,128)(2,1)}, bf16[256,256]{1,0:T(8,128)(2,1)S(1)}, u32[]{:S(2)}, u32[]{:S(2)}) collective-permute-start(bf16[256,256]{1,0:T(8,128)(2,1)} %get-tuple-element.71), channel_id=1, source_target_pairs={{2,0},{3,1},{4,2},{5,3},{6,4},{7,5},{8,6},{9,7},{10,8},{11,9},{12,... | collective-permute-start | bytes 393224 | tf_op jit(solution)/shard_map/ppermute | solution.py:21
  125.4 5.5 %copy-start.2 = (f32[32,8,4,256]{3,1,2,0:T(8,128)S(1)}, f32[32,8,4,256]{3,1,2,0:T(8,128)}, u32[]{:S(2)}) copy-start(f32[32,8,4,256]{3,1,2,0:T(8,128)} %copy.216) | copy-start | bytes 3145732
  125.4 5.5 %copy-start.3 = (f32[4,32,8,256]{3,2,0,1:T(8,128)S(1)}, f32[4,32,8,256]{3,2,0,1:T(8,128)}, u32[]{:S(2)}) copy-start(f32[4,32,8,256]{3,2,0,1:T(8,128)} %copy.215) | copy-start | bytes 3145732
  125.4 15.9 %collective-permute-start.6 = (bf16[256,256]{1,0:T(8,128)(2,1)}, bf16[256,256]{1,0:T(8,128)(2,1)}, u32[]{:S(2)}, u32[]{:S(2)}) collective-permute-start(bf16[256,256]{1,0:T(8,128)(2,1)} %get-tuple-element.70), channel_id=1, source_target_pairs={{1,0},{2,1},{3,2},{4,3},{5,4},{6,5},{7,6},{8,7},{9,8},{10,9},{11,1... | collective-permute-start | bytes 393224 | tf_op jit(solution)/shard_map/ppermute | solution.py:21
  133.9 3.4 %copy-start.14 = (bf16[256,1024]{1,0:T(8,128)(2,1)S(1)}, bf16[256,1024]{1,0:T(8,128)(2,1)}, u32[]{:S(2)}) copy-start(bf16[256,1024]{1,0:T(8,128)(2,1)} %get-tuple-element.61) | copy-start | bytes 1572868
  142.3 4.1 %copy-start.11 = (bf16[256,640]{1,0:T(8,128)(2,1)S(1)}, bf16[256,640]{1,0:T(8,128)(2,1)}, u32[]{:S(2)}) copy-start(bf16[256,640]{1,0:T(8,128)(2,1)} %copy-done.10) | copy-start | bytes 983044
  142.3 4.1 %copy-start.23 = (bf16[256,512]{1,0:T(8,128)(2,1)S(1)}, bf16[256,512]{1,0:T(8,128)(2,1)}, u32[]{:S(2)}) copy-start(bf16[256,512]{1,0:T(8,128)(2,1)} %slice.228) | copy-start | bytes 786436
  142.3 4.1 %copy-start.24 = (bf16[256,512]{1,0:T(8,128)(2,1)S(1)}, bf16[256,512]{1,0:T(8,128)(2,1)}, u32[]{:S(2)}) copy-start(bf16[256,512]{1,0:T(8,128)(2,1)} %slice.227) | copy-start | bytes 786436
  196.9 10.8 %copy-start.25 = (f32[16,640]{1,0:T(8,128)S(1)}, f32[16,640]{1,0:T(8,128)}, u32[]{:S(2)}) copy-start(f32[16,640]{1,0:T(8,128)} %get-tuple-element.127) | copy-start | bytes 122884
  (13 other events, 23.6 us)

commit v2 on v0

v2 whole, which is shorter than its diff:
```python
import math

import jax
import jax.numpy as jnp
from jax import lax
from jax.experimental import pallas as pl
from jax.experimental.pallas import tpu as pltpu
from jax.sharding import PartitionSpec as P

MESH = pl.DeviceIdType.MESH
BF = jnp.bfloat16
F32 = jnp.float32
T = 256
D = 640
HD = 256
HEADS = 4
SPAN = 3 * T
WINDOW = 512
EPSILON = 1e-06
ROPE_BASE = 10000.0
NEG_FILL = -1e30
SCALE = 1.0 / math.sqrt(HD)
GELU_A = math.sqrt(2.0 / math.pi)
GELU_B = 0.044715
WX1, WZ1, WX2, WZ2, WD, WO = 512, 384, 1024, 1024, 640, 384
SEMS = 232
VMEM_CAP = 62 << 20


def place(x, z, y, c):
    return ((x % 4) * 4 + (z % 4)) * 8 + (y % 4) * 2 + c


class Links:
    def __init__(self, send_sems, recv_sems):
        self.me = lax.axis_index("dp")
        self.at = {"x": self.me // 32, "z": (self.me // 8) % 4, "y": (self.me // 2) % 4}
        self.core = self.me % 2
        self.other = 1 - self.core
        self.sib = place(self.at["x"], self.at["z"], self.at["y"], self.other)
        self.xz = self.at["x"] * 4 + self.at["z"]
        self.send_sems, self.recv_sems, self.used, self.open = send_sems, recv_sems, 0, []

    def peer(self, axis, steps):
        moved = dict(self.at)
        moved[axis] = moved[axis] + steps
        return place(moved["x"], moved["z"], moved["y"], self.core)

    def along(self, steps):
        return (self.me + 128 + steps) % 128

    def slot(self, axis, steps):
        return (self.at[axis] + steps) % 4

    def greet(self):
        sem = pltpu.get_barrier_semaphore()
        partners = [self.sib] + [self.along(s) for s in (1, 2, -1, -2)]
        for axis in ("x", "z", "y"):
            partners += [self.peer(axis, o) for o in (1, 2, 3)]
        for p in partners:
            pl.semaphore_signal(sem, inc=1, device_id=(p,), device_id_type=MESH)
        self.greeted = len(partners)

    def meet(self):
        pl.semaphore_wait(pltpu.get_barrier_semaphore(), self.greeted)

    def send(self, src, dst, target):
        i = self.used
        self.used += 1
        copy = pltpu.make_async_remote_copy(
            src_ref=src,
            dst_ref=dst,
            send_sem=self.send_sems.at[i],
            recv_sem=self.recv_sems.at[i],
            device_id=(target,),
            device_id_type=MESH,
        )
        copy.start()
        self.open.append(copy.wait_send)
        return copy

    def local(self, src, dst):
        i = self.used
        self.used += 1
        copy = pltpu.make_async_copy(src, dst, self.send_sems.at[i])
        copy.start()
        return copy

    def finish(self):
        for wait in self.open:
            wait()
        self.open = []


class Rows:
    def __init__(self, net, axes, width, refs):
        self.net, self.axes, self.width = net, axes, width
        self.own, self.e_src, self.e_dst, self.s1, self.s2, self.b3, self.w, self.tmp = refs
        self.ends = []

    def view(self, slot, at, n):
        rows = pl.ds(pl.multiple_of(slot * 160 + at * 16, 16), n * 16)
        return self.w.at[self.net.core, rows]

    def step0(self):
        self.e_src[...] = self.own[self.net.other].astype(BF)

    def step0b(self):
        self.swap = self.net.send(self.e_src, self.e_dst, self.net.sib)

    def step1(self):
        net, wide = self.net, slice(0, self.width)
        self.swap.wait_recv()
        mine = self.own[net.core][0:5]
        theirs = self.e_dst[...].astype(F32)[0:5]
        first = net.core == 0
        self.tmp[0:5, wide] = jnp.where(first, mine, theirs)
        self.tmp[5:10, wide] = jnp.where(first, theirs, mine)
        slot = self.s1.at[net.at[self.axes[0]]]
        slot[...] = self.tmp[0:16, wide].astype(BF)
        self.p = [net.send(slot, slot, net.peer(self.axes[0], o)) for o in (1, 2, 3)]

    def step2(self):
        net, wide = self.net, slice(0, self.width)
        for copy in self.p:
            copy.wait_recv()
        for j in range(4):
            self.tmp[10 * j : 10 * j + 10, wide] = self.s1[j].astype(F32)[0:10]
        slot = self.s2.at[net.at[self.axes[1]]]
        slot[...] = self.tmp[0:48, wide].astype(BF)
        self.p = [net.send(slot, slot, net.peer(self.axes[1], o)) for o in (1, 2, 3)]

    def step3(self):
        net, wide = self.net, slice(0, self.width)
        for copy in self.p:
            copy.wait_recv()
        for j in range(4):
            self.tmp[40 * j : 40 * j + 40, wide] = self.s2[j].astype(F32)[0:40]
        self.b3[...] = self.tmp[0:160, wide].astype(BF)
        axis = self.axes[2]
        dst = self.view(net.at[axis], 0, 10)
        self.up = net.send(self.b3, dst, net.peer(axis, 1))
        self.down = net.send(self.b3, dst, net.peer(axis, 3))
        self.ends.append(net.send(self.b3, dst, net.sib).wait_recv)
        self.ends.append(net.local(self.b3, dst).wait)

    blocks = 10

    def step4(self):
        net, axis, n = self.net, self.axes[2], self.blocks
        half = n // 2
        self.up.wait_recv()
        part = self.view(net.slot(axis, 3), 0, half)
        self.far_up = net.send(part, part, net.peer(axis, 1))
        self.down.wait_recv()
        part = self.view(net.slot(axis, 1), half, half)
        self.far_down = net.send(part, part, net.peer(axis, 3))
        for steps in (3, 1):
            whole = self.view(net.slot(axis, steps), 0, n)
            self.ends.append(net.send(whole, whole, net.sib).wait_recv)

    def step5(self):
        net, axis, half = self.net, self.axes[2], self.blocks // 2
        for copy, at in ((self.far_up, 0), (self.far_down, half)):
            copy.wait_recv()
            part = self.view(net.slot(axis, 2), at, half)
            self.ends.append(net.send(part, part, net.sib).wait_recv)

    def step6(self):
        for wait in self.ends:
            wait()


class Tiles(Rows):
    blocks = 16

    def __init__(self, net, w, by_core):
        self.net, self.w, self.by_core, self.axes = net, w, by_core, ("z", "x", "y")
        self.ends = []

    def view(self, slot, at, n):
        if self.by_core:
            return self.w.at[pl.ds(at, n), slot, self.net.core]
        return self.w.at[self.net.core, pl.ds(at, n), slot]

    def first(self, src):
        net = self.net
        dst = self.w.at[net.xz, net.at["y"], net.core] if self.by_core else self.w.at[net.core, net.xz, net.at["y"]]
        self.p = [net.send(src, dst, net.peer("z", o)) for o in (1, 2, 3)]
        self.kept = net.local(src, dst)

    def step2(self):
        net = self.net
        for copy in self.p:
            copy.wait_recv()
        self.kept.wait()
        part = self.view(net.at["y"], net.at["x"] * 4, 4)
        self.p = [net.send(part, part, net.peer("x", o)) for o in (1, 2, 3)]

    def step3(self):
        net = self.net
        for copy in self.p:
            copy.wait_recv()
        part = self.view(net.at["y"], 0, 16)
        self.up = net.send(part, part, net.peer("y", 1))
        self.down = net.send(part, part, net.peer("y", 3))
        self.ends.append(net.send(part, part, net.sib).wait_recv)


class RowSums:
    blocks = 10

    def __init__(self, net, axes, width, refs):
        self.net, self.axes, self.width = net, axes, width
        (self.g, self.b, self.f, self.n, self.t2, self.r2, self.t1, self.r1, self.total) = refs[:9]
        self.rest = refs[9:]
        self.swaps, self.onward, self.near = {}, {}, {}

    def view(self, steps, at, n, which):
        slot = self.net.slot(self.axes[2], steps)
        rows = pl.ds(pl.multiple_of(slot * 160 + at * 16, 16), n * 16)
        return self.g.at[which, rows]

    def rows(self, at, n):
        return pl.ds(at * 16, n * 16)

    def tile(self, steps, i):
        slot = self.net.slot(self.axes[2], steps)
        return (self.net.core, pl.ds(pl.multiple_of(slot * 160 + i * 16, 16), 16))

    def block(self, i):
        return pl.ds(pl.multiple_of(i * 16, 16), 16)

    def step0(self):
        net = self.net
        for steps in (2, 1, 3, 0):
            src = self.view(steps, 0, self.blocks, net.other)
            self.swaps[steps] = net.send(src, self.b.at[steps], net.sib)

    def add(self, steps, held, at, count):
        def body(i, carry):
            where = self.tile(steps, i + at)
            total = self.g[where].astype(F32) + held[self.block(i)].astype(F32)
            self.g[where] = total.astype(BF)
            return carry

        lax.fori_loop(0, count, body, 0)

    def step1(self):
        net, axis, n, core = self.net, self.axes[2], self.blocks, self.net.core
        half = n // 2
        for steps in (2, 1, 3, 0):
            self.swaps[steps].wait_recv()
            self.add(steps, self.b.at[steps], 0, n)
            if steps == 2:
                self.onward[1] = net.send(self.view(2, 0, half, core), self.f.at[0], net.peer(axis, 1))
                self.onward[3] = net.send(self.view(2, half, half, core), self.f.at[1], net.peer(axis, 3))
            elif steps == 1:
                self.near["a"] = net.send(
                    self.view(1, half, half, core), self.n.at[0, self.rows(half, half)], net.peer(axis, 1)
                )
            elif steps == 3:
                self.near["b"] = net.send(
                    self.view(3, 0, half, core), self.n.at[1, self.rows(0, half)], net.peer(axis, 3)
                )

    def step2(self):
        net, axis, core = self.net, self.axes[2], self.net.core
        half = self.blocks // 2
        self.onward[1].wait_recv()
        self.add(1, self.f.at[0], 0, half)
        self.near["c"] = net.send(self.view(1, 0, half, core), self.n.at[0, self.rows(0, half)], net.peer(axis, 1))
        self.onward[3].wait_recv()
        self.add(3, self.f.at[1], half, half)
        self.near["d"] = net.send(
            self.view(3, half, half, core), self.n.at[1, self.rows(half, half)], net.peer(axis, 3)
        )

    def total3(self, i):
        at = self.block(i)
        return self.g[self.tile(0, i)].astype(F32) + self.n[0, at].astype(F32) + self.n[1, at].astype(F32)

    def step3(self):
        net, width, axis = self.net, self.width, self.axes[1]
        for part in "abcd":
            self.near[part].wait_recv()

        def body(i, carry):
            self.total[self.block(i), 0 : self.width] = self.total3(i)
            return carry

        lax.fori_loop(0, 10, body, 0)
        for j in range(4):
            part = self.total[40 * j : 40 * j + 40, 0:width]
            self.t2[j] = jnp.concatenate([part, jnp.zeros((8, width), F32)], axis=0).astype(BF)
        self.p = [net.send(self.t2.at[net.slot(axis, o)], self.r2.at[o - 1], net.peer(axis, o)) for o in (1, 2, 3)]

    def step4(self):
        net, width, axis = self.net, self.width, self.axes[0]
        for copy in self.p:
            copy.wait_recv()
        own = self.t2[net.at[self.axes[1]]].astype(F32)
        for o in range(3):
            own = own + self.r2[o].astype(F32)
        self.total[0:48, 0:width] = own
        for j in range(4):
            part = self.total[10 * j : 10 * j + 10, 0:width]
            self.t1[j] = jnp.concatenate([part, jnp.zeros((6, width), F32)], axis=0).astype(BF)
        self.p = [net.send(self.t1.at[net.slot(axis, o)], self.r1.at[o - 1], net.peer(axis, o)) for o in (1, 2, 3)]

    def step5(self):
        net = self.net
        swap, got, out = self.rest
        for copy in self.p:
            copy.wait_recv()
        own = self.t1[net.at[self.axes[0]]].astype(F32)
        for o in range(3):
            own = own + self.r1[o].astype(F32)
        self.total[0:16, 0 : self.width] = own
        low_rows = self.total[0:8, 0 : self.width]
        high_rows = self.total[5:13, 0 : self.width]
        first = net.core == 0
        swap[...] = jnp.where(first, high_rows, low_rows)
        out[net.core] = jnp.where(first, low_rows, high_rows)
        self.last = net.send(swap, got, net.sib)

    def step6(self):
        swap, got, out = self.rest
        self.last.wait_recv()
        out[self.net.other] = got[...]


class TileSums(RowSums):
    blocks = 16

    def __init__(self, net, width, by_core, refs):
        self.by_core = by_core
        super().__init__(net, ("z", "x", "y"), width, refs)

    def view(self, steps, at, n, which):
        slot = self.net.slot("y", steps)
        if self.by_core:
            return self.g.at[pl.ds(at, n), slot, which]
        return self.g.at[which, pl.ds(at, n), slot]

    def rows(self, at, n):
        return pl.ds(at, n)

    def tile(self, steps, i):
        slot = self.net.slot("y", steps)
        return (i, slot, self.net.core) if self.by_core else (self.net.core, i, slot)

    def block(self, i):
        return i

    def step3(self):
        net = self.net
        for part in "abcd":
            self.near[part].wait_recv()

        def body(i, carry):
            self.t2[i] = self.total3(i).astype(BF)
            return carry

        lax.fori_loop(0, 16, body, 0)
        self.p = [
            net.send(self.t2.at[pl.ds(net.slot("x", o) * 4, 4)], self.r2.at[o - 1], net.peer("x", o))
            for o in (1, 2, 3)
        ]

    def step4(self):
        net = self.net
        for copy in self.p:
            copy.wait_recv()
        for j in range(4):
            value = self.t2[net.at["x"] * 4 + j].astype(F32)
            for o in range(3):
                value = value + self.r2[o, j].astype(F32)
            self.t1[j] = value.astype(BF)
        self.p = [net.send(self.t1.at[net.slot("z", o)], self.r1.at[o - 1], net.peer("z", o)) for o in (1, 2, 3)]

    def step5(self):
        net = self.net
        for copy in self.p:
            copy.wait_recv()
        own = self.t1[net.at["z"]].astype(F32)
        for o in range(3):
            own = own + self.r1[o].astype(F32)
        if self.by_core:
            self.rest[0][...] = own
            return
        swap, got, out = self.rest
        first = net.core == 0
        swap[...] = jnp.where(first, own[8:16], own[0:8])
        out[net.core] = jnp.where(first, own[0:8], own[8:16])
        self.last = net.send(swap, got, net.sib)

    def step6(self):
        if not self.by_core:
            super().step6()


def mm(left, right):
    return jnp.dot(left, right, preferred_element_type=F32)


def mm_t(left, right):
    return lax.dot_general(left, right, (((1,), (1,)), ((), ())), preferred_element_type=F32)


def t_mm(left, right):
    return lax.dot_general(left, right, (((0,), (0,)), ((), ())), preferred_element_type=F32)


def inv_of(values):
    return lax.rsqrt(jnp.mean(values * values, axis=-1, keepdims=True) + EPSILON)


def norm_back(upstream, unit_rows, inv_rms):
    return inv_rms * (upstream - unit_rows * jnp.mean(unit_rows * upstream, axis=-1, keepdims=True))


def spin(values, cosine, sine):
    a, b = values[:, :128], values[:, 128:]
    return jnp.concatenate([a * cosine - b * sine, b * cosine + a * sine], axis=1)


def spin_back(values, cosine, sine):
    a, b = values[:, :128], values[:, 128:]
    return jnp.concatenate([a * cosine + b * sine, b * cosine - a * sine], axis=1)


def count(shape, dim):
    return lax.broadcasted_iota(jnp.int32, shape, dim)


def hot(condition):
    return jnp.where(condition, 1.0, 0.0).astype(BF)


def split_dot(value, fixed):
    high = value.astype(BF)
    low = (value - high.astype(F32)).astype(BF)
    return mm_t(high, fixed) + mm_t(low, fixed)


class Refs:
    pass


def gather_setup(net, r):
    for ref in (r.own_x1, r.own_z1, r.own_x2, r.own_z2, r.own_o):
        ref[...] = jnp.zeros_like(ref)
    q = r.q[...].astype(F32)
    r.own_x1[0, 0:5] = q[:, 0:512]
    r.own_x1[1, 0:5, 0:256] = r.k[...].astype(F32)
    lane, row = count((8, 128), 1), count((8, 128), 0)
    fifth = (lane * 205) >> 10
    model = (lane < 20) & (lane - 5 * fifth == row)
    head = (lane >= 20) & (lane < 24) & (((lane - 20) & 1) == row)
    spread = jnp.where(model | head, jnp.broadcast_to(r.gains[...], (8, 128)), 0.0).astype(BF)
    source, target = count((128, 128), 0), count((128, 128), 1)
    place_of = jnp.where(source < 20, (source * 205) >> 10, 4 + ((source - 20) >> 1))
    tile = mm(spread, hot((place_of == target) & (source < 24)))
    r.own_x1[1, 0:5, 256:384] = tile[0:5]
    r.own_z1[0, 0:5] = q[:, 512:896]
    r.own_z1[1, 0:5, 0:128] = q[:, 896:1024]
    r.own_z1[1, 0:5, 128:384] = r.v[...].astype(F32)
    g, u = r.g[...].astype(F32), r.u[...].astype(F32)
    r.own_x2[0, 0:5] = g[:, 0:1024]
    r.own_x2[1, 0:5] = u[:, 0:1024]
    r.own_z2[0, 0:5] = g[:, 1024:2048]
    r.own_z2[1, 0:5] = u[:, 1024:2048]
    o = r.o[...].astype(F32)
    r.own_o[0, 0:8] = o[:, 0:384]
    r.own_o[1, 0:8, 0:256] = o[:, 384:640]

    def rows(name, axes, width):
        names = ("own_", "es_", "ed_", "s1_", "s2_", "b3_", "w_")
        return Rows(net, axes, width, [getattr(r, n + name) for n in names] + [r.tmp])

    x1 = rows("x1", ("y", "z", "x"), WX1)
    z1 = rows("z1", ("x", "y", "z"), WZ1)
    x2 = rows("x2", ("y", "z", "x"), WX2)
    z2 = rows("z2", ("x", "y", "z"), WZ2)
    for s in (x1, z1, x2, z2):
        s.step0()
    r.es_o[...] = r.own_o[net.other].astype(BF)
    return x1, z1, x2, z2, Tiles(net, r.w_o, False), Tiles(net, r.w_d, True)


def layer_kernel(names, *refs):
    r = Refs()
    for name, ref in zip(names, refs):
        setattr(r, name, ref)
    r.g_x2, r.g_z2, r.g_d, r.g_o = r.w_x2, r.w_z2, r.w_d, r.w_o
    for name in ("x1", "z1", "x2", "z2"):
        setattr(r, "t2_" + name, getattr(r, "s2_" + name))
        setattr(r, "t1_" + name, getattr(r, "s1_" + name))
    r.total_x2 = r.total_x1 = r.total_o = r.total_d = r.tmp
    r.g_middle = r.igrad
    net = Links(r.send_sems, r.recv_sems)
    net.greet()
    x1, z1, x2, z2, ow, dw = gather_setup(net, r)
    net.meet()
    x1.step0b()
    z1.step0b()
    swap_o = net.send(r.es_o, r.ed_o, net.sib)
    x2.step0b()
    z2.step0b()
    x1.step1()
    z1.step1()
    swap_o.wait_recv()
    mine, theirs = r.own_o[net.core][0:8], r.ed_o[...].astype(F32)[0:8]
    r.tmp[0:8, 0:WO] = jnp.where(net.core == 0, mine, theirs)
    r.tmp[8:16, 0:WO] = jnp.where(net.core == 0, theirs, mine)
    r.s1_o[...] = r.tmp[0:16, 0:WO].astype(BF)
    ow.first(r.s1_o)
    x2.step1()
    z2.step1()
    dw.first(r.d)

    k_dim, j_dim = count((D, D), 0), count((D, D), 1)
    tens = (j_dim * 52429) >> 19
    source = (tens & 3) * 160 + (tens >> 4) * 40 + ((tens >> 2) & 3) * 10 + (j_dim - 10 * tens)
    r.turn[...] = hot(k_dim == source)
    r.eye[...] = hot(k_dim == j_dim)
    spot = count((64, 64), 0)
    lens = jnp.broadcast_to(r.lens[...].astype(F32), (64, 64))
    column = jnp.sum(jnp.where(spot == count((64, 64), 1), lens, 0.0), axis=1, keepdims=True)
    ends = jnp.sum(jnp.where(spot <= count((64, 64), 1), column, 0.0), axis=0, keepdims=True)
    offset = net.me * T
    token = (count((T, 64), 0) + offset).astype(F32)
    start = jnp.max(jnp.where(ends <= token, ends, 0.0), axis=1, keepdims=True)
    position = token[:, 0:1] - start
    pair = count((1, 128), 1).astype(F32)
    angle = position * jnp.exp(pair * (-2.0 * math.log(ROPE_BASE) / HD))
    r.cosine[...] = jnp.cos(angle)
    r.sine[...] = jnp.sin(angle)
    ahead = count((T, SPAN), 1) - 2 * T
    distance = count((T, SPAN), 0) - ahead
    inside = (distance >= 0) & (distance < WINDOW) & ((ahead + offset).astype(F32) >= start)
    r.bias[...] = jnp.where(inside, 0.0, NEG_FILL)
    hidden = r.h[...].astype(F32)
    input_inv = inv_of(hidden)
    r.in_unit[...] = hidden * input_inv

    for s in (x1, z1, ow, x2, z2, dw):
        s.step2()
    for s in (x1, z1, ow, x2, z2, dw):
        s.step3()
    for s in (x1, z1, ow):
        s.step4()
    for s in (x1, z1, ow):
        s.step5()
    x1.step6()
    z1.step6()

    gain_tile = r.w_x1[1, :, 256:384]
    gain_rows = t_mm(gain_tile, r.eye[...])
    far, near = count((D, HD), 0), count((D, HD), 1)
    r.pick[...] = hot(far == 5 * (near >> 1) + (near & 1))
    head_rows = t_mm(gain_tile, r.pick[...])
    r.mults[0:4] = 1.0 + gain_rows[0:4]
    r.mults[4:6, 0:HD] = 1.0 + head_rows[4:6]
    normed = (r.in_unit[...] * r.mults[0:1]).astype(BF)
    r.normed[...] = normed
    turned = mm(normed, r.turn[...]).astype(BF)
    r.normed_t[...] = turned
    cosine, sine = r.cosine[...], r.sine[...]
    key_raw = mm(normed, r.w_x1[1, :, 0:256])
    key_inv = inv_of(key_raw)
    r.k_unit[...] = key_raw * key_inv
    r.keys[2 * T :] = spin(r.k_unit[...] * r.mults[5:6, 0:HD], cosine, sine).astype(BF)
    r.values[2 * T :] = mm(turned, r.w_z1[1, :, 128:384]).astype(BF)
    halo = []
    for steps, at in ((1, T), (2, 0)):
        for whole in (r.keys, r.values):
            halo.append(net.send(whole.at[pl.ds(2 * T, T)], whole.at[pl.ds(at, T)], net.along(steps)))
    for h in range(HEADS):
        if h < 2:
            raw = mm(normed, r.w_x1[0, :, 256 * h : 256 * h + 256])
        elif h == 2:
            raw = mm(turned, r.w_z1[0, :, 0:256])
        else:
            raw = jnp.concatenate(
                [mm(turned, r.w_z1[0, :, 256:384]), mm(turned, r.w_z1[1, :, 0:128])], axis=1
            )
        inv = inv_of(raw)
        r.q_inv[h] = inv
        r.q_unit[h] = raw * inv
        r.queries[h] = spin(raw * inv * r.mults[4:5, 0:HD], cosine, sine).astype(BF)
    for s in (x2, z2, dw):
        s.step4()
    for copy in halo:
        copy.wait_recv()

    def attend(h, carry):
        scores = mm_t(r.queries[h], r.keys[...]) * SCALE + r.bias[...]
        row_max = jnp.max(scores, axis=1, keepdims=True)
        weights = jnp.exp(scores - row_max)
        probs = weights / jnp.sum(weights, axis=1, keepdims=True)
        r.probs[h] = probs
        r.attended[h] = mm(probs.astype(BF), r.values[...]).astype(BF)
        return carry

    lax.fori_loop(0, 2, attend, 0)
    for s in (x2, z2, dw):
        s.step5()
    lax.fori_loop(2, 4, attend, 0)

    ow.step6()
    left = jnp.zeros((T, 384), F32)
    right = jnp.zeros((T, 256), F32)
    for h in range(HEADS):
        some = slice(4 * h, 4 * h + 4)
        left = left + mm(r.attended[h], r.w_o[0, some].reshape(256, WO))
        right = right + mm(r.attended[h], r.w_o[1, some].reshape(256, WO)[:, 0:256])
    mixer_out = jnp.concatenate([left, right], axis=1)
    mixer_inv = inv_of(mixer_out)
    r.mix_unit[...] = mixer_out * mixer_inv
    middle = r.h[...].astype(F32) + r.mix_unit[...] * r.mults[1:2]
    middle_inv = inv_of(middle)
    r.mid_unit[...] = middle * middle_inv
    r.middle[...] = middle
    r.mid[...] = (r.mid_unit[...] * r.mults[2:3]).astype(BF)
    r.mid_t[...] = mm(r.mid[...], r.turn[...]).astype(BF)
    for s in (x2, z2, dw):
        s.step6()

    r.acc[...] = jnp.zeros_like(r.acc)
    for w, rows_in, first in ((r.w_x2, r.mid, 0), (r.w_z2, r.mid_t, 2)):

        def forward(j, carry, w=w, rows_in=rows_in, first=first):
            cols = pl.ds(pl.multiple_of(j * 512, 512), 512)
            gate = mm(rows_in[...], w[0, :, cols])
            up = mm(rows_in[...], w[1, :, cols])
            square = gate * gate
            tanh = jnp.tanh(GELU_A * gate * (1.0 + GELU_B * square))
            active = 0.5 * gate * (1.0 + tanh)
            slope = 0.5 * (1.0 + tanh) + 0.5 * gate * (1.0 - tanh * tanh) * (
                GELU_A * (1.0 + 3.0 * GELU_B * square)
            )
            units = (active * up).astype(BF)
            part = first + j
            r.units[part] = units
            r.active[part] = active
            r.slope_up[part] = slope * up
            r.acc[...] += mm(units, r.w_d[pl.ds(part * 4, 4)].reshape(512, D))
            return carry

        lax.fori_loop(0, 2, forward, 0)
    ffn_out = r.acc[...]
    ffn_inv = inv_of(ffn_out)
    ffn_unit = ffn_out * ffn_inv
    r.mixed[...] = (r.middle[...] + ffn_unit * r.mults[3:4]).astype(BF)
    grad_out = r.og[...].astype(F32)
    r.gain_sums[...] = jnp.zeros_like(r.gain_sums)
    r.gain_sums[3:4] = jnp.sum(grad_out * ffn_unit, axis=0, keepdims=True)
    r.g_ffn[...] = norm_back(grad_out * r.mults[3:4], ffn_unit, ffn_inv).astype(BF)
    net.finish()
    for w, g, rows_in, first, total in (
        (r.w_x2, r.g_x2, r.mid, 0, r.acc),
        (r.w_z2, r.g_z2, r.mid_t, 2, r.acc_t),
    ):
        total[...] = jnp.zeros_like(total)

        def backward(j, carry, w=w, g=g, rows_in=rows_in, first=first, total=total):
            cols = pl.ds(pl.multiple_of(j * 512, 512), 512)
            part = first + j
            some = pl.ds(part * 4, 4)
            g_ffn = r.g_ffn[...]
            grad_hidden = mm_t(g_ffn, r.w_d[some].reshape(512, D))
            r.g_d[some] = t_mm(r.units[part], g_ffn).astype(BF).reshape(4, 4, 2, 16, D)
            grad_gate = (grad_hidden * r.slope_up[part]).astype(BF)
            grad_up = (grad_hidden * r.active[part]).astype(BF)
            total[...] += mm_t(grad_gate, w[0, :, cols]) + mm_t(grad_up, w[1, :, cols])
            g[0, :, cols] = t_mm(rows_in[...], grad_gate).astype(BF)
            g[1, :, cols] = t_mm(rows_in[...], grad_up).astype(BF)
            return carry

        lax.fori_loop(0, 2, backward, 0)

    def sums(kind, name, *args):
        tags = ("g_", "b_", "f_", "n_", "t2_", "r2_", "t1_", "r1_", "total_", "swap_", "got_", "out_")
        if name == "d":
            tags = tags[:9] + tags[11:]
        return kind(net, *args, [getattr(r, tag + name) for tag in tags])

    sx1 = sums(RowSums, "x1", ("y", "z", "x"), WX1)
    sz1 = sums(RowSums, "z1", ("x", "y", "z"), WZ1)
    sx2 = sums(RowSums, "x2", ("y", "z", "x"), WX2)
    sz2 = sums(RowSums, "z2", ("x", "y", "z"), WZ2)
    so = sums(TileSums, "o", WO, False)
    sd = sums(TileSums, "d", WD, True)
    for s in (sx2, sz2, sd):
        s.step0()

    grad_in = r.acc[...] + split_dot(r.acc_t[...], r.turn[...])
    mid_unit = r.mid_unit[...]
    r.gain_sums[2:3] = jnp.sum(grad_in * mid_unit, axis=0, keepdims=True)
    grad_middle = r.og[...].astype(F32) + norm_back(grad_in * r.mults[2:3], mid_unit, inv_of(r.middle[...]))
    r.g_middle[...] = grad_middle
    mix_unit = r.mix_unit[...]
    r.gain_sums[1:2] = jnp.sum(grad_middle * mix_unit, axis=0, keepdims=True)
    grad_mixer = norm_back(grad_middle * r.mults[1:2], mix_unit, mixer_inv).astype(BF)
    for h in range(HEADS):
        some = slice(4 * h, 4 * h + 4)
        r.g_att[h] = (
            mm_t(grad_mixer[:, 0:384], r.w_o[0, some].reshape(256, WO))
            + mm_t(grad_mixer[:, 384:640], r.w_o[1, some].reshape(256, WO)[:, 0:256])
        ).astype(BF)
        grad = t_mm(r.attended[h], grad_mixer).astype(BF)
        r.g_o[0, some] = grad[:, 0:384].reshape(4, 4, 16, 384)
        r.g_o[1, some, :, :, 0:256] = grad[:, 384:640].reshape(4, 4, 16, 256)
    so.step0()
    for s in (sx2, sz2, sd, so):
        s.step1()

    r.d_keys[...] = jnp.zeros_like(r.d_keys)
    r.d_values[...] = jnp.zeros_like(r.d_values)
    r.q_gain[...] = jnp.zeros_like(r.q_gain)

    def attend_back(h, carry):
        probs = r.probs[h]
        g_att = r.g_att[h]
        grad_probs = mm_t(g_att, r.values[...])
        delta = jnp.sum(probs * grad_probs, axis=1, keepdims=True)
        grad_scores = (probs * (grad_probs - delta)).astype(BF)
        grad_q = mm(grad_scores, r.keys[...]) * SCALE
        r.d_keys[...] += t_mm(grad_scores, r.queries[h])
        r.d_values[...] += t_mm(probs.astype(BF), g_att)
        back = spin_back(grad_q, r.cosine[...], r.sine[...])
        unit = r.q_unit[h]
        r.q_gain[...] += jnp.sum(back * unit, axis=0, keepdims=True)
        r.g_q[h] = norm_back(back * r.mults[4:5, 0:HD], unit, r.q_inv[h]).astype(BF)
        return carry

    lax.fori_loop(0, 2, attend_back, 0)
    for s in (sx2, sz2, sd, so):
        s.step2()
    lax.fori_loop(2, 4, attend_back, 0)
    back_halo = []
    for i, (whole, low) in enumerate(((r.d_keys, r.dk_low), (r.d_values, r.dv_low))):
        scale = SCALE if i == 0 else 1.0
        low[...] = (whole[0 : 2 * T] * scale).astype(BF)
        for steps, at in ((-1, T), (-2, 0)):
            back_halo.append(
                net.send(low.at[pl.ds(at, T)], r.halo_back.at[i, 0 if at else 1], net.along(steps))
            )

    normed, turned = r.normed[...], r.normed_t[...]
    for h in range(HEADS):
        if h < 2:
            r.g_x1[0, :, 256 * h : 256 * h + 256] = t_mm(normed, r.g_q[h]).astype(BF)
        elif h == 2:
            r.g_z1[0, :, 0:256] = t_mm(turned, r.g_q[h]).astype(BF)
        else:
            last = t_mm(turned, r.g_q[h]).astype(BF)
            r.g_z1[0, :, 256:384] = last[:, 0:128]
            r.g_z1[1, :, 0:128] = last[:, 128:256]
    for s in (sx2, sz2, sd, so):
        s.step3()
    for copy in back_halo:
        copy.wait_recv()
    own_k = r.d_keys[2 * T :] * SCALE
    own_v = r.d_values[2 * T :]
    for i in range(2):
        own_k = own_k + r.halo_back[0, i].astype(F32)
        own_v = own_v + r.halo_back[1, i].astype(F32)
    key_back = spin_back(own_k, r.cosine[...], r.sine[...])
    k_unit = r.k_unit[...]
    key_gain = jnp.sum(key_back * k_unit, axis=0, keepdims=True)
    grad_k = norm_back(key_back * r.mults[5:6, 0:HD], k_unit, key_inv).astype(BF)
    grad_v = own_v.astype(BF)
    r.g_z1[1, :, 128:384] = t_mm(turned, grad_v).astype(BF)
    sz1.step0()
    r.g_x1[1, :, 0:256] = t_mm(normed, grad_k).astype(BF)
    r.g_x1[1, :, 384:512] = jnp.zeros((D, 128), BF)
    grad_natural = (
        mm_t(r.g_q[0], r.w_x1[0, :, 0:256])
        + mm_t(r.g_q[1], r.w_x1[0, :, 256:512])
        + mm_t(grad_k, r.w_x1[1, :, 0:256])
    )
    g_last = r.g_q[3]
    grad_turned = (
        mm_t(r.g_q[2], r.w_z1[0, :, 0:256])
        + mm_t(g_last[:, 0:128], r.w_z1[0, :, 256:384])
        + mm_t(g_last[:, 128:256], r.w_z1[1, :, 0:128])
        + mm_t(grad_v, r.w_z1[1, :, 128:384])
    )
    grad_normed = grad_natural + split_dot(grad_turned, r.turn[...])
    in_unit = r.in_unit[...]
    r.gain_sums[0:1] = jnp.sum(grad_normed * in_unit, axis=0, keepdims=True)
    both = jnp.concatenate([r.q_gain[...], key_gain, jnp.zeros((6, HD), F32)], axis=0).astype(BF)
    r.gain_sums[4:6] = mm_t(both, r.pick[...])[0:2]
    r.g_x1[1, :, 256:384] = mm_t(r.eye[...], r.gain_sums[...].astype(BF)).astype(BF)
    sx1.step0()
    r.igrad[...] = r.g_middle[...] + norm_back(grad_normed * r.mults[0:1], in_unit, input_inv)
    for s in (sx2, sz2, sd, so):
        s.step4()
    sz1.step1()
    sx1.step1()
    for s in (sx2, sz2, sd, so):
        s.step5()
    for step in ("step2", "step3", "step4", "step5", "step6"):
        for s in (sz1, sx1):
            getattr(s, step)()
    for s in (sx2, sz2, sd, so):
        s.step6()
    net.finish()


def layer(h, q, k, v, o, g, u, d, gains, lens, og):
    vmem = pltpu.VMEM
    ins = ("h", "q", "k", "v", "o", "g", "u", "d", "gains", "lens", "og")
    outs = {
        "mixed": ((T, D), BF),
        "igrad": ((T, D), F32),
        "out_x1": ((2, 8, WX1), F32),
        "out_z1": ((2, 8, WZ1), F32),
        "out_o": ((2, 8, WO), F32),
        "out_x2": ((2, 8, WX2), F32),
        "out_z2": ((2, 8, WZ2), F32),
        "out_d": ((16, WD), F32),
    }
    scratch = {}
    for name, w in (("x1", WX1), ("z1", WZ1), ("x2", WX2), ("z2", WZ2)):
        scratch |= {
            "own_" + name: ((2, 16, w), F32),
            "es_" + name: ((16, w), BF),
            "ed_" + name: ((16, w), BF),
            "s1_" + name: ((4, 16, w), BF),
            "s2_" + name: ((4, 48, w), BF),
            "b3_" + name: ((160, w), BF),
            "w_" + name: ((2, D, w), BF),
            "b_" + name: ((4, 160, w), BF),
            "f_" + name: ((2, 80, w), BF),
            "n_" + name: ((2, 160, w), BF),
            "r2_" + name: ((3, 48, w), BF),
            "r1_" + name: ((3, 16, w), BF),
            "swap_" + name: ((8, w), F32),
            "got_" + name: ((8, w), F32),
        }
    for name, w in (("o", WO), ("d", WD)):
        scratch |= {
            "b_" + name: ((4, 16, 16, w), BF),
            "f_" + name: ((2, 8, 16, w), BF),
            "n_" + name: ((2, 16, 16, w), BF),
            "t2_" + name: ((16, 16, w), BF),
            "r2_" + name: ((3, 4, 16, w), BF),
            "t1_" + name: ((4, 16, w), BF),
            "r1_" + name: ((3, 16, w), BF),
        }
    scratch |= {
        "g_x1": ((2, D, WX1), BF),
        "g_z1": ((2, D, WZ1), BF),
        "total_z2": ((160, WZ2), F32),
        "total_z1": ((160, WZ1), F32),
        "own_o": ((2, 16, WO), F32),
        "es_o": ((16, WO), BF),
        "ed_o": ((16, WO), BF),
        "s1_o": ((16, WO), BF),
        "swap_o": ((8, WO), F32),
        "got_o": ((8, WO), F32),
        "w_o": ((2, 16, 4, 16, WO), BF),
        "w_d": ((16, 4, 2, 16, WD), BF),
        "tmp": ((160, 1024), F32),
        "turn": ((D, D), BF),
        "eye": ((D, D), BF),
        "pick": ((D, HD), BF),
        "cosine": ((T, 128), F32),
        "sine": ((T, 128), F32),
        "bias": ((T, SPAN), F32),
        "mults": ((8, D), F32),
        "gain_sums": ((128, D), F32),
        "in_unit": ((T, D), F32),
        "normed": ((T, D), BF),
        "normed_t": ((T, D), BF),
        "k_unit": ((T, HD), F32),
        "keys": ((SPAN, HD), BF),
        "values": ((SPAN, HD), BF),
        "queries": ((HEADS, T, HD), BF),
        "q_unit": ((HEADS, T, HD), F32),
        "q_inv": ((HEADS, T, 1), F32),
        "probs": ((HEADS, T, SPAN), F32),
        "attended": ((HEADS, T, HD), BF),
        "mix_unit": ((T, D), F32),
        "mid_unit": ((T, D), F32),
        "middle": ((T, D), F32),
        "mid": ((T, D), BF),
        "mid_t": ((T, D), BF),
        "units": ((4, T, 512), BF),
        "active": ((4, T, 512), F32),
        "slope_up": ((4, T, 512), F32),
        "acc": ((T, D), F32),
        "acc_t": ((T, D), F32),
        "g_ffn": ((T, D), BF),
        "g_att": ((HEADS, T, HD), BF),
        "g_q": ((HEADS, T, HD), BF),
        "d_keys": ((SPAN, HD), F32),
        "d_values": ((SPAN, HD), F32),
        "dk_low": ((2 * T, HD), BF),
        "dv_low": ((2 * T, HD), BF),
        "halo_back": ((2, 2, T, HD), BF),
        "q_gain": ((1, HD), F32),
    }
    inside = pl.BlockSpec(memory_space=vmem)
    names = (*ins, *outs, *scratch, "send_sems", "recv_sems")
    return pl.pallas_call(
        lambda *refs: layer_kernel(names, *refs),
        out_shape=[jax.ShapeDtypeStruct(*s) for s in outs.values()],
        in_specs=[inside] * len(ins),
        out_specs=[inside] * len(outs),
        scratch_shapes=[vmem(*s) for s in scratch.values()] + [pltpu.SemaphoreType.DMA((SEMS,))] * 2,
        compiler_params=pltpu.CompilerParams(
            collective_id=0, has_side_effects=True, vmem_limit_bytes=VMEM_CAP
        ),
        name="decoder_layer",
    )(h, q, k, v, o, g, u, d, gains, lens, og)


def per_device(
    hidden_in,
    query_weight,
    key_weight,
    value_weight,
    output_weight,
    gate_weight,
    up_weight,
    down_weight,
    input_gain,
    query_gain,
    key_gain,
    mixer_gain,
    middle_gain,
    output_gain,
    seq_lengths,
    out_grad,
):
    gains = jnp.concatenate([input_gain, mixer_gain, middle_gain, output_gain, query_gain, key_gain])
    gains = jnp.pad(gains.astype(F32), (0, 104)).reshape(1, 128)
    mixed, igrad, x1, z1, o, x2, z2, down_grad = layer(
        hidden_in,
        query_weight,
        key_weight,
        value_weight,
        output_weight,
        gate_weight,
        up_weight,
        down_weight,
        gains,
        seq_lengths.reshape(1, 64),
        out_grad,
    )
    sums = x1[1, :5, 256:384]
    return (
        mixed,
        igrad,
        jnp.concatenate([x1[0, :5], z1[0, :5], z1[1, :5, 0:128]], axis=1),
        x1[1, :5, 0:256],
        z1[1, :5, 128:384],
        jnp.concatenate([o[0], o[1, :, 0:256]], axis=1),
        jnp.concatenate([x2[0, :5], z2[0, :5]], axis=1),
        jnp.concatenate([x2[1, :5], z2[1, :5]], axis=1),
        down_grad,
        sums[:, 0],
        sums[:2, 4],
        sums[:2, 5],
        sums[:, 1],
        sums[:, 2],
        sums[:, 3],
    )


def solution(mesh):
    return jax.shard_map(
        per_device,
        mesh=mesh,
        in_specs=(
            P("dp", None),
            P("dp", None),
            P("dp", None),
            P("dp", None),
            P("dp", None),
            P("dp", None),
            P("dp", None),
            P("dp", None),
            P("dp"),
            P("dp"),
            P("dp"),
            P("dp"),
            P("dp"),
            P("dp"),
            P(),
            P("dp", None),
        ),
        out_specs=(
            P("dp", None),
            P("dp", None),
            P("dp", None),
            P("dp", None),
            P("dp", None),
            P("dp", None),
            P("dp", None),
            P("dp", None),
            P("dp", None),
            P("dp"),
            P("dp"),
            P("dp"),
            P("dp"),
            P("dp"),
            P("dp"),
        ),
        check_vma=False,
    )
```

time: 646 us -> 143 us (0.22)
  waiting for transfers between devices: 296 us -> 0 us
  blocking collectives: 139 us -> 0 us
  Pallas kernels: 0 us -> 131 us
  local copies, waits for them, and re-layouts: 104 us -> 7.96 us
  matrix products: 49.7 us -> 0 us
  other arithmetic: 22.3 us -> 3.02 us
  starting transfers between devices: 17.7 us -> 0 us
  between operations: 14.7 us -> 0.72 us
    unnamed x6 -> x0, waiting for transfers between devices: 156 us -> none
    all_gather x4 -> x0, waiting for transfers between devices: 140 us -> none  [the longest x2 66.3 us: side_by_side(): whole, at, done = (lax.all_gather(both, axis, axis=dim, tiled=True), 0, [])]
    unnamed x2 -> x0, blocking collectives: 139 us -> none
    pallas_call x0 -> x1, Pallas kernels: none -> 131 us  [layer(): pl.pallas_call(lambda *refs: layer_kernel(names, *refs), out_shape=[jax.S...]
    dot_general x27 -> x0, matrix products: 49.7 us -> none  [the longest x7 16.5 us: mat_t_mul(): lax.dot_general(left_side, right_side, (((0,), (0,)), ((), ())), preferre...]
    unnamed x107 -> x25, local copies, waits for them, and re-layouts: 34.1 us -> 3.01 us
    another operation x4 -> x0, local copies, waits for them, and re-layouts: 19.1 us -> none  [the longest x3 18.3 us: one_scatter(): lines = jnp.concatenate([b.reshape(size, -1) for b in tiles], axis=1)]
    reshape x8 -> x0, local copies, waits for them, and re-layouts: 18.7 us -> none  [the longest x1 14 us: one_scatter(): jnp.pad(lines, ((0, 0), (0, rows * 128 - lines.shape[1]))).reshape(-1, 128)]
  transfers between devices with their start and end apart: 13 -> 0, of which waited for: 4 -> 0; matrix products, arithmetic and copies ran while one was open for 20% -> 0% of each run, Pallas kernels for 0% -> 0%
where the time goes in v2:
time: 143 us
  Pallas kernels  131 us (92%)
  local copies, waits for them, and re-layouts  7.96 us (6%)
  other arithmetic  3.02 us (2%)
    pallas_call x1, Pallas kernels, layer(): pl.pallas_call(lambda *refs: layer_kernel(names, *refs), out_shape=[jax.S...  131 us
    unnamed x25, local copies, waits for them, and re-layouts  3.01 us

profile of v2, /device:TPU:1, one launch (start us, length us, event | category | flops | bytes accessed | tf_op | source)
XLA Modules:
  0.0 142.5 jit_solution(12064523960126830902)
XLA Ops:
  0.6 0.0 copy-start.10
  0.7 0.0 copy-start.9
  0.7 0.6 copy-done.10
  1.3 0.0 copy-done.9
  1.3 0.0 copy-done.8
  1.3 2.1 %concatenate.15 = bf16[24]{0:T(256)(128)(2,1)S(1)} concatenate(bf16[5]{0:T(256)(128)(2,1)S(1)} %copy-done.8, bf16[5]{0:T(256)(128)(2,1)S(1)} %copy-done.9, bf16[5]{0:T(256)(128)(2,1)S(1)} %copy-done.10, bf16[5]{0:T(256)(128)(2,1)} %param.29, bf16[2]{0:T(256)(128)(2,1)} %param.25, bf16[2]{0:T(256)(128)(2,1)} %param.26), dimensions={0} | concatenate | bytes 96 | tf_op jit(solution)/shard_map/concatenate | solution.py:941
  3.4 0.5 bitcast_convert_fusion.refs_8_
  3.9 130.8 %decoder_layer.1 = (bf16[256,640]{1,0:T(8,128)(2,1)}, f32[256,640]{1,0:T(8,128)}, f32[2,8,512]{2,1,0:T(8,128)}, f32[2,8,384]{2,1,0:T(8,128)}, f32[2,8,384]{2,1,0...) custom-call(bf16[256,640]{1,0:T(8,128)(2,1)} %refs_0_.1, bf16[5,1024]{1,0:T(8,128)(2,1)} %refs_1_.1, ...), custom_call_target="tpu_custom_call" | custom-call | tf_op jit(solution)/shard_map/decoder_layer/pallas_call | solution.py:910
  134.8 0.8 slice_bitcast_fusion.7
  135.6 0.0 copy-done.7
  135.6 0.6 pad_maximum_fusion.3
  136.2 0.1 copy-done.5
  136.3 0.0 copy-done.6
  136.3 0.7 slice_reduce_fusion.4
  137.1 0.7 slice_reduce_fusion
  137.8 0.6 slice_bitcast_fusion.8
  138.4 0.6 pad_maximum_fusion.2
  139.1 0.0 copy-done.2
  139.1 0.6 pad_maximum_fusion.1
  139.7 0.6 pad_maximum_fusion
  140.4 0.0 copy-done.1
  140.4 0.7 copy.34
  141.1 0.8 copy.35
  141.9 0.6 copy.36
  (17 shorter events, 0.0 us)
Async XLA Ops:
  0.6 0.7 copy-start.10
  0.7 0.7 copy-start.9
  0.7 0.7 copy-start.8
  134.8 0.8 copy-start.7
  135.6 0.8 copy-start.5
  135.6 0.8 copy-start.6
  137.8 1.3 copy-start.2
  137.8 1.3 copy-start.3
  137.8 2.5 %copy-start.1 = (bf16[256,640]{1,0:T(8,128)(2,1)S(1)}, bf16[256,640]{1,0:T(8,128)(2,1)}, u32[]{:S(2)}) copy-start(bf16[256,640]{1,0:T(8,128)(2,1)} %get-tuple-element.62) | copy-start | bytes 983044
  137.8 3.3 %copy-start = (f32[256,640]{1,0:T(8,128)S(1)}, f32[256,640]{1,0:T(8,128)}, u32[]{:S(2)}) copy-start(f32[256,640]{1,0:T(8,128)} %get-tuple-element.63) | copy-start | bytes 1966084
  141.1 0.8 copy-start.4

commit v3 on v2

--- a/solution.py
+++ b/solution.py
@@ -24,6 +24,7 @@
 GELU_B = 0.044715
 WX1, WZ1, WX2, WZ2, WD, WO = 512, 384, 1024, 1024, 640, 384
 SEMS = 232
+GAINS = ("n_in", "n_mix", "n_mid", "n_out", "n_q", "n_k")
 VMEM_CAP = 62 << 20
 
 
@@ -231,38 +232,36 @@
     def block(self, i):
         return pl.ds(pl.multiple_of(i * 16, 16), 16)
 
-    def step0(self):
-        net = self.net
-        for steps in (2, 1, 3, 0):
-            src = self.view(steps, 0, self.blocks, net.other)
-            self.swaps[steps] = net.send(src, self.b.at[steps], net.sib)
+    def give(self, steps):
+        src = self.view(steps, 0, self.blocks, self.net.other)
+        self.swaps[steps] = self.net.send(src, self.b.at[steps], self.net.sib)
 
     def add(self, steps, held, at, count):
         def body(i, carry):
             where = self.tile(steps, i + at)
-            total = self.g[where].astype(F32) + held[self.block(i)].astype(F32)
-            self.g[where] = total.astype(BF)
+            self.g[where] = self.g[where] + held[self.block(i)]
             return carry
 
         lax.fori_loop(0, count, body, 0)
 
-    def step1(self):
+    def take(self, steps):
         net, axis, n, core = self.net, self.axes[2], self.blocks, self.net.core
         half = n // 2
-        for steps in (2, 1, 3, 0):
-            self.swaps[steps].wait_recv()
-            self.add(steps, self.b.at[steps], 0, n)
-            if steps == 2:
-                self.onward[1] = net.send(self.view(2, 0, half, core), self.f.at[0], net.peer(axis, 1))
-                self.onward[3] = net.send(self.view(2, half, half, core), self.f.at[1], net.peer(axis, 3))
-            elif steps == 1:
-                self.near["a"] = net.send(
-                    self.view(1, half, half, core), self.n.at[0, self.rows(half, half)], net.peer(axis, 1)
-                )
-            elif steps == 3:
-                self.near["b"] = net.send(
-                    self.view(3, 0, half, core), self.n.at[1, self.rows(0, half)], net.peer(axis, 3)
-                )
+        self.swaps[steps].wait_recv()
+        if steps == 0:
+            return
+        self.add(steps, self.b.at[steps], 0, n)
+        if steps == 2:
+            self.onward[1] = net.send(self.view(2, 0, half, core), self.f.at[0], net.peer(axis, 1))
+            self.onward[3] = net.send(self.view(2, half, half, core), self.f.at[1], net.peer(axis, 3))
+        elif steps == 1:
+            self.near["a"] = net.send(
+                self.view(1, half, half, core), self.n.at[0, self.rows(half, half)], net.peer(axis, 1)
+            )
+        else:
+            self.near["b"] = net.send(
+                self.view(3, 0, half, core), self.n.at[1, self.rows(0, half)], net.peer(axis, 3)
+            )
 
     def step2(self):
         net, axis, core = self.net, self.axes[2], self.net.core
@@ -278,7 +277,8 @@
 
     def total3(self, i):
         at = self.block(i)
-        return self.g[self.tile(0, i)].astype(F32) + self.n[0, at].astype(F32) + self.n[1, at].astype(F32)
+        own = self.g[self.tile(0, i)].astype(F32) + self.b[0, at].astype(F32)
+        return own + self.n[0, at].astype(F32) + self.n[1, at].astype(F32)
 
     def step3(self):
         net, width, axis = self.net, self.width, self.axes[1]
@@ -454,14 +454,10 @@
     q = r.q[...].astype(F32)
     r.own_x1[0, 0:5] = q[:, 0:512]
     r.own_x1[1, 0:5, 0:256] = r.k[...].astype(F32)
-    lane, row = count((8, 128), 1), count((8, 128), 0)
-    fifth = (lane * 205) >> 10
-    model = (lane < 20) & (lane - 5 * fifth == row)
-    head = (lane >= 20) & (lane < 24) & (((lane - 20) & 1) == row)
-    spread = jnp.where(model | head, jnp.broadcast_to(r.gains[...], (8, 128)), 0.0).astype(BF)
-    source, target = count((128, 128), 0), count((128, 128), 1)
-    place_of = jnp.where(source < 20, (source * 205) >> 10, 4 + ((source - 20) >> 1))
-    tile = mm(spread, hot((place_of == target) & (source < 24)))
+    r.gain_rows[...] = jnp.zeros_like(r.gain_rows)
+    for i, gain in enumerate((r.n_in, r.n_mix, r.n_mid, r.n_out, r.n_q, r.n_k)):
+        r.gain_rows[i : i + 1, 0 : gain.shape[1]] = gain[...].astype(F32)
+    tile = t_mm(r.gain_rows[...].astype(BF), hot(count((16, 128), 0) == count((16, 128), 1)))
     r.own_x1[1, 0:5, 256:384] = tile[0:5]
     r.own_z1[0, 0:5] = q[:, 512:896]
     r.own_z1[1, 0:5, 0:128] = q[:, 896:1024]
@@ -545,13 +541,18 @@
     input_inv = inv_of(hidden)
     r.in_unit[...] = hidden * input_inv
 
-    for s in (x1, z1, ow, x2, z2, dw):
+    early, late = (x1, z1, ow), (x2, z2, dw)
+    for s in early:
         s.step2()
-    for s in (x1, z1, ow, x2, z2, dw):
+    for s in late:
+        s.step2()
+    for s in early:
         s.step3()
-    for s in (x1, z1, ow):
+    for s in early:
         s.step4()
-    for s in (x1, z1, ow):
+    for s in late:
+        s.step3()
+    for s in early:
         s.step5()
     x1.step6()
     z1.step6()
@@ -590,24 +591,25 @@
         r.q_inv[h] = inv
         r.q_unit[h] = raw * inv
         r.queries[h] = spin(raw * inv * r.mults[4:5, 0:HD], cosine, sine).astype(BF)
-    for s in (x2, z2, dw):
+    for s in late:
         s.step4()
     for copy in halo:
         copy.wait_recv()
 
-    def attend(h, carry):
+    def attend(h):
         scores = mm_t(r.queries[h], r.keys[...]) * SCALE + r.bias[...]
         row_max = jnp.max(scores, axis=1, keepdims=True)
         weights = jnp.exp(scores - row_max)
         probs = weights / jnp.sum(weights, axis=1, keepdims=True)
         r.probs[h] = probs
         r.attended[h] = mm(probs.astype(BF), r.values[...]).astype(BF)
-        return carry
-
-    lax.fori_loop(0, 2, attend, 0)
-    for s in (x2, z2, dw):
+
+    attend(0)
+    attend(1)
+    for s in late:
         s.step5()
-    lax.fori_loop(2, 4, attend, 0)
+    attend(2)
+    attend(3)
 
     ow.step6()
     left = jnp.zeros((T, 384), F32)
@@ -625,7 +627,7 @@
     r.middle[...] = middle
     r.mid[...] = (r.mid_unit[...] * r.mults[2:3]).astype(BF)
     r.mid_t[...] = mm(r.mid[...], r.turn[...]).astype(BF)
-    for s in (x2, z2, dw):
+    for s in late:
         s.step6()
 
     r.acc[...] = jnp.zeros_like(r.acc)
@@ -659,6 +661,20 @@
     r.gain_sums[3:4] = jnp.sum(grad_out * ffn_unit, axis=0, keepdims=True)
     r.g_ffn[...] = norm_back(grad_out * r.mults[3:4], ffn_unit, ffn_inv).astype(BF)
     net.finish()
+
+    def sums(kind, name, *args):
+        tags = ("g_", "b_", "f_", "n_", "t2_", "r2_", "t1_", "r1_", "total_", "swap_", "got_", "out_")
+        if name == "d":
+            tags = tags[:9] + tags[11:]
+        return kind(net, *args, [getattr(r, tag + name) for tag in tags])
+
+    sx1 = sums(RowSums, "x1", ("y", "z", "x"), WX1)
+    sz1 = sums(RowSums, "z1", ("x", "y", "z"), WZ1)
+    sx2 = sums(RowSums, "x2", ("y", "z", "x"), WX2)
+    sz2 = sums(RowSums, "z2", ("x", "y", "z"), WZ2)
+    so = sums(TileSums, "o", WO, False)
+    sd = sums(TileSums, "d", WD, True)
+    wide = (sx2, sz2, sd)
     for w, g, rows_in, first, total in (
         (r.w_x2, r.g_x2, r.mid, 0, r.acc),
         (r.w_z2, r.g_z2, r.mid_t, 2, r.acc_t),
@@ -680,21 +696,12 @@
             return carry
 
         lax.fori_loop(0, 2, backward, 0)
-
-    def sums(kind, name, *args):
-        tags = ("g_", "b_", "f_", "n_", "t2_", "r2_", "t1_", "r1_", "total_", "swap_", "got_", "out_")
-        if name == "d":
-            tags = tags[:9] + tags[11:]
-        return kind(net, *args, [getattr(r, tag + name) for tag in tags])
-
-    sx1 = sums(RowSums, "x1", ("y", "z", "x"), WX1)
-    sz1 = sums(RowSums, "z1", ("x", "y", "z"), WZ1)
-    sx2 = sums(RowSums, "x2", ("y", "z", "x"), WX2)
-    sz2 = sums(RowSums, "z2", ("x", "y", "z"), WZ2)
-    so = sums(TileSums, "o", WO, False)
-    sd = sums(TileSums, "d", WD, True)
-    for s in (sx2, sz2, sd):
-        s.step0()
+        if first == 0:
+            for steps in (2, 1, 3, 0):
+                sx2.give(steps)
+    for steps in (2, 1, 3, 0):
+        sz2.give(steps)
+        sd.give(steps)
 
     grad_in = r.acc[...] + split_dot(r.acc_t[...], r.turn[...])
     mid_unit = r.mid_unit[...]
@@ -704,6 +711,8 @@
     mix_unit = r.mix_unit[...]
     r.gain_sums[1:2] = jnp.sum(grad_middle * mix_unit, axis=0, keepdims=True)
     grad_mixer = norm_back(grad_middle * r.mults[1:2], mix_unit, mixer_inv).astype(BF)
+    for s in wide:
+        s.take(2)
     for h in range(HEADS):
         some = slice(4 * h, 4 * h + 4)
         r.g_att[h] = (
@@ -713,15 +722,16 @@
         grad = t_mm(r.attended[h], grad_mixer).astype(BF)
         r.g_o[0, some] = grad[:, 0:384].reshape(4, 4, 16, 384)
         r.g_o[1, some, :, :, 0:256] = grad[:, 384:640].reshape(4, 4, 16, 256)
-    so.step0()
-    for s in (sx2, sz2, sd, so):
-        s.step1()
+    for steps in (2, 1, 3, 0):
+        so.give(steps)
+    for s in wide:
+        s.take(1)
 
     r.d_keys[...] = jnp.zeros_like(r.d_keys)
     r.d_values[...] = jnp.zeros_like(r.d_values)
     r.q_gain[...] = jnp.zeros_like(r.q_gain)
 
-    def attend_back(h, carry):
+    def attend_back(h):
         probs = r.probs[h]
         g_att = r.g_att[h]
         grad_probs = mm_t(g_att, r.values[...])
@@ -734,12 +744,17 @@
         unit = r.q_unit[h]
         r.q_gain[...] += jnp.sum(back * unit, axis=0, keepdims=True)
         r.g_q[h] = norm_back(back * r.mults[4:5, 0:HD], unit, r.q_inv[h]).astype(BF)
-        return carry
-
-    lax.fori_loop(0, 2, attend_back, 0)
-    for s in (sx2, sz2, sd, so):
-        s.step2()
-    lax.fori_loop(2, 4, attend_back, 0)
+
+    attend_back(0)
+    for s in wide:
+        s.take(3)
+    so.take(2)
+    attend_back(1)
+    so.take(1)
+    so.take(3)
+    attend_back(2)
+    sx2.step2()
+    attend_back(3)
     back_halo = []
     for i, (whole, low) in enumerate(((r.d_keys, r.dk_low), (r.d_values, r.dv_low))):
         scale = SCALE if i == 0 else 1.0
@@ -748,6 +763,9 @@
             back_halo.append(
                 net.send(low.at[pl.ds(at, T)], r.halo_back.at[i, 0 if at else 1], net.along(steps))
             )
+    sz2.step2()
+    sd.step2()
+    so.step2()
 
     normed, turned = r.normed[...], r.normed_t[...]
     for h in range(HEADS):
@@ -759,8 +777,6 @@
             last = t_mm(turned, r.g_q[h]).astype(BF)
             r.g_z1[0, :, 256:384] = last[:, 0:128]
             r.g_z1[1, :, 0:128] = last[:, 128:256]
-    for s in (sx2, sz2, sd, so):
-        s.step3()
     for copy in back_halo:
         copy.wait_recv()
     own_k = r.d_keys[2 * T :] * SCALE
@@ -774,7 +790,8 @@
     grad_k = norm_back(key_back * r.mults[5:6, 0:HD], k_unit, key_inv).astype(BF)
     grad_v = own_v.astype(BF)
     r.g_z1[1, :, 128:384] = t_mm(turned, grad_v).astype(BF)
-    sz1.step0()
+    for steps in (2, 1, 3, 0):
+        sz1.give(steps)
     r.g_x1[1, :, 0:256] = t_mm(normed, grad_k).astype(BF)
     r.g_x1[1, :, 384:512] = jnp.zeros((D, 128), BF)
     grad_natural = (
@@ -795,25 +812,40 @@
     both = jnp.concatenate([r.q_gain[...], key_gain, jnp.zeros((6, HD), F32)], axis=0).astype(BF)
     r.gain_sums[4:6] = mm_t(both, r.pick[...])[0:2]
     r.g_x1[1, :, 256:384] = mm_t(r.eye[...], r.gain_sums[...].astype(BF)).astype(BF)
-    sx1.step0()
+    for steps in (2, 1, 3, 0):
+        sx1.give(steps)
+    wide = (sx2, sz2, sd, so)
+    slim = (sz1, sx1)
+    for s in wide:
+        s.take(0)
+        s.step3()
+    for steps in (2, 1, 3):
+        for s in slim:
+            s.take(steps)
     r.igrad[...] = r.g_middle[...] + norm_back(grad_normed * r.mults[0:1], in_unit, input_inv)
-    for s in (sx2, sz2, sd, so):
+    for s in wide:
         s.step4()
-    sz1.step1()
-    sx1.step1()
-    for s in (sx2, sz2, sd, so):
+    for s in slim:
+        s.step2()
+    for s in wide:
         s.step5()
-    for step in ("step2", "step3", "step4", "step5", "step6"):
-        for s in (sz1, sx1):
-            getattr(s, step)()
-    for s in (sx2, sz2, sd, so):
+    for s in slim:
+        s.take(0)
+        s.step3()
+    for s in wide:
+        s.step6()
+    for s in slim:
+        s.step4()
+    for s in slim:
+        s.step5()
+    for s in slim:
         s.step6()
     net.finish()
 
 
-def layer(h, q, k, v, o, g, u, d, gains, lens, og):
+def layer(*args):
     vmem = pltpu.VMEM
-    ins = ("h", "q", "k", "v", "o", "g", "u", "d", "gains", "lens", "og")
+    ins = ("h", "q", "k", "v", "o", "g", "u", "d", *GAINS, "lens", "og")
     outs = {
         "mixed": ((T, D), BF),
         "igrad": ((T, D), F32),
@@ -866,6 +898,7 @@
         "w_o": ((2, 16, 4, 16, WO), BF),
         "w_d": ((16, 4, 2, 16, WD), BF),
         "tmp": ((160, 1024), F32),
+        "gain_rows": ((16, 128), F32),
         "turn": ((D, D), BF),
         "eye": ((D, D), BF),
         "pick": ((D, HD), BF),
@@ -917,7 +950,39 @@
             collective_id=0, has_side_effects=True, vmem_limit_bytes=VMEM_CAP
         ),
         name="decoder_layer",
-    )(h, q, k, v, o, g, u, d, gains, lens, og)
+    )(*args)
+
+
+def deliver_kernel(mixed, igrad, x1, z1, o, x2, z2, d, *outs):
+    outs[0][...] = mixed[...]
+    outs[1][...] = igrad[...]
+    outs[2][:, 0:512] = x1[0, 0:5]
+    outs[2][:, 512:896] = z1[0, 0:5]
+    outs[2][:, 896:1024] = z1[1, 0:5, 0:128]
+    outs[3][...] = x1[1, 0:5, 0:256]
+    outs[4][...] = z1[1, 0:5, 128:384]
+    outs[5][:, 0:384] = o[0]
+    outs[5][:, 384:640] = o[1, :, 0:256]
+    for i in range(2):
+        outs[6 + i][:, 0:1024] = x2[i, 0:5]
+        outs[6 + i][:, 1024:2048] = z2[i, 0:5]
+    outs[8][...] = d[...]
+    gains = x1[1, :, 256:384].T
+    for at, row, n in ((9, 0, 5), (10, 4, 2), (11, 5, 2), (12, 1, 5), (13, 2, 5), (14, 3, 5)):
+        outs[at][...] = gains[row : row + 1, 0:n].reshape(n)
+
+
+def deliver(*parts):
+    inside = pl.BlockSpec(memory_space=pltpu.VMEM)
+    shapes = [(T, D), (5, 1024), (5, 256), (5, 256), (8, D), (5, 2048), (5, 2048), (16, D)]
+    shapes += [(5,), (2,), (2,), (5,), (5,), (5,)]
+    return pl.pallas_call(
+        deliver_kernel,
+        out_shape=[jax.ShapeDtypeStruct((T, D), BF)] + [jax.ShapeDtypeStruct(s, F32) for s in shapes],
+        in_specs=[inside] * len(parts),
+        out_specs=[inside] * 15,
+        name="deliver",
+    )(*parts)
 
 
 def per_device(
@@ -938,9 +1003,8 @@
     seq_lengths,
     out_grad,
 ):
-    gains = jnp.concatenate([input_gain, mixer_gain, middle_gain, output_gain, query_gain, key_gain])
-    gains = jnp.pad(gains.astype(F32), (0, 104)).reshape(1, 128)
-    mixed, igrad, x1, z1, o, x2, z2, down_grad = layer(
+    gains = (input_gain, mixer_gain, middle_gain, output_gain, query_gain, key_gain)
+    parts = layer(
         hidden_in,
         query_weight,
         key_weight,
@@ -949,28 +1013,11 @@
         gate_weight,
         up_weight,
         down_weight,
-        gains,
+        *[a.reshape(1, -1) for a in gains],
         seq_lengths.reshape(1, 64),
         out_grad,
     )
-    sums = x1[1, :5, 256:384]
-    return (
-        mixed,
-        igrad,
-        jnp.concatenate([x1[0, :5], z1[0, :5], z1[1, :5, 0:128]], axis=1),
-        x1[1, :5, 0:256],
-        z1[1, :5, 128:384],
-        jnp.concatenate([o[0], o[1, :, 0:256]], axis=1),
-        jnp.concatenate([x2[0, :5], z2[0, :5]], axis=1),
-        jnp.concatenate([x2[1, :5], z2[1, :5]], axis=1),
-        down_grad,
-        sums[:, 0],
-        sums[:2, 4],
-        sums[:2, 5],
-        sums[:, 1],
-        sums[:, 2],
-        sums[:, 3],
-    )
+    return tuple(deliver(*parts))
 
 
 def solution(mesh):

time: 143 us -> 125 us (0.87)
  local copies, waits for them, and re-layouts: 7.96 us -> 0 us
  Pallas kernels: 131 us -> 124 us
  other arithmetic: 3.02 us -> 0 us
    pallas_call x1, Pallas kernels: 131 us -> 122 us  [layer(): pl.pallas_call(lambda *refs: layer_kernel(names, *refs), out_shape=[jax.S...]
    unnamed x25 -> x0, local copies, waits for them, and re-layouts: 3.01 us -> none
    concatenate x4 -> x0, other arithmetic: 2.5 us -> none  [the longest x1 0.64 us: per_device(): jnp.concatenate([x2[1, :5], z2[1, :5]], axis=1)]
    pallas_call x0 -> x1, Pallas kernels: none -> 2.3 us  [deliver(): pl.pallas_call(deliver_kernel, out_shape=[jax.ShapeDtypeStruct((T, D), BF...]
    concatenate x1 -> x0, local copies, waits for them, and re-layouts: 2.1 us -> none  [per_device(): jnp.concatenate([input_gain, mixer_gain, middle_gain, output_gain, query_...]
    slice x2 -> x0, local copies, waits for them, and re-layouts: 1.47 us -> none  [the longest x1 0.73 us: per_device(): sums[:, 3]]
where the time goes in v3:
time: 125 us
  Pallas kernels  124 us (99%)
    pallas_call x1, Pallas kernels, layer(): pl.pallas_call(lambda *refs: layer_kernel(names, *refs), out_shape=[jax.S...  122 us

profile of v3, /device:TPU:1, one launch (start us, length us, event | category | flops | bytes accessed | tf_op | source)
XLA Modules:
  0.0 125.3 jit_solution(18271450511116721557)
XLA Ops:
  0.7 122.2 %decoder_layer.1 = (bf16[256,640]{1,0:T(8,128)(2,1)}, f32[256,640]{1,0:T(8,128)}, f32[2,8,512]{2,1,0:T(8,128)}, f32[2,8,384]{2,1,0:T(8,128)}, f32[2,8,384]{2,1,0...) custom-call(bf16[256,640]{1,0:T(8,128)(2,1)} %refs_0_.1, bf16[5,1024]{1,0:T(8,128)(2,1)} %refs_1_.1, ...), custom_call_target="tpu_custom_call" | custom-call | tf_op jit(solution)/shard_map/decoder_layer/pallas_call | solution.py:943
  122.9 2.3 %deliver.1 = (bf16[256,640]{1,0:T(8,128)(2,1)}, f32[256,640]{1,0:T(8,128)}, f32[5,1024]{1,0:T(8,128)}, f32[5,256]{1,0:T(8,128)}, f32[5,256]{1,0:T(8,128)}, /*ind...) custom-call(bf16[256,640]{1,0:T(8,128)(2,1)} %get-tuple-element.23.m, ...), custom_call_target="tpu_custom_call" | custom-call | tf_op jit(solution)/shard_map/deliver/pallas_call | solution.py:979

commit v4 on v3

--- a/solution.py
+++ b/solution.py
@@ -546,12 +546,10 @@
         s.step2()
     for s in late:
         s.step2()
-    for s in early:
+    for s in (*early, *late):
         s.step3()
-    for s in early:
+    for s in (*early, *late):
         s.step4()
-    for s in late:
-        s.step3()
     for s in early:
         s.step5()
     x1.step6()
@@ -592,7 +590,7 @@
         r.q_unit[h] = raw * inv
         r.queries[h] = spin(raw * inv * r.mults[4:5, 0:HD], cosine, sine).astype(BF)
     for s in late:
-        s.step4()
+        s.step5()
     for copy in halo:
         copy.wait_recv()
 
@@ -604,12 +602,8 @@
         r.probs[h] = probs
         r.attended[h] = mm(probs.astype(BF), r.values[...]).astype(BF)
 
-    attend(0)
-    attend(1)
-    for s in late:
-        s.step5()
-    attend(2)
-    attend(3)
+    for h in range(HEADS):
+        attend(h)
 
     ow.step6()
     left = jnp.zeros((T, 384), F32)
@@ -748,13 +742,8 @@
     attend_back(0)
     for s in wide:
         s.take(3)
-    so.take(2)
-    attend_back(1)
-    so.take(1)
-    so.take(3)
-    attend_back(2)
-    sx2.step2()
-    attend_back(3)
+    for h in range(1, HEADS):
+        attend_back(h)
     back_halo = []
     for i, (whole, low) in enumerate(((r.d_keys, r.dk_low), (r.d_values, r.dv_low))):
         scale = SCALE if i == 0 else 1.0
@@ -763,9 +752,6 @@
             back_halo.append(
                 net.send(low.at[pl.ds(at, T)], r.halo_back.at[i, 0 if at else 1], net.along(steps))
             )
-    sz2.step2()
-    sd.step2()
-    so.step2()
 
     normed, turned = r.normed[...], r.normed_t[...]
     for h in range(HEADS):
@@ -777,6 +763,8 @@
             last = t_mm(turned, r.g_q[h]).astype(BF)
             r.g_z1[0, :, 256:384] = last[:, 0:128]
             r.g_z1[1, :, 0:128] = last[:, 128:256]
+    for s in wide:
+        s.step2()
     for copy in back_halo:
         copy.wait_recv()
     own_k = r.d_keys[2 * T :] * SCALE
@@ -814,28 +802,27 @@
     r.g_x1[1, :, 256:384] = mm_t(r.eye[...], r.gain_sums[...].astype(BF)).astype(BF)
     for steps in (2, 1, 3, 0):
         sx1.give(steps)
-    wide = (sx2, sz2, sd, so)
-    slim = (sz1, sx1)
+    slim = (so, sz1, sx1)
+    for steps in (2, 1, 3):
+        for s in slim:
+            s.take(steps)
     for s in wide:
         s.take(0)
         s.step3()
-    for steps in (2, 1, 3):
-        for s in slim:
-            s.take(steps)
     r.igrad[...] = r.g_middle[...] + norm_back(grad_normed * r.mults[0:1], in_unit, input_inv)
-    for s in wide:
-        s.step4()
     for s in slim:
         s.step2()
     for s in wide:
-        s.step5()
+        s.step4()
     for s in slim:
         s.take(0)
         s.step3()
     for s in wide:
-        s.step6()
+        s.step5()
     for s in slim:
         s.step4()
+    for s in wide:
+        s.step6()
     for s in slim:
         s.step5()
     for s in slim:

time: 125 us -> 120 us (0.960)
  Pallas kernels: 124 us -> 119 us
    pallas_call x1, Pallas kernels: 122 us -> 117 us  [layer(): pl.pallas_call(lambda *refs: layer_kernel(names, *refs), out_shape=[jax.S...]
where the time goes in v4:
time: 120 us
  Pallas kernels  119 us (99%)
    pallas_call x1, Pallas kernels, layer(): pl.pallas_call(lambda *refs: layer_kernel(names, *refs), out_shape=[jax.S...  117 us

profile of v4, /device:TPU:1, one launch (start us, length us, event | category | flops | bytes accessed | tf_op | source)
XLA Modules:
  0.0 120.3 jit_solution(13481749324208587244)
XLA Ops:
  0.7 117.2 %decoder_layer.1 = (bf16[256,640]{1,0:T(8,128)(2,1)}, f32[256,640]{1,0:T(8,128)}, f32[2,8,512]{2,1,0:T(8,128)}, f32[2,8,384]{2,1,0:T(8,128)}, f32[2,8,384]{2,1,0...) custom-call(bf16[256,640]{1,0:T(8,128)(2,1)} %refs_0_.1, bf16[5,1024]{1,0:T(8,128)(2,1)} %refs_1_.1, ...), custom_call_target="tpu_custom_call" | custom-call | tf_op jit(solution)/shard_map/decoder_layer/pallas_call | solution.py:930
  117.8 2.3 %deliver.1 = (bf16[256,640]{1,0:T(8,128)(2,1)}, f32[256,640]{1,0:T(8,128)}, f32[5,1024]{1,0:T(8,128)}, f32[5,256]{1,0:T(8,128)}, f32[5,256]{1,0:T(8,128)}, /*ind...) custom-call(bf16[256,640]{1,0:T(8,128)(2,1)} %get-tuple-element.23.m, ...), custom_call_target="tpu_custom_call" | custom-call | tf_op jit(solution)/shard_map/deliver/pallas_call | solution.py:966

commit v5 on v4

--- a/solution.py
+++ b/solution.py
@@ -55,7 +55,7 @@
 
     def greet(self):
         sem = pltpu.get_barrier_semaphore()
-        partners = [self.sib] + [self.along(s) for s in (1, 2, -1, -2)]
+        partners = [self.sib] + [self.along(s) for s in (2, -2)]
         for axis in ("x", "z", "y"):
             partners += [self.peer(axis, o) for o in (1, 2, 3)]
         for p in partners:
@@ -175,19 +175,20 @@
 class Tiles(Rows):
     blocks = 16
 
-    def __init__(self, net, w, by_core):
-        self.net, self.w, self.by_core, self.axes = net, w, by_core, ("z", "x", "y")
+    def __init__(self, net, axes, w, by_core):
+        self.net, self.axes, self.w, self.by_core = net, axes, w, by_core
         self.ends = []
 
     def view(self, slot, at, n):
         if self.by_core:
             return self.w.at[pl.ds(at, n), slot, self.net.core]
-        return self.w.at[self.net.core, pl.ds(at, n), slot]
+        return self.w.at[self.net.core, slot, pl.ds(at, n)]
 
     def first(self, src):
         net = self.net
-        dst = self.w.at[net.xz, net.at["y"], net.core] if self.by_core else self.w.at[net.core, net.xz, net.at["y"]]
-        self.p = [net.send(src, dst, net.peer("z", o)) for o in (1, 2, 3)]
+        a, b, c = (net.at[axis] for axis in self.axes)
+        dst = self.w.at[b * 4 + a, c, net.core] if self.by_core else self.w.at[net.core, c, b * 4 + a]
+        self.p = [net.send(src, dst, net.peer(self.axes[0], o)) for o in (1, 2, 3)]
         self.kept = net.local(src, dst)
 
     def step2(self):
@@ -195,16 +196,16 @@
         for copy in self.p:
             copy.wait_recv()
         self.kept.wait()
-        part = self.view(net.at["y"], net.at["x"] * 4, 4)
-        self.p = [net.send(part, part, net.peer("x", o)) for o in (1, 2, 3)]
+        part = self.view(net.at[self.axes[2]], net.at[self.axes[1]] * 4, 4)
+        self.p = [net.send(part, part, net.peer(self.axes[1], o)) for o in (1, 2, 3)]
 
     def step3(self):
-        net = self.net
+        net, axis = self.net, self.axes[2]
         for copy in self.p:
             copy.wait_recv()
-        part = self.view(net.at["y"], 0, 16)
-        self.up = net.send(part, part, net.peer("y", 1))
-        self.down = net.send(part, part, net.peer("y", 3))
+        part = self.view(net.at[axis], 0, 16)
+        self.up = net.send(part, part, net.peer(axis, 1))
+        self.down = net.send(part, part, net.peer(axis, 3))
         self.ends.append(net.send(part, part, net.sib).wait_recv)
 
 
@@ -333,22 +334,22 @@
 class TileSums(RowSums):
     blocks = 16
 
-    def __init__(self, net, width, by_core, refs):
+    def __init__(self, net, axes, width, by_core, refs):
         self.by_core = by_core
-        super().__init__(net, ("z", "x", "y"), width, refs)
+        super().__init__(net, axes, width, refs)
 
     def view(self, steps, at, n, which):
-        slot = self.net.slot("y", steps)
+        slot = self.net.slot(self.axes[2], steps)
         if self.by_core:
             return self.g.at[pl.ds(at, n), slot, which]
-        return self.g.at[which, pl.ds(at, n), slot]
+        return self.g.at[which, slot, pl.ds(at, n)]
 
     def rows(self, at, n):
         return pl.ds(at, n)
 
     def tile(self, steps, i):
-        slot = self.net.slot("y", steps)
-        return (i, slot, self.net.core) if self.by_core else (self.net.core, i, slot)
+        slot = self.net.slot(self.axes[2], steps)
+        return (i, slot, self.net.core) if self.by_core else (self.net.core, slot, i)
 
     def block(self, i):
         return i
@@ -364,7 +365,9 @@
 
         lax.fori_loop(0, 16, body, 0)
         self.p = [
-            net.send(self.t2.at[pl.ds(net.slot("x", o) * 4, 4)], self.r2.at[o - 1], net.peer("x", o))
+            net.send(
+                self.t2.at[pl.ds(net.slot(self.axes[1], o) * 4, 4)], self.r2.at[o - 1], net.peer(self.axes[1], o)
+            )
             for o in (1, 2, 3)
         ]
 
@@ -373,17 +376,18 @@
         for copy in self.p:
             copy.wait_recv()
         for j in range(4):
-            value = self.t2[net.at["x"] * 4 + j].astype(F32)
+            value = self.t2[net.at[self.axes[1]] * 4 + j].astype(F32)
             for o in range(3):
                 value = value + self.r2[o, j].astype(F32)
             self.t1[j] = value.astype(BF)
-        self.p = [net.send(self.t1.at[net.slot("z", o)], self.r1.at[o - 1], net.peer("z", o)) for o in (1, 2, 3)]
+        axis = self.axes[0]
+        self.p = [net.send(self.t1.at[net.slot(axis, o)], self.r1.at[o - 1], net.peer(axis, o)) for o in (1, 2, 3)]
 
     def step5(self):
         net = self.net
         for copy in self.p:
             copy.wait_recv()
-        own = self.t1[net.at["z"]].astype(F32)
+        own = self.t1[net.at[self.axes[0]]].astype(F32)
         for o in range(3):
             own = own + self.r1[o].astype(F32)
         if self.by_core:
@@ -482,7 +486,7 @@
     for s in (x1, z1, x2, z2):
         s.step0()
     r.es_o[...] = r.own_o[net.other].astype(BF)
-    return x1, z1, x2, z2, Tiles(net, r.w_o, False), Tiles(net, r.w_d, True)
+    return x1, z1, x2, z2, Tiles(net, ("y", "x", "z"), r.w_o, False), Tiles(net, ("z", "x", "y"), r.w_d, True)
 
 
 def layer_kernel(names, *refs):
@@ -498,12 +502,14 @@
     net = Links(r.send_sems, r.recv_sems)
     net.greet()
     x1, z1, x2, z2, ow, dw = gather_setup(net, r)
+    r.rows_in[0] = r.h[...]
     net.meet()
     x1.step0b()
     z1.step0b()
     swap_o = net.send(r.es_o, r.ed_o, net.sib)
     x2.step0b()
     z2.step0b()
+    ahead_copy = net.send(r.rows_in.at[0], r.rows_in.at[1], net.along(2))
     x1.step1()
     z1.step1()
     swap_o.wait_recv()
@@ -526,7 +532,7 @@
     column = jnp.sum(jnp.where(spot == count((64, 64), 1), lens, 0.0), axis=1, keepdims=True)
     ends = jnp.sum(jnp.where(spot <= count((64, 64), 1), column, 0.0), axis=0, keepdims=True)
     offset = net.me * T
-    token = (count((T, 64), 0) + offset).astype(F32)
+    token = (count((SPAN, 64), 0) + (offset - 2 * T)).astype(F32)
     start = jnp.max(jnp.where(ends <= token, ends, 0.0), axis=1, keepdims=True)
     position = token[:, 0:1] - start
     pair = count((1, 128), 1).astype(F32)
@@ -535,7 +541,7 @@
     r.sine[...] = jnp.sin(angle)
     ahead = count((T, SPAN), 1) - 2 * T
     distance = count((T, SPAN), 0) - ahead
-    inside = (distance >= 0) & (distance < WINDOW) & ((ahead + offset).astype(F32) >= start)
+    inside = (distance >= 0) & (distance < WINDOW) & ((ahead + offset).astype(F32) >= start[2 * T :])
     r.bias[...] = jnp.where(inside, 0.0, NEG_FILL)
     hidden = r.h[...].astype(F32)
     input_inv = inv_of(hidden)
@@ -546,6 +552,8 @@
         s.step2()
     for s in late:
         s.step2()
+    ahead_copy.wait_recv()
+    side_copy = net.send(r.rows_in.at[net.core], r.rows_side, net.sib)
     for s in (*early, *late):
         s.step3()
     for s in (*early, *late):
@@ -566,16 +574,22 @@
     r.normed[...] = normed
     turned = mm(normed, r.turn[...]).astype(BF)
     r.normed_t[...] = turned
-    cosine, sine = r.cosine[...], r.sine[...]
-    key_raw = mm(normed, r.w_x1[1, :, 0:256])
-    key_inv = inv_of(key_raw)
-    r.k_unit[...] = key_raw * key_inv
-    r.keys[2 * T :] = spin(r.k_unit[...] * r.mults[5:6, 0:HD], cosine, sine).astype(BF)
-    r.values[2 * T :] = mm(turned, r.w_z1[1, :, 128:384]).astype(BF)
-    halo = []
-    for steps, at in ((1, T), (2, 0)):
-        for whole in (r.keys, r.values):
-            halo.append(net.send(whole.at[pl.ds(2 * T, T)], whole.at[pl.ds(at, T)], net.along(steps)))
+    cosine, sine = r.cosine[2 * T :], r.sine[2 * T :]
+    side_copy.wait_recv()
+    for i in range(3):
+        some = slice(T * i, T * i + T)
+        if i < 2:
+            rows = (r.rows_in[1] if i == 0 else r.rows_side[...]).astype(F32)
+            here = (rows * inv_of(rows) * r.mults[0:1]).astype(BF)
+            there = mm(here, r.turn[...]).astype(BF)
+        else:
+            here, there = normed, turned
+        key_raw = mm(here, r.w_x1[1, :, 0:256])
+        key_inv = inv_of(key_raw)
+        key_unit = key_raw * key_inv
+        r.keys[some] = spin(key_unit * r.mults[5:6, 0:HD], r.cosine[some], r.sine[some]).astype(BF)
+        r.values[some] = mm(there, r.w_z1[1, :, 128:384]).astype(BF)
+    r.k_unit[...] = key_unit
     for h in range(HEADS):
         if h < 2:
             raw = mm(normed, r.w_x1[0, :, 256 * h : 256 * h + 256])
@@ -591,8 +605,6 @@
         r.queries[h] = spin(raw * inv * r.mults[4:5, 0:HD], cosine, sine).astype(BF)
     for s in late:
         s.step5()
-    for copy in halo:
-        copy.wait_recv()
 
     def attend(h):
         scores = mm_t(r.queries[h], r.keys[...]) * SCALE + r.bias[...]
@@ -610,8 +622,8 @@
     right = jnp.zeros((T, 256), F32)
     for h in range(HEADS):
         some = slice(4 * h, 4 * h + 4)
-        left = left + mm(r.attended[h], r.w_o[0, some].reshape(256, WO))
-        right = right + mm(r.attended[h], r.w_o[1, some].reshape(256, WO)[:, 0:256])
+        left = left + mm(r.attended[h], r.w_o[0, :, some].reshape(256, WO))
+        right = right + mm(r.attended[h], r.w_o[1, :, some].reshape(256, WO)[:, 0:256])
     mixer_out = jnp.concatenate([left, right], axis=1)
     mixer_inv = inv_of(mixer_out)
     r.mix_unit[...] = mixer_out * mixer_inv
@@ -666,8 +678,8 @@
     sz1 = sums(RowSums, "z1", ("x", "y", "z"), WZ1)
     sx2 = sums(RowSums, "x2", ("y", "z", "x"), WX2)
     sz2 = sums(RowSums, "z2", ("x", "y", "z"), WZ2)
-    so = sums(TileSums, "o", WO, False)
-    sd = sums(TileSums, "d", WD, True)
+    so = sums(TileSums, "o", ("y", "x", "z"), WO, False)
+    sd = sums(TileSums, "d", ("z", "x", "y"), WD, True)
     wide = (sx2, sz2, sd)
     for w, g, rows_in, first, total in (
         (r.w_x2, r.g_x2, r.mid, 0, r.acc),
@@ -710,19 +722,38 @@
     for h in range(HEADS):
         some = slice(4 * h, 4 * h + 4)
         r.g_att[h] = (
-            mm_t(grad_mixer[:, 0:384], r.w_o[0, some].reshape(256, WO))
-            + mm_t(grad_mixer[:, 384:640], r.w_o[1, some].reshape(256, WO)[:, 0:256])
+            mm_t(grad_mixer[:, 0:384], r.w_o[0, :, some].reshape(256, WO))
+            + mm_t(grad_mixer[:, 384:640], r.w_o[1, :, some].reshape(256, WO)[:, 0:256])
         ).astype(BF)
         grad = t_mm(r.attended[h], grad_mixer).astype(BF)
-        r.g_o[0, some] = grad[:, 0:384].reshape(4, 4, 16, 384)
-        r.g_o[1, some, :, :, 0:256] = grad[:, 384:640].reshape(4, 4, 16, 256)
+        r.g_o[0, :, some] = grad[:, 0:384].reshape(4, 4, 16, 384)
+        r.g_o[1, :, some, :, 0:256] = grad[:, 384:640].reshape(4, 4, 16, 256)
     for steps in (2, 1, 3, 0):
         so.give(steps)
+    r.d_values[...] = t_mm(r.probs[0].astype(BF), r.g_att[0])
+    for h in range(1, HEADS):
+        r.d_values[...] += t_mm(r.probs[h].astype(BF), r.g_att[h])
+
+    def halo_aside(i, whole, scale):
+        r.low[i] = (whole[0 : 2 * T] * scale).astype(BF)
+        return net.send(r.low.at[i, pl.ds(T, T)], r.side.at[i], net.sib)
+
+    def halo_back(i, copy):
+        copy.wait_recv()
+        far = r.low[i, 0:T]
+        r.onward[i] = jnp.where(net.core == 1, far + r.side[i], far)
+        return net.send(r.onward.at[i], r.back.at[i], net.along(-2))
+
+    def halo_sum(i, whole, scale, copy):
+        copy.wait_recv()
+        side = jnp.where(net.core == 0, r.side[i].astype(F32), 0.0)
+        return whole[2 * T :] * scale + r.back[i].astype(F32) + side
+
+    aside_v = halo_aside(1, r.d_values, 1.0)
     for s in wide:
         s.take(1)
 
     r.d_keys[...] = jnp.zeros_like(r.d_keys)
-    r.d_values[...] = jnp.zeros_like(r.d_values)
     r.q_gain[...] = jnp.zeros_like(r.q_gain)
 
     def attend_back(h):
@@ -733,27 +764,22 @@
         grad_scores = (probs * (grad_probs - delta)).astype(BF)
         grad_q = mm(grad_scores, r.keys[...]) * SCALE
         r.d_keys[...] += t_mm(grad_scores, r.queries[h])
-        r.d_values[...] += t_mm(probs.astype(BF), g_att)
-        back = spin_back(grad_q, r.cosine[...], r.sine[...])
+        back = spin_back(grad_q, r.cosine[2 * T :], r.sine[2 * T :])
         unit = r.q_unit[h]
         r.q_gain[...] += jnp.sum(back * unit, axis=0, keepdims=True)
         r.g_q[h] = norm_back(back * r.mults[4:5, 0:HD], unit, r.q_inv[h]).astype(BF)
 
     attend_back(0)
-    for s in wide:
+    back_v = halo_back(1, aside_v)
+    for s in (sx2, sz2):
         s.take(3)
     for h in range(1, HEADS):
         attend_back(h)
-    back_halo = []
-    for i, (whole, low) in enumerate(((r.d_keys, r.dk_low), (r.d_values, r.dv_low))):
-        scale = SCALE if i == 0 else 1.0
-        low[...] = (whole[0 : 2 * T] * scale).astype(BF)
-        for steps, at in ((-1, T), (-2, 0)):
-            back_halo.append(
-                net.send(low.at[pl.ds(at, T)], r.halo_back.at[i, 0 if at else 1], net.along(steps))
-            )
+    aside_k = halo_aside(0, r.d_keys, SCALE)
 
     normed, turned = r.normed[...], r.normed_t[...]
+    back_k = halo_back(0, aside_k)
+    sd.take(3)
     for h in range(HEADS):
         if h < 2:
             r.g_x1[0, :, 256 * h : 256 * h + 256] = t_mm(normed, r.g_q[h]).astype(BF)
@@ -765,14 +791,9 @@
             r.g_z1[1, :, 0:128] = last[:, 128:256]
     for s in wide:
         s.step2()
-    for copy in back_halo:
-        copy.wait_recv()
-    own_k = r.d_keys[2 * T :] * SCALE
-    own_v = r.d_values[2 * T :]
-    for i in range(2):
-        own_k = own_k + r.halo_back[0, i].astype(F32)
-        own_v = own_v + r.halo_back[1, i].astype(F32)
-    key_back = spin_back(own_k, r.cosine[...], r.sine[...])
+    own_k = halo_sum(0, r.d_keys, SCALE, back_k)
+    own_v = halo_sum(1, r.d_values, 1.0, back_v)
+    key_back = spin_back(own_k, cosine, sine)
     k_unit = r.k_unit[...]
     key_gain = jnp.sum(key_back * k_unit, axis=0, keepdims=True)
     grad_k = norm_back(key_back * r.mults[5:6, 0:HD], k_unit, key_inv).astype(BF)
@@ -882,15 +903,17 @@
         "s1_o": ((16, WO), BF),
         "swap_o": ((8, WO), F32),
         "got_o": ((8, WO), F32),
-        "w_o": ((2, 16, 4, 16, WO), BF),
+        "w_o": ((2, 4, 16, 16, WO), BF),
         "w_d": ((16, 4, 2, 16, WD), BF),
         "tmp": ((160, 1024), F32),
         "gain_rows": ((16, 128), F32),
         "turn": ((D, D), BF),
         "eye": ((D, D), BF),
         "pick": ((D, HD), BF),
-        "cosine": ((T, 128), F32),
-        "sine": ((T, 128), F32),
+        "cosine": ((SPAN, 128), F32),
+        "sine": ((SPAN, 128), F32),
+        "rows_in": ((2, T, D), BF),
+        "rows_side": ((T, D), BF),
         "bias": ((T, SPAN), F32),
         "mults": ((8, D), F32),
         "gain_sums": ((128, D), F32),
@@ -920,9 +943,10 @@
         "g_q": ((HEADS, T, HD), BF),
         "d_keys": ((SPAN, HD), F32),
         "d_values": ((SPAN, HD), F32),
-        "dk_low": ((2 * T, HD), BF),
-        "dv_low": ((2 * T, HD), BF),
-        "halo_back": ((2, 2, T, HD), BF),
+        "low": ((2, 2 * T, HD), BF),
+        "side": ((2, T, HD), BF),
+        "onward": ((2, T, HD), BF),
+        "back": ((2, T, HD), BF),
         "q_gain": ((1, HD), F32),
     }
     inside = pl.BlockSpec(memory_space=vmem)

time: 120 us -> 121 us (level)
  no operation moved by 1% of the time
where the time goes in v5:
time: 121 us
  Pallas kernels  120 us (99%)
    pallas_call x1, Pallas kernels, layer(): pl.pallas_call(lambda *refs: layer_kernel(names, *refs), out_shape=[jax.S...  118 us

profile of v5, /device:TPU:1, one launch (start us, length us, event | category | flops | bytes accessed | tf_op | source)
XLA Modules:
  0.0 121.0 jit_solution(16608582507773413643)
XLA Ops:
  0.7 117.9 %decoder_layer.1 = (bf16[256,640]{1,0:T(8,128)(2,1)}, f32[256,640]{1,0:T(8,128)}, f32[2,8,512]{2,1,0:T(8,128)}, f32[2,8,384]{2,1,0:T(8,128)}, f32[2,8,384]{2,1,0...) custom-call(bf16[256,640]{1,0:T(8,128)(2,1)} %refs_0_.1, bf16[5,1024]{1,0:T(8,128)(2,1)} %refs_1_.1, ...), custom_call_target="tpu_custom_call" | custom-call | tf_op jit(solution)/shard_map/decoder_layer/pallas_call | solution.py:954
  118.5 2.3 %deliver.1 = (bf16[256,640]{1,0:T(8,128)(2,1)}, f32[256,640]{1,0:T(8,128)}, f32[5,1024]{1,0:T(8,128)}, f32[5,256]{1,0:T(8,128)}, f32[5,256]{1,0:T(8,128)}, /*ind...) custom-call(bf16[256,640]{1,0:T(8,128)(2,1)} %get-tuple-element.23.m, ...), custom_call_target="tpu_custom_call" | custom-call | tf_op jit(solution)/shard_map/deliver/pallas_call | solution.py:990

commit v6 on v5

--- a/solution.py
+++ b/solution.py
@@ -457,15 +457,14 @@
         ref[...] = jnp.zeros_like(ref)
     q = r.q[...].astype(F32)
     r.own_x1[0, 0:5] = q[:, 0:512]
-    r.own_x1[1, 0:5, 0:256] = r.k[...].astype(F32)
+    r.own_x1[1, 0:5] = q[:, 512:1024]
     r.gain_rows[...] = jnp.zeros_like(r.gain_rows)
     for i, gain in enumerate((r.n_in, r.n_mix, r.n_mid, r.n_out, r.n_q, r.n_k)):
         r.gain_rows[i : i + 1, 0 : gain.shape[1]] = gain[...].astype(F32)
     tile = t_mm(r.gain_rows[...].astype(BF), hot(count((16, 128), 0) == count((16, 128), 1)))
-    r.own_x1[1, 0:5, 256:384] = tile[0:5]
-    r.own_z1[0, 0:5] = q[:, 512:896]
-    r.own_z1[1, 0:5, 0:128] = q[:, 896:1024]
-    r.own_z1[1, 0:5, 128:384] = r.v[...].astype(F32)
+    r.own_z1[0, 0:5, 256:384] = tile[0:5]
+    r.own_z1[0, 0:5, 0:256] = r.k[...].astype(F32)
+    r.own_z1[1, 0:5, 0:256] = r.v[...].astype(F32)
     g, u = r.g[...].astype(F32), r.u[...].astype(F32)
     r.own_x2[0, 0:5] = g[:, 0:1024]
     r.own_x2[1, 0:5] = u[:, 0:1024]
@@ -509,7 +508,6 @@
     swap_o = net.send(r.es_o, r.ed_o, net.sib)
     x2.step0b()
     z2.step0b()
-    ahead_copy = net.send(r.rows_in.at[0], r.rows_in.at[1], net.along(2))
     x1.step1()
     z1.step1()
     swap_o.wait_recv()
@@ -526,7 +524,6 @@
     tens = (j_dim * 52429) >> 19
     source = (tens & 3) * 160 + (tens >> 4) * 40 + ((tens >> 2) & 3) * 10 + (j_dim - 10 * tens)
     r.turn[...] = hot(k_dim == source)
-    r.eye[...] = hot(k_dim == j_dim)
     spot = count((64, 64), 0)
     lens = jnp.broadcast_to(r.lens[...].astype(F32), (64, 64))
     column = jnp.sum(jnp.where(spot == count((64, 64), 1), lens, 0.0), axis=1, keepdims=True)
@@ -552,10 +549,11 @@
         s.step2()
     for s in late:
         s.step2()
+    ahead_copy = net.send(r.rows_in.at[0], r.rows_in.at[1], net.along(2))
+    for s in (*early, *late):
+        s.step3()
     ahead_copy.wait_recv()
     side_copy = net.send(r.rows_in.at[net.core], r.rows_side, net.sib)
-    for s in (*early, *late):
-        s.step3()
     for s in (*early, *late):
         s.step4()
     for s in early:
@@ -563,11 +561,12 @@
     x1.step6()
     z1.step6()
 
-    gain_tile = r.w_x1[1, :, 256:384]
-    gain_rows = t_mm(gain_tile, r.eye[...])
+    gain_rows = lax.dot_general(
+        r.w_z1[0, :, 256:384], r.turn[...], (((0,), (1,)), ((), ())), preferred_element_type=F32
+    )
     far, near = count((D, HD), 0), count((D, HD), 1)
     r.pick[...] = hot(far == 5 * (near >> 1) + (near & 1))
-    head_rows = t_mm(gain_tile, r.pick[...])
+    head_rows = mm(gain_rows.astype(BF), r.pick[...])
     r.mults[0:4] = 1.0 + gain_rows[0:4]
     r.mults[4:6, 0:HD] = 1.0 + head_rows[4:6]
     normed = (r.in_unit[...] * r.mults[0:1]).astype(BF)
@@ -575,6 +574,12 @@
     turned = mm(normed, r.turn[...]).astype(BF)
     r.normed_t[...] = turned
     cosine, sine = r.cosine[2 * T :], r.sine[2 * T :]
+    for h in range(HEADS):
+        raw = mm(normed, r.w_x1[h // 2, :, 256 * (h % 2) : 256 * (h % 2) + 256])
+        inv = inv_of(raw)
+        r.q_inv[h] = inv
+        r.q_unit[h] = raw * inv
+        r.queries[h] = spin(raw * inv * r.mults[4:5, 0:HD], cosine, sine).astype(BF)
     side_copy.wait_recv()
     for i in range(3):
         some = slice(T * i, T * i + T)
@@ -583,26 +588,13 @@
             here = (rows * inv_of(rows) * r.mults[0:1]).astype(BF)
             there = mm(here, r.turn[...]).astype(BF)
         else:
-            here, there = normed, turned
-        key_raw = mm(here, r.w_x1[1, :, 0:256])
+            there = turned
+        key_raw = mm(there, r.w_z1[0, :, 0:256])
         key_inv = inv_of(key_raw)
         key_unit = key_raw * key_inv
         r.keys[some] = spin(key_unit * r.mults[5:6, 0:HD], r.cosine[some], r.sine[some]).astype(BF)
-        r.values[some] = mm(there, r.w_z1[1, :, 128:384]).astype(BF)
+        r.values[some] = mm(there, r.w_z1[1, :, 0:256]).astype(BF)
     r.k_unit[...] = key_unit
-    for h in range(HEADS):
-        if h < 2:
-            raw = mm(normed, r.w_x1[0, :, 256 * h : 256 * h + 256])
-        elif h == 2:
-            raw = mm(turned, r.w_z1[0, :, 0:256])
-        else:
-            raw = jnp.concatenate(
-                [mm(turned, r.w_z1[0, :, 256:384]), mm(turned, r.w_z1[1, :, 0:128])], axis=1
-            )
-        inv = inv_of(raw)
-        r.q_inv[h] = inv
-        r.q_unit[h] = raw * inv
-        r.queries[h] = spin(raw * inv * r.mults[4:5, 0:HD], cosine, sine).astype(BF)
     for s in late:
         s.step5()
 
@@ -776,21 +768,20 @@
     for h in range(1, HEADS):
         attend_back(h)
     aside_k = halo_aside(0, r.d_keys, SCALE)
+    for steps in (2, 1, 3):
+        so.take(steps)
 
     normed, turned = r.normed[...], r.normed_t[...]
+    for h in range(HEADS):
+        r.g_x1[h // 2, :, 256 * (h % 2) : 256 * (h % 2) + 256] = t_mm(normed, r.g_q[h]).astype(BF)
+    for steps in (2, 1, 3, 0):
+        sx1.give(steps)
     back_k = halo_back(0, aside_k)
     sd.take(3)
-    for h in range(HEADS):
-        if h < 2:
-            r.g_x1[0, :, 256 * h : 256 * h + 256] = t_mm(normed, r.g_q[h]).astype(BF)
-        elif h == 2:
-            r.g_z1[0, :, 0:256] = t_mm(turned, r.g_q[h]).astype(BF)
-        else:
-            last = t_mm(turned, r.g_q[h]).astype(BF)
-            r.g_z1[0, :, 256:384] = last[:, 0:128]
-            r.g_z1[1, :, 0:128] = last[:, 128:256]
     for s in wide:
         s.step2()
+    for steps in (2, 1, 3):
+        sx1.take(steps)
     own_k = halo_sum(0, r.d_keys, SCALE, back_k)
     own_v = halo_sum(1, r.d_values, 1.0, back_v)
     key_back = spin_back(own_k, cosine, sine)
@@ -798,56 +789,53 @@
     key_gain = jnp.sum(key_back * k_unit, axis=0, keepdims=True)
     grad_k = norm_back(key_back * r.mults[5:6, 0:HD], k_unit, key_inv).astype(BF)
     grad_v = own_v.astype(BF)
-    r.g_z1[1, :, 128:384] = t_mm(turned, grad_v).astype(BF)
-    for steps in (2, 1, 3, 0):
-        sz1.give(steps)
-    r.g_x1[1, :, 0:256] = t_mm(normed, grad_k).astype(BF)
-    r.g_x1[1, :, 384:512] = jnp.zeros((D, 128), BF)
-    grad_natural = (
-        mm_t(r.g_q[0], r.w_x1[0, :, 0:256])
-        + mm_t(r.g_q[1], r.w_x1[0, :, 256:512])
-        + mm_t(grad_k, r.w_x1[1, :, 0:256])
-    )
-    g_last = r.g_q[3]
-    grad_turned = (
-        mm_t(r.g_q[2], r.w_z1[0, :, 0:256])
-        + mm_t(g_last[:, 0:128], r.w_z1[0, :, 256:384])
-        + mm_t(g_last[:, 128:256], r.w_z1[1, :, 0:128])
-        + mm_t(grad_v, r.w_z1[1, :, 128:384])
-    )
+    r.g_z1[0, :, 0:256] = t_mm(turned, grad_k).astype(BF)
+    r.g_z1[1, :, 0:256] = t_mm(turned, grad_v).astype(BF)
+    r.g_z1[1, :, 256:384] = jnp.zeros((D, 128), BF)
+    grad_natural = mm_t(r.g_q[0], r.w_x1[0, :, 0:256])
+    for h in range(1, HEADS):
+        grad_natural = grad_natural + mm_t(r.g_q[h], r.w_x1[h // 2, :, 256 * (h % 2) : 256 * (h % 2) + 256])
+    grad_turned = mm_t(grad_k, r.w_z1[0, :, 0:256]) + mm_t(grad_v, r.w_z1[1, :, 0:256])
     grad_normed = grad_natural + split_dot(grad_turned, r.turn[...])
     in_unit = r.in_unit[...]
     r.gain_sums[0:1] = jnp.sum(grad_normed * in_unit, axis=0, keepdims=True)
     both = jnp.concatenate([r.q_gain[...], key_gain, jnp.zeros((6, HD), F32)], axis=0).astype(BF)
     r.gain_sums[4:6] = mm_t(both, r.pick[...])[0:2]
-    r.g_x1[1, :, 256:384] = mm_t(r.eye[...], r.gain_sums[...].astype(BF)).astype(BF)
+    r.g_z1[0, :, 256:384] = lax.dot_general(
+        r.turn[...], r.gain_sums[...].astype(BF), (((0,), (1,)), ((), ())), preferred_element_type=F32
+    ).astype(BF)
     for steps in (2, 1, 3, 0):
-        sx1.give(steps)
-    slim = (so, sz1, sx1)
+        sz1.give(steps)
+    so.step2()
     for steps in (2, 1, 3):
-        for s in slim:
-            s.take(steps)
+        sz1.take(steps)
     for s in wide:
         s.take(0)
         s.step3()
+    sx1.step2()
     r.igrad[...] = r.g_middle[...] + norm_back(grad_normed * r.mults[0:1], in_unit, input_inv)
-    for s in slim:
-        s.step2()
+    sz1.step2()
+    so.take(0)
+    so.step3()
     for s in wide:
         s.step4()
-    for s in slim:
-        s.take(0)
-        s.step3()
+    sx1.take(0)
+    sx1.step3()
+    sz1.take(0)
+    sz1.step3()
+    so.step4()
     for s in wide:
         s.step5()
-    for s in slim:
-        s.step4()
+    sx1.step4()
+    sz1.step4()
+    so.step5()
+    sx1.step5()
     for s in wide:
         s.step6()
-    for s in slim:
-        s.step5()
-    for s in slim:
-        s.step6()
+    sz1.step5()
+    so.step6()
+    sx1.step6()
+    sz1.step6()
     net.finish()
 
 
@@ -908,7 +896,6 @@
         "tmp": ((160, 1024), F32),
         "gain_rows": ((16, 128), F32),
         "turn": ((D, D), BF),
-        "eye": ((D, D), BF),
         "pick": ((D, HD), BF),
         "cosine": ((SPAN, 128), F32),
         "sine": ((SPAN, 128), F32),
@@ -968,17 +955,16 @@
     outs[0][...] = mixed[...]
     outs[1][...] = igrad[...]
     outs[2][:, 0:512] = x1[0, 0:5]
-    outs[2][:, 512:896] = z1[0, 0:5]
-    outs[2][:, 896:1024] = z1[1, 0:5, 0:128]
-    outs[3][...] = x1[1, 0:5, 0:256]
-    outs[4][...] = z1[1, 0:5, 128:384]
+    outs[2][:, 512:1024] = x1[1, 0:5]
+    outs[3][...] = z1[0, 0:5, 0:256]
+    outs[4][...] = z1[1, 0:5, 0:256]
     outs[5][:, 0:384] = o[0]
     outs[5][:, 384:640] = o[1, :, 0:256]
     for i in range(2):
         outs[6 + i][:, 0:1024] = x2[i, 0:5]
         outs[6 + i][:, 1024:2048] = z2[i, 0:5]
     outs[8][...] = d[...]
-    gains = x1[1, :, 256:384].T
+    gains = z1[0, :, 256:384].T
     for at, row, n in ((9, 0, 5), (10, 4, 2), (11, 5, 2), (12, 1, 5), (13, 2, 5), (14, 3, 5)):
         outs[at][...] = gains[row : row + 1, 0:n].reshape(n)
 

time: 121 us -> 117 us (0.967)
  Pallas kernels: 120 us -> 116 us
    pallas_call x1, Pallas kernels: 118 us -> 113 us  [layer(): pl.pallas_call(lambda *refs: layer_kernel(names, *refs), out_shape=[jax.S...]
where the time goes in v6:
time: 117 us
  Pallas kernels  116 us (99%)
    pallas_call x1, Pallas kernels, layer(): pl.pallas_call(lambda *refs: layer_kernel(names, *refs), out_shape=[jax.S...  113 us

profile of v6, /device:TPU:1, one launch (start us, length us, event | category | flops | bytes accessed | tf_op | source)
XLA Modules:
  0.0 116.6 jit_solution(12828778275069186392)
XLA Ops:
  0.7 113.5 %decoder_layer.1 = (bf16[256,640]{1,0:T(8,128)(2,1)}, f32[256,640]{1,0:T(8,128)}, f32[2,8,512]{2,1,0:T(8,128)}, f32[2,8,384]{2,1,0:T(8,128)}, f32[2,8,384]{2,1,0...) custom-call(bf16[256,640]{1,0:T(8,128)(2,1)} %refs_0_.1, bf16[5,1024]{1,0:T(8,128)(2,1)} %refs_1_.1, ...), custom_call_target="tpu_custom_call" | custom-call | tf_op jit(solution)/shard_map/decoder_layer/pallas_call | solution.py:941
  114.2 2.3 %deliver.1 = (bf16[256,640]{1,0:T(8,128)(2,1)}, f32[256,640]{1,0:T(8,128)}, f32[5,1024]{1,0:T(8,128)}, f32[5,256]{1,0:T(8,128)}, f32[5,256]{1,0:T(8,128)}, /*ind...) custom-call(bf16[256,640]{1,0:T(8,128)(2,1)} %get-tuple-element.23.m, ...), custom_call_target="tpu_custom_call" | custom-call | tf_op jit(solution)/shard_map/deliver/pallas_call | solution.py:976

commit v7 on v6

--- a/solution.py
+++ b/solution.py
@@ -632,7 +632,7 @@
     for w, rows_in, first in ((r.w_x2, r.mid, 0), (r.w_z2, r.mid_t, 2)):
 
         def forward(j, carry, w=w, rows_in=rows_in, first=first):
-            cols = pl.ds(pl.multiple_of(j * 512, 512), 512)
+            cols = slice(512 * j, 512 * j + 512)
             gate = mm(rows_in[...], w[0, :, cols])
             up = mm(rows_in[...], w[1, :, cols])
             square = gate * gate
@@ -646,10 +646,11 @@
             r.units[part] = units
             r.active[part] = active
             r.slope_up[part] = slope * up
-            r.acc[...] += mm(units, r.w_d[pl.ds(part * 4, 4)].reshape(512, D))
+            r.acc[...] += mm(units, r.w_d[4 * part : 4 * part + 4].reshape(512, D))
             return carry
 
-        lax.fori_loop(0, 2, forward, 0)
+        for j in range(2):
+            forward(j, 0)
     ffn_out = r.acc[...]
     ffn_inv = inv_of(ffn_out)
     ffn_unit = ffn_out * ffn_inv
@@ -680,9 +681,9 @@
         total[...] = jnp.zeros_like(total)
 
         def backward(j, carry, w=w, g=g, rows_in=rows_in, first=first, total=total):
-            cols = pl.ds(pl.multiple_of(j * 512, 512), 512)
+            cols = slice(512 * j, 512 * j + 512)
             part = first + j
-            some = pl.ds(part * 4, 4)
+            some = slice(4 * part, 4 * part + 4)
             g_ffn = r.g_ffn[...]
             grad_hidden = mm_t(g_ffn, r.w_d[some].reshape(512, D))
             r.g_d[some] = t_mm(r.units[part], g_ffn).astype(BF).reshape(4, 4, 2, 16, D)
@@ -693,7 +694,8 @@
             g[1, :, cols] = t_mm(rows_in[...], grad_up).astype(BF)
             return carry
 
-        lax.fori_loop(0, 2, backward, 0)
+        for j in range(2):
+            backward(j, 0)
         if first == 0:
             for steps in (2, 1, 3, 0):
                 sx2.give(steps)
@@ -750,13 +752,15 @@
 
     def attend_back(h):
         probs = r.probs[h]
-        g_att = r.g_att[h]
-        grad_probs = mm_t(g_att, r.values[...])
+        grad_probs = mm_t(r.g_att[h], r.values[...])
         delta = jnp.sum(probs * grad_probs, axis=1, keepdims=True)
-        grad_scores = (probs * (grad_probs - delta)).astype(BF)
-        grad_q = mm(grad_scores, r.keys[...]) * SCALE
-        r.d_keys[...] += t_mm(grad_scores, r.queries[h])
-        back = spin_back(grad_q, r.cosine[2 * T :], r.sine[2 * T :])
+        grad_scores = probs * (grad_probs - delta)
+        r.probs[h] = grad_scores
+        r.d_keys[...] += t_mm(grad_scores.astype(BF), r.queries[h])
+
+    def query_back(h):
+        grad_q = mm(r.probs[h].astype(BF), r.keys[...]) * SCALE
+        back = spin_back(grad_q, cosine, sine)
         unit = r.q_unit[h]
         r.q_gain[...] += jnp.sum(back * unit, axis=0, keepdims=True)
         r.g_q[h] = norm_back(back * r.mults[4:5, 0:HD], unit, r.q_inv[h]).astype(BF)
@@ -768,35 +772,40 @@
     for h in range(1, HEADS):
         attend_back(h)
     aside_k = halo_aside(0, r.d_keys, SCALE)
-    for steps in (2, 1, 3):
-        so.take(steps)
 
     normed, turned = r.normed[...], r.normed_t[...]
+    query_back(0)
+    back_k = halo_back(0, aside_k)
+    for h in range(1, HEADS):
+        query_back(h)
     for h in range(HEADS):
         r.g_x1[h // 2, :, 256 * (h % 2) : 256 * (h % 2) + 256] = t_mm(normed, r.g_q[h]).astype(BF)
     for steps in (2, 1, 3, 0):
         sx1.give(steps)
-    back_k = halo_back(0, aside_k)
     sd.take(3)
+    for steps in (2, 1, 3):
+        so.take(steps)
     for s in wide:
         s.step2()
     for steps in (2, 1, 3):
         sx1.take(steps)
-    own_k = halo_sum(0, r.d_keys, SCALE, back_k)
     own_v = halo_sum(1, r.d_values, 1.0, back_v)
-    key_back = spin_back(own_k, cosine, sine)
-    k_unit = r.k_unit[...]
-    key_gain = jnp.sum(key_back * k_unit, axis=0, keepdims=True)
-    grad_k = norm_back(key_back * r.mults[5:6, 0:HD], k_unit, key_inv).astype(BF)
     grad_v = own_v.astype(BF)
-    r.g_z1[0, :, 0:256] = t_mm(turned, grad_k).astype(BF)
     r.g_z1[1, :, 0:256] = t_mm(turned, grad_v).astype(BF)
     r.g_z1[1, :, 256:384] = jnp.zeros((D, 128), BF)
     grad_natural = mm_t(r.g_q[0], r.w_x1[0, :, 0:256])
     for h in range(1, HEADS):
         grad_natural = grad_natural + mm_t(r.g_q[h], r.w_x1[h // 2, :, 256 * (h % 2) : 256 * (h % 2) + 256])
-    grad_turned = mm_t(grad_k, r.w_z1[0, :, 0:256]) + mm_t(grad_v, r.w_z1[1, :, 0:256])
-    grad_normed = grad_natural + split_dot(grad_turned, r.turn[...])
+    r.acc[...] = grad_natural
+    r.acc_t[...] = mm_t(grad_v, r.w_z1[1, :, 0:256])
+    own_k = halo_sum(0, r.d_keys, SCALE, back_k)
+    key_back = spin_back(own_k, cosine, sine)
+    k_unit = r.k_unit[...]
+    key_gain = jnp.sum(key_back * k_unit, axis=0, keepdims=True)
+    grad_k = norm_back(key_back * r.mults[5:6, 0:HD], k_unit, key_inv).astype(BF)
+    r.g_z1[0, :, 0:256] = t_mm(turned, grad_k).astype(BF)
+    grad_turned = r.acc_t[...] + mm_t(grad_k, r.w_z1[0, :, 0:256])
+    grad_normed = r.acc[...] + split_dot(grad_turned, r.turn[...])
     in_unit = r.in_unit[...]
     r.gain_sums[0:1] = jnp.sum(grad_normed * in_unit, axis=0, keepdims=True)
     both = jnp.concatenate([r.q_gain[...], key_gain, jnp.zeros((6, HD), F32)], axis=0).astype(BF)
@@ -952,8 +961,10 @@
 
 
 def deliver_kernel(mixed, igrad, x1, z1, o, x2, z2, d, *outs):
-    outs[0][...] = mixed[...]
-    outs[1][...] = igrad[...]
+    *outs, sems = outs
+    large = [pltpu.make_async_copy(a, b, sems.at[i]) for i, (a, b) in enumerate(((mixed, outs[0]), (igrad, outs[1])))]
+    for copy in large:
+        copy.start()
     outs[2][:, 0:512] = x1[0, 0:5]
     outs[2][:, 512:1024] = x1[1, 0:5]
     outs[3][...] = z1[0, 0:5, 0:256]
@@ -967,17 +978,21 @@
     gains = z1[0, :, 256:384].T
     for at, row, n in ((9, 0, 5), (10, 4, 2), (11, 5, 2), (12, 1, 5), (13, 2, 5), (14, 3, 5)):
         outs[at][...] = gains[row : row + 1, 0:n].reshape(n)
+    for copy in large:
+        copy.wait()
 
 
 def deliver(*parts):
     inside = pl.BlockSpec(memory_space=pltpu.VMEM)
+    anywhere = pl.BlockSpec(memory_space=pl.ANY)
     shapes = [(T, D), (5, 1024), (5, 256), (5, 256), (8, D), (5, 2048), (5, 2048), (16, D)]
     shapes += [(5,), (2,), (2,), (5,), (5,), (5,)]
     return pl.pallas_call(
         deliver_kernel,
         out_shape=[jax.ShapeDtypeStruct((T, D), BF)] + [jax.ShapeDtypeStruct(s, F32) for s in shapes],
-        in_specs=[inside] * len(parts),
-        out_specs=[inside] * 15,
+        in_specs=[anywhere] * 2 + [inside] * (len(parts) - 2),
+        out_specs=[anywhere] * 2 + [inside] * 13,
+        scratch_shapes=[pltpu.SemaphoreType.DMA((2,))],
         name="deliver",
     )(*parts)
 

time: 117 us -> 145 us (1.24)
  Pallas kernels: 116 us -> 144 us
    pallas_call x1, Pallas kernels: 2.3 us -> 32.6 us  [deliver(): pl.pallas_call(deliver_kernel, out_shape=[jax.ShapeDtypeStruct((T, D), BF...]
    pallas_call x1, Pallas kernels: 113 us -> 112 us  [layer(): pl.pallas_call(lambda *refs: layer_kernel(names, *refs), out_shape=[jax.S...]
where the time goes in v7:
time: 145 us
  Pallas kernels  144 us (99%)
    pallas_call x1, Pallas kernels, layer(): pl.pallas_call(lambda *refs: layer_kernel(names, *refs), out_shape=[jax.S...  112 us
    pallas_call x1, Pallas kernels, deliver(): pl.pallas_call(deliver_kernel, out_shape=[jax.ShapeDtypeStruct((T, D), BF...  32.6 us

profile of v7, /device:TPU:1, one launch (start us, length us, event | category | flops | bytes accessed | tf_op | source)
XLA Modules:
  0.0 145.3 jit_solution(14927919184243003521)
XLA Ops:
  0.7 111.9 %decoder_layer.1 = (bf16[256,640]{1,0:T(8,128)(2,1)}, f32[256,640]{1,0:T(8,128)}, f32[2,8,512]{2,1,0:T(8,128)}, f32[2,8,384]{2,1,0:T(8,128)}, f32[2,8,384]{2,1,0...) custom-call(bf16[256,640]{1,0:T(8,128)(2,1)} %refs_0_.1, bf16[5,1024]{1,0:T(8,128)(2,1)} %refs_1_.1, ...), custom_call_target="tpu_custom_call" | custom-call | tf_op jit(solution)/shard_map/decoder_layer/pallas_call | solution.py:950
  112.5 32.6 %deliver.1 = (bf16[256,640]{1,0:T(8,128)(2,1)}, f32[256,640]{1,0:T(8,128)}, f32[5,1024]{1,0:T(8,128)}, f32[5,256]{1,0:T(8,128)}, f32[5,256]{1,0:T(8,128)}, /*ind...) custom-call(bf16[256,640]{1,0:T(8,128)(2,1)} %get-tuple-element.23.m, ...), custom_call_target="tpu_custom_call" | custom-call | tf_op jit(solution)/shard_map/deliver/pallas_call | solution.py:990

commit v8 on v7

--- a/solution.py
+++ b/solution.py
@@ -961,10 +961,8 @@
 
 
 def deliver_kernel(mixed, igrad, x1, z1, o, x2, z2, d, *outs):
-    *outs, sems = outs
-    large = [pltpu.make_async_copy(a, b, sems.at[i]) for i, (a, b) in enumerate(((mixed, outs[0]), (igrad, outs[1])))]
-    for copy in large:
-        copy.start()
+    outs[0][...] = mixed[...]
+    outs[1][...] = igrad[...]
     outs[2][:, 0:512] = x1[0, 0:5]
     outs[2][:, 512:1024] = x1[1, 0:5]
     outs[3][...] = z1[0, 0:5, 0:256]
@@ -978,21 +976,17 @@
     gains = z1[0, :, 256:384].T
     for at, row, n in ((9, 0, 5), (10, 4, 2), (11, 5, 2), (12, 1, 5), (13, 2, 5), (14, 3, 5)):
         outs[at][...] = gains[row : row + 1, 0:n].reshape(n)
-    for copy in large:
-        copy.wait()
 
 
 def deliver(*parts):
     inside = pl.BlockSpec(memory_space=pltpu.VMEM)
-    anywhere = pl.BlockSpec(memory_space=pl.ANY)
     shapes = [(T, D), (5, 1024), (5, 256), (5, 256), (8, D), (5, 2048), (5, 2048), (16, D)]
     shapes += [(5,), (2,), (2,), (5,), (5,), (5,)]
     return pl.pallas_call(
         deliver_kernel,
         out_shape=[jax.ShapeDtypeStruct((T, D), BF)] + [jax.ShapeDtypeStruct(s, F32) for s in shapes],
-        in_specs=[anywhere] * 2 + [inside] * (len(parts) - 2),
-        out_specs=[anywhere] * 2 + [inside] * 13,
-        scratch_shapes=[pltpu.SemaphoreType.DMA((2,))],
+        in_specs=[inside] * len(parts),
+        out_specs=[inside] * 15,
         name="deliver",
     )(*parts)
 

time: 145 us -> 115 us (0.79)
  Pallas kernels: 144 us -> 114 us
    pallas_call x1, Pallas kernels: 32.6 us -> 2.3 us  [deliver(): pl.pallas_call(deliver_kernel, out_shape=[jax.ShapeDtypeStruct((T, D), BF...]
where the time goes in v8:
time: 115 us
  Pallas kernels  114 us (99%)
    pallas_call x1, Pallas kernels, layer(): pl.pallas_call(lambda *refs: layer_kernel(names, *refs), out_shape=[jax.S...  112 us
    pallas_call x1, Pallas kernels, deliver(): pl.pallas_call(deliver_kernel, out_shape=[jax.ShapeDtypeStruct((T, D), BF...  2.3 us

profile of v8, /device:TPU:1, one launch (start us, length us, event | category | flops | bytes accessed | tf_op | source)
XLA Modules:
  0.0 115.0 jit_solution(18438503489300788869)
XLA Ops:
  0.7 111.9 %decoder_layer.1 = (bf16[256,640]{1,0:T(8,128)(2,1)}, f32[256,640]{1,0:T(8,128)}, f32[2,8,512]{2,1,0:T(8,128)}, f32[2,8,384]{2,1,0:T(8,128)}, f32[2,8,384]{2,1,0...) custom-call(bf16[256,640]{1,0:T(8,128)(2,1)} %refs_0_.1, bf16[5,1024]{1,0:T(8,128)(2,1)} %refs_1_.1, ...), custom_call_target="tpu_custom_call" | custom-call | tf_op jit(solution)/shard_map/decoder_layer/pallas_call | solution.py:950
  112.5 2.3 %deliver.1 = (bf16[256,640]{1,0:T(8,128)(2,1)}, f32[256,640]{1,0:T(8,128)}, f32[5,1024]{1,0:T(8,128)}, f32[5,256]{1,0:T(8,128)}, f32[5,256]{1,0:T(8,128)}, /*ind...) custom-call(bf16[256,640]{1,0:T(8,128)(2,1)} %get-tuple-element.23.m, ...), custom_call_target="tpu_custom_call" | custom-call | tf_op jit(solution)/shard_map/deliver/pallas_call | solution.py:985
